TPU v7x, 32 devices: a whole 2x2x4 slice. The times are simulated.
32 devices in a mesh: groups: 2 (over y), expert: 4 (over x, core), dp: 4 (over z).
Axes of the slice: x: 2, y: 2, z: 4, core: 2. Of those that a mesh axis runs over, the one named last changes fastest.
Arguments:
- tokens: bfloat16 [2048, 7168], P(('groups', 'expert', 'dp')), parts along dimension 0, may hold values from -6 to 6
- expert_ids: int32 [2048, 8], P(('groups', 'expert', 'dp')), parts along dimension 0, may hold values from 0 to 255, all different within a row; in each aligned block of 64 rows (0 to 63, 64 to 127, ...) at most 4 rows name the same one
- gate_weights: float32 [2048, 8], P(('groups', 'expert', 'dp')), parts along dimension 0, may hold values from 0.05 to 0.6
- w_gate: bfloat16 [4, 7168, 2048], P('expert', None, 'dp'), may hold values from -0.0625 to 0.0625
- w_up: bfloat16 [4, 7168, 2048], P('expert', None, 'dp'), may hold values from -0.0625 to 0.0625
- w_down: bfloat16 [4, 2048, 7168], P('expert', 'dp'), may hold values from -0.125 to 0.125
Outputs:
- embedding: bfloat16 [2048, 7168], P(('groups', 'expert', 'dp')), parts along dimension 0
There are 2 independent parts, one for each index of `groups`. A program takes and returns all parts, laid end to end along the dimension named above; an argument that names none is the same for every part. Nothing has to cross between parts.
Inputs may be any that keep to these rules, and one draw needn't show every extreme that they name: `expert_ids`: each token names 8 different experts; among the 64 tokens of one device no expert is named more than 4 times, a bound that some block reaches.
All inputs are finite; a program needn't handle non-finite values.
Results may differ from a plain program's by a relative error of at most 0.012.
Values may be sent and summed in bfloat16 or wider, within the bound.
No kernel may reach another device: no remote copies, remote signals or barrier semaphores. Data moves between devices by JAX's collectives and lax.ppermute only.
A program may use at most 64 MiB of HBM per device.

v0:
```python
import jax
import jax.numpy as jnp
from jax import lax
from jax.sharding import PartitionSpec as P

CAP = 4


def build_slots(expert_ids, gate_weights, window, capacity):
    expert_list = jnp.arange(window, dtype=jnp.int32)
    matches = expert_ids[:, :, None] == expert_list[None, None, :]
    chosen = jnp.sum(matches.astype(jnp.int32), axis=1)
    route_weight = jnp.sum(jnp.where(matches, gate_weights[:, :, None], jnp.float32(0.0)), axis=1)
    position = jnp.cumsum(chosen, axis=0) - chosen
    slot_index = jnp.arange(capacity, dtype=jnp.int32)
    select = (position.T[:, None, :] == slot_index[None, :, None]) & (chosen.T[:, None, :] > 0)
    return (select.astype(jnp.float32), route_weight)


def local(tokens, expert_ids, gate_weights, w_gate, w_up, w_down):
    window = lax.axis_size("expert")
    select, route_weight = build_slots(expert_ids, gate_weights, window, CAP)
    outgoing = jnp.einsum(
        "wct,td->wcd", select.astype(jnp.bfloat16), tokens, preferred_element_type=jnp.float32
    ).astype(jnp.bfloat16)
    gate_mat = w_gate[0]
    up_mat = w_up[0]
    down_mat = w_down[0]
    copies = lax.all_gather(outgoing, "dp", axis=1, tiled=True)
    row_block = lax.all_to_all(copies, "expert", split_axis=0, concat_axis=0, tiled=True)
    sources = row_block.shape[0]
    count = row_block.shape[1]
    flat_rows = row_block.reshape(sources * count, row_block.shape[2])
    gate_proj = jnp.dot(flat_rows, gate_mat, preferred_element_type=jnp.float32)
    up_proj = jnp.dot(flat_rows, up_mat, preferred_element_type=jnp.float32)
    hidden = (jax.nn.silu(gate_proj) * up_proj).astype(jnp.bfloat16)
    partial_value = jnp.dot(hidden, down_mat, preferred_element_type=jnp.float32)
    partial_value = partial_value.reshape(sources, count, partial_value.shape[1])
    returned = lax.all_to_all(
        partial_value.astype(jnp.bfloat16), "expert", split_axis=0, concat_axis=0, tiled=True
    )
    expert_out = lax.psum_scatter(
        returned.astype(jnp.float32).astype(jnp.bfloat16), "dp", scatter_dimension=1, tiled=True
    ).astype(jnp.float32)
    combine = select * route_weight.T[:, None, :]
    mixed = jnp.einsum("wct,wcd->td", combine, expert_out, precision=lax.Precision.HIGHEST)
    return mixed.astype(jnp.bfloat16)


def solution(mesh):
    placed = (
        P(("groups", "expert", "dp"), None),
        P(("groups", "expert", "dp"), None),
        P(("groups", "expert", "dp"), None),
        P("expert", None, "dp"),
        P("expert", None, "dp"),
        P("expert", "dp", None),
    )
    return jax.shard_map(
        local,
        mesh=mesh,
        in_specs=placed,
        out_specs=P(("groups", "expert", "dp"), None),
        check_vma=False,
    )
```

profile of v0, /device:TPU:0, one launch (start us, length us, event | category | flops | bytes accessed | tf_op | source)
XLA Modules:
  0.0 128.1 jit_solution(11296890111677346302)
XLA Ops:
  6.5 0.0 copy-start
  6.5 0.0 all-reduce.3.cloned.1.call-start
  6.5 0.8 convert_reduce_fusion
  7.3 0.1 copy.27
  7.4 0.1 reduce_window_sum.11
  7.5 0.1 copy.29
  7.6 0.1 copy-done
  7.7 0.2 convolution_convert_fusion.1
  8.0 0.1 copy.31
  8.1 22.8 %all_gather.3 = bf16[4,16,7168]{2,0,1:T(4,128)(2,1)S(1)} all-gather(bf16[4,4,7168]{2,0,1:T(4,128)(2,1)S(1)} %copy.31), channel_id=1, replica_groups=mesh['groups'=2,'expert'=4,'dp'=4] {'dp'}, dimensions={1}, use_global_device_ids=true | all-gather | bytes 1146880 | tf_op jit(solution)/shard_map/all_gather | solution.py:29
  30.9 0.3 copy.32
  31.1 0.0 slice-start
  31.1 0.0 slice-start.2
  31.2 16.0 %all_to_all.10 = bf16[4,16,7168]{2,1,0:T(8,128)(2,1)S(1)} all-to-all(bf16[4,16,7168]{2,1,0:T(8,128)(2,1)S(1)} %copy.32), channel_id=1, replica_groups=mesh['groups'=2,'expert'=4,'dp'=4] {'expert'}, dimensions={0} | all-to-all | bytes 1835008 | tf_op jit(solution)/shard_map/all_to_all | solution.py:30
  47.2 0.0 slice-start.1
  47.2 0.0 slice-start.3
  47.2 4.6 %fusion.4 = f32[64,512]{1,0:T(8,128)S(1)} fusion(bf16[64,7168]{1,0:T(8,128)(2,1)S(1)} %bitcast.34, bf16[1,7168,512]{2,1,0:T(8,128)(2,1)} %param.9), kind=kOutput, calls=%fused_computation.7 | convolution fusion | flops 469762048 | bytes 8388608 | tf_op jit(solution)/shard_map/dot_general | solution.py:34
  51.8 0.0 slice-done
  51.8 0.0 slice-done.1
  51.8 1.4 %fusion.9 = bf16[64,512]{1,0:T(8,128)(2,1)S(1)} fusion(bf16[64,7168]{1,0:T(8,128)(2,1)S(1)} %bitcast.35, bf16[1,7168,512]{2,1,0:T(8,128)(2,1)S(1)} %bitcast.33, f32[64,512]{1,0:T(8,128)S(1)} %fusion.4), kind=kOutput, calls=%fused_computation.10 | convolution fusion | flops 469958656 | bytes 8454144 | tf_op jit(solution)/shard_map/dot_general | solution.py:35
  53.2 0.0 copy-start.3
  53.2 0.0 copy-start.1
  53.2 0.0 copy-start.2
  53.2 0.0 slice-done.2
  53.2 0.0 slice-done.3
  53.3 1.4 %convolution_convert_fusion = bf16[4,16,7168]{2,1,0:T(8,128)(2,1)S(1)} fusion(bf16[4,16,512]{2,1,0:T(8,128)(2,1)S(1)} %bitcast.38, bf16[1,512,7168]{2,1,0:T(8,128)(2,1)S(1)} %bitcast.37), kind=kOutput, calls=%fused_computation.1 | convolution fusion | flops 470220800 | bytes 8323072 | tf_op jit(solution)/shard_map/dot_general | solution.py:37
  54.7 15.5 %all_to_all.11 = bf16[4,16,7168]{2,1,0:T(8,128)(2,1)S(1)} all-to-all(bf16[4,16,7168]{2,1,0:T(8,128)(2,1)S(1)} %convolution_convert_fusion), channel_id=1, replica_groups=mesh['groups'=2,'expert'=4,'dp'=4] {'expert'}, dimensions={0} | all-to-all | bytes 1835008 | tf_op jit(solution)/shard_map/all_to_all | solution.py:39
  70.1 1.6 %copy.33 = bf16[4,16,7168]{2,0,1:T(4,128)(2,1)} copy(bf16[4,16,7168]{2,1,0:T(8,128)(2,1)S(1)} %all_to_all.11) | data formatting | bytes 1835008 | tf_op jit(solution)/shard_map/all_to_all | solution.py:39
  71.8 0.0 all-reduce.3.cloned.1.call-update
  71.8 0.0 copy-done.3
  71.8 0.6 dynamic-slice
  73.1 0.0 copy-done.1
  73.1 0.0 copy-done.2
  73.2 45.2 %all-reduce.3.cloned.1.call-done = bf16[4,16,7168]{2,0,1:T(4,128)(2,1)} async-done(((bf16[4,16,7168]{2,0,1:T(4,128)(2,1)}), bf16[4,16,7168]{2,0,1:T(4,128)(2,1)}) %all-reduce.3.cloned.1.call-update) | async-done | bytes 917520
  118.3 2.9 %fusion = bf16[64,7168]{1,0:T(8,128)(2,1)} fusion(bf16[4,16,7168]{2,0,1:T(4,128)(2,1)} %all-reduce.3.cloned.1.call-done, u32[]{:T(128)S(6)} %multiply.1, f32[4,64]{1,0:T(4,128)S(1)} %bitcast.39, s32[4,64]{1,0:T(4,128)S(1)} %copy.29, pred[4,64]{1,0:T(4,128)(4,1)S(1)} %compare_bitcast_fusion), kind=kOutput, calls=%fused_computation.2 | convolution fusion | flops 88542208 | bytes 1149188 | tf_op jit(solution)/shard_map/wct,wcd->td/dot_general | solution.py:46
  (6 shorter events, 0.0 us)
Async XLA Ops:
  6.5 1.2 copy-start
  6.5 111.8 %all-reduce.3.cloned.1.call-start = ((), (), s32[]{:S(2)}) async-start(), calls=%async_computation.2 | async-start | bytes 1835008
  31.1 20.6 %slice-start = ((s8[7340032]{0:T(1024)(128)(4,1)}), s8[4194304]{0:T(1024)(128)(4,1)S(1)}, s32[]{:S(2)}) async-start(s8[7340032]{0:T(1024)(128)(4,1)} %bitcast.32), calls=%async_computation.3 | async-start | bytes 8388608
  31.1 22.1 %slice-start.2 = ((s8[7340032]{0:T(1024)(128)(4,1)}), s8[4194304]{0:T(1024)(128)(4,1)S(1)}, s32[]{:S(2)}) async-start(s8[7340032]{0:T(1024)(128)(4,1)} %bitcast.36), calls=%async_computation.5 | async-start | bytes 8388608
  47.2 4.6 %slice-start.1 = ((s8[7340032]{0:T(1024)(128)(4,1)}), s8[3145728]{0:T(1024)(128)(4,1)S(1)}, s32[]{:S(2)}) async-start(s8[7340032]{0:T(1024)(128)(4,1)} %bitcast.32), calls=%async_computation.4 | async-start | bytes 6291456
  47.2 6.1 %slice-start.3 = ((s8[7340032]{0:T(1024)(128)(4,1)}), s8[3145728]{0:T(1024)(128)(4,1)S(1)}, s32[]{:S(2)}) async-start(s8[7340032]{0:T(1024)(128)(4,1)} %bitcast.36), calls=%async_computation.6 | async-start | bytes 6291456
  53.2 18.6 %copy-start.3 = (u32[32]{0:T(128)S(1)}, u32[32]{0:T(128)}, u32[]{:S(2)}) copy-start(u32[32]{0:T(128)} %constant.17) | copy-start | bytes 388
  53.2 19.9 %copy-start.1 = (s32[64,8]{0,1:T(8,128)S(1)}, s32[64,8]{0,1:T(8,128)}, u32[]{:S(2)}) copy-start(s32[64,8]{0,1:T(8,128)} %param.7) | copy-start | bytes 6148
  53.2 19.9 %copy-start.2 = (f32[64,8]{0,1:T(8,128)S(1)}, f32[64,8]{0,1:T(8,128)}, u32[]{:S(2)}) copy-start(f32[64,8]{0,1:T(8,128)} %param.8) | copy-start | bytes 6148
Sparse Core Ops, SparseCore 0:
  71.9 46.3 all-reduce.2
where the time goes:
time: 128 us
  blocking collectives  54.2 us (42%)
  waiting for transfers between devices  45.2 us (35%)
  between operations  14.2 us (11%)
  matrix products  10.5 us (8%)
  local copies, waits for them, and re-layouts  3 us (2%)
    unnamed x2, waiting for transfers between devices  45.2 us
    all_gather x1, blocking collectives, local(): copies = lax.all_gather(outgoing, 'dp', axis=1, tiled=True)  22.8 us
    all_to_all x1, blocking collectives, local(): lax.all_to_all(copies, 'expert', split_axis=0, concat_axis=0, tiled=True)  16 us
    all_to_all x1, blocking collectives, local(): lax.all_to_all(partial_value.astype(jnp.bfloat16), 'expert', split_axis=0...  15.5 us
    dot_general x1, matrix products, local(): gate_proj = jnp.dot(flat_rows, gate_mat, preferred_element_type=jnp.float32)  4.6 us
    dot_general x1, matrix products, local(): jnp.einsum('wct,wcd->td', combine, expert_out, precision=lax.Precision.HI...  2.88 us
  transfers between devices with their start and end apart: 1, of which 1 were waited for; matrix products, arithmetic and copies ran while one was open for 1% of the time, Pallas kernels for 0%

commit v1 on v0

v1 whole, which is shorter than its diff:
```python
import jax
import jax.numpy as jnp
from jax import lax
from jax.sharding import PartitionSpec as P

CAP = 4
CORES = 2


def routing(expert_ids, gate_weights, experts):
    matches = expert_ids[:, :, None] == experts[None, None, :]
    chosen = jnp.any(matches, axis=1)
    weight = jnp.sum(jnp.where(matches, gate_weights[:, :, None], jnp.float32(0.0)), axis=1)
    count = chosen.astype(jnp.int32)
    tokens = count.shape[0]
    before = lax.broadcasted_iota(jnp.int32, (tokens, tokens), 0) > lax.broadcasted_iota(jnp.int32, (tokens, tokens), 1)
    position = jnp.dot(
        before.astype(jnp.bfloat16), count.astype(jnp.bfloat16), preferred_element_type=jnp.float32
    ).astype(jnp.int32)
    slot = jnp.arange(CAP, dtype=jnp.int32)
    select = (position.T[:, None, :] == slot[None, :, None]) & chosen.T[:, None, :]
    return select, weight


def ring(n):
    return [(i, (i + 1) % n) for i in range(n)]


def gather_ring(block, n):
    parts = [block]
    for _ in range(n - 1):
        parts.append(lax.ppermute(parts[-1], "dp", ring(n)))
    return parts


def scatter_ring(parts, n):
    total = parts[1 % n]
    for step in range(1, n):
        arrived = lax.ppermute(total, "dp", ring(n))
        total = (arrived.astype(jnp.float32) + parts[(step + 1) % n].astype(jnp.float32)).astype(jnp.bfloat16)
    return total


def local(tokens, expert_ids, gate_weights, w_gate, w_up, w_down):
    window = lax.axis_size("expert")
    shards = lax.axis_size("dp")
    chips = window // CORES
    width = tokens.shape[1]
    me = lax.axis_index("expert")
    chip, core = me // CORES, me % CORES
    offset = jnp.arange(window, dtype=jnp.int32)
    core_offset, chip_offset = offset // chips, offset % chips
    experts = ((chip + chip_offset) % chips) * CORES + (core + core_offset) % CORES
    select, route_weight = routing(expert_ids, gate_weights, experts)
    flat_select = select.reshape(window * CAP, -1)
    outgoing = jnp.dot(
        flat_select.astype(jnp.bfloat16), tokens, preferred_element_type=jnp.float32
    ).astype(jnp.bfloat16)

    core_pairs = [(i, i ^ 1) for i in range(window)]

    def chip_pairs(shift):
        return [
            (c * CORES + k, ((c + shift) % chips) * CORES + k) for c in range(chips) for k in range(CORES)
        ]

    half = chips * CAP
    kept = outgoing[:half].reshape(chips, CAP, width)
    swapped = lax.ppermute(outgoing[half:], "expert", core_pairs).reshape(chips, CAP, width)
    blocks = jnp.concatenate([kept, swapped], axis=1)
    chunk_a = blocks[0]
    chunk_b = [lax.ppermute(blocks[shift], "expert", chip_pairs(shift)) for shift in range(1, chips)]
    chunk_b = jnp.concatenate(chunk_b, axis=0)
    parts_a = gather_ring(chunk_a, shards)
    parts_b = gather_ring(chunk_b, shards)
    rows = jnp.concatenate(parts_b + parts_a, axis=0)

    gate_proj = jnp.dot(rows, w_gate[0], preferred_element_type=jnp.float32)
    up_proj = jnp.dot(rows, w_up[0], preferred_element_type=jnp.float32)
    hidden = (jax.nn.silu(gate_proj) * up_proj).astype(jnp.bfloat16)
    partial = jnp.dot(hidden, w_down[0], preferred_element_type=jnp.float32).astype(jnp.bfloat16)

    size_b, size_a = chunk_b.shape[0], chunk_a.shape[0]
    back_b = [partial[i * size_b:(i + 1) * size_b] for i in range(shards)]
    rest = partial[shards * size_b:]
    back_a = [rest[i * size_a:(i + 1) * size_a] for i in range(shards)]
    sum_b = scatter_ring(back_b, shards)
    sum_a = scatter_ring(back_a, shards)
    home = [sum_a]
    for shift in range(1, chips):
        home.append(
            lax.ppermute(
                sum_b[(shift - 1) * 2 * CAP:shift * 2 * CAP], "expert", chip_pairs(chips - shift)
            )
        )
    home = jnp.stack(home)
    mine = home[:, :CAP].reshape(half, width)
    other = lax.ppermute(home[:, CAP:].reshape(half, width), "expert", core_pairs)
    expert_out = jnp.concatenate([mine, other], axis=0)

    combine = (select.astype(jnp.float32) * route_weight.T[:, None, :]).reshape(window * CAP, -1)
    high = lax.reduce_precision(combine, 8, 7)
    low = combine - high
    mixed = jnp.einsum(
        "ct,cd->td",
        jnp.concatenate([high, low], axis=0).astype(jnp.bfloat16),
        jnp.concatenate([expert_out, expert_out], axis=0),
        preferred_element_type=jnp.float32,
    )
    return mixed.astype(jnp.bfloat16)


def solution(mesh):
    placed = (
        P(("groups", "expert", "dp"), None),
        P(("groups", "expert", "dp"), None),
        P(("groups", "expert", "dp"), None),
        P("expert", None, "dp"),
        P("expert", None, "dp"),
        P("expert", "dp", None),
    )
    return jax.shard_map(
        local,
        mesh=mesh,
        in_specs=placed,
        out_specs=P(("groups", "expert", "dp"), None),
        check_vma=False,
    )
```

time: 128 us -> 97.3 us (0.76)
  blocking collectives: 54.2 us -> 0 us
  waiting for transfers between devices: 45.2 us -> 73.4 us
  between operations: 14.2 us -> 0.19 us
  starting transfers between devices: 0.01 us -> 6.79 us
  matrix products: 10.5 us -> 14.1 us
  local copies, waits for them, and re-layouts: 3 us -> 0.37 us
    ppermute x0 -> x16, waiting for transfers between devices: none -> 73.4 us  [the longest x6 39 us: gather_ring(): parts.append(lax.ppermute(parts[-1], 'dp', ring(n)))]
    unnamed x2 -> x0, waiting for transfers between devices: 45.2 us -> none
    all_to_all x2 -> x0, blocking collectives: 31.5 us -> none  [the longest x1 16 us: local(): lax.all_to_all(copies, 'expert', split_axis=0, concat_axis=0, tiled=True)]
    all_gather x1 -> x0, blocking collectives: 22.8 us -> none  [local(): copies = lax.all_gather(outgoing, 'dp', axis=1, tiled=True)]
    ppermute x0 -> x16, starting transfers between devices: none -> 6.79 us  [the longest x1 2.91 us: local(): lax.ppermute(blocks[shift], 'expert', chip_pairs(shift))]
    dot_general x5, matrix products: 10.5 us -> 14.1 us  [the longest x1 7.93 us: local(): jnp.dot(hidden, w_down[0], preferred_element_type=jnp.float32)]
    all_to_all x1 -> x0, local copies, waits for them, and re-layouts: 1.63 us -> none  [local(): lax.all_to_all(partial_value.astype(jnp.bfloat16), 'expert', split_axis=0...]
  transfers between devices with their start and end apart: 1 -> 16, of which waited for: 1 -> 16; matrix products, arithmetic and copies ran while one was open for 1% -> 0% of each run, Pallas kernels for 0% -> 0%
where the time goes in v1:
time: 97.3 us; the launch traced here: 97 us
  waiting for transfers between devices  73.4 us (75%)
  matrix products  14.1 us (14%)
  starting transfers between devices  6.79 us (7%)
  other arithmetic  2.12 us (2%)
    ppermute x6, waiting for transfers between devices, gather_ring(): parts.append(lax.ppermute(parts[-1], 'dp', ring(n)))  39 us
    ppermute x6, waiting for transfers between devices, scatter_ring(): arrived = lax.ppermute(total, 'dp', ring(n))  25 us
    dot_general x1, matrix products, local(): jnp.dot(hidden, w_down[0], preferred_element_type=jnp.float32)  7.93 us
    dot_general x1, matrix products, local(): up_proj = jnp.dot(rows, w_up[0], preferred_element_type=jnp.float32)  4.45 us
    ppermute x1, waiting for transfers between devices, local(): lax.ppermute(sum_b[(shift - 1) * 2 * CAP:shift * 2 * CAP], 'expert', chip...  3.81 us
    ppermute x1, waiting for transfers between devices, local(): lax.ppermute(blocks[shift], 'expert', chip_pairs(shift))  3.46 us
    ppermute x1, starting transfers between devices, local(): lax.ppermute(blocks[shift], 'expert', chip_pairs(shift))  2.91 us
  transfers between devices with their start and end apart: 16, of which 16 were waited for; matrix products, arithmetic and copies ran while one was open for 0% of the time, Pallas kernels for 0%

profile of v1, /device:TPU:0, one launch (start us, length us, event | category | flops | bytes accessed | tf_op | source)
XLA Modules:
  0.0 97.0 jit_solution(15446530926578845359)
XLA Ops:
  0.0 0.9 compare_reduce_fusion
  0.9 0.1 convolution_convert_fusion.3
  1.0 0.8 fusion.22
  1.8 0.1 eq.46
  1.9 0.1 reduce-precision_convert_fusion
  2.0 0.2 convolution_convert_fusion.2
  2.3 0.5 collective-permute-start
  2.8 0.1 reshape.72
  2.8 0.9 collective-permute-done
  3.7 0.1 reshape.73
  3.8 0.1 fusion.15
  3.9 2.9 %collective-permute-start.1 = (bf16[8,7168]{1,0:T(8,128)(2,1)S(1)}, bf16[8,7168]{1,0:T(8,128)(2,1)S(1)}, u32[]{:S(2)}, u32[]{:S(2)}) collective-permute-start(bf16[8,7168]{1,0:T(8,128)(2,1)S(1)} %fusion.15), channel_id=1, source_target_pairs={{0,8},{4,12},{8,0},{12,4},{1,9},{5,13},{9,1},{13,5},{2,10},{6,14},... | collective-permute-start | bytes 344072 | tf_op jit(solution)/shard_map/ppermute | solution.py:72
  6.8 3.5 %collective-permute-done.1 = bf16[8,7168]{1,0:T(8,128)(2,1)S(1)} collective-permute-done((bf16[8,7168]{1,0:T(8,128)(2,1)S(1)}, bf16[8,7168]{1,0:T(8,128)(2,1)S(1)}, u32[]{:S(2)}, u32[]{:S(2)}) %collective-permute-start.1) | collective-permute-done | bytes 114720 | tf_op jit(solution)/shard_map/ppermute | solution.py:72
  10.2 1.8 %collective-permute-start.2 = (bf16[8,7168]{1,0:T(8,128)(2,1)S(1)}, bf16[8,7168]{1,0:T(8,128)(2,1)S(1)}, u32[]{:S(2)}, u32[]{:S(2)}) collective-permute-start(bf16[8,7168]{1,0:T(8,128)(2,1)S(1)} %collective-permute-done.1), channel_id=1, source_target_pairs={{0,1},{1,2},{2,3},{3,0},{4,5},{5,6},{6,7},{7,4},{8,9},{9,10},{10,1... | collective-permute-start | bytes 344072 | tf_op jit(solution)/shard_map/ppermute | solution.py:32
  12.1 4.8 %collective-permute-done.2 = bf16[8,7168]{1,0:T(8,128)(2,1)S(1)} collective-permute-done((bf16[8,7168]{1,0:T(8,128)(2,1)S(1)}, bf16[8,7168]{1,0:T(8,128)(2,1)S(1)}, u32[]{:S(2)}, u32[]{:S(2)}) %collective-permute-start.2) | collective-permute-done | bytes 114720 | tf_op jit(solution)/shard_map/ppermute | solution.py:32
  16.9 0.0 collective-permute-start.3
  16.9 6.6 %collective-permute-done.3 = bf16[8,7168]{1,0:T(8,128)(2,1)S(1)} collective-permute-done((bf16[8,7168]{1,0:T(8,128)(2,1)S(1)}, bf16[8,7168]{1,0:T(8,128)(2,1)S(1)}, u32[]{:S(2)}, u32[]{:S(2)}) %collective-permute-start.3) | collective-permute-done | bytes 114720 | tf_op jit(solution)/shard_map/ppermute | solution.py:32
  23.4 0.0 collective-permute-start.4
  23.5 6.6 %collective-permute-done.4 = bf16[8,7168]{1,0:T(8,128)(2,1)S(1)} collective-permute-done((bf16[8,7168]{1,0:T(8,128)(2,1)S(1)}, bf16[8,7168]{1,0:T(8,128)(2,1)S(1)}, u32[]{:S(2)}, u32[]{:S(2)}) %collective-permute-start.4) | collective-permute-done | bytes 114720 | tf_op jit(solution)/shard_map/ppermute | solution.py:32
  30.0 0.1 constant_dynamic-update-slice_fusion.3
  30.1 0.1 collective-permute-start.5
  30.2 7.2 %collective-permute-done.5 = bf16[8,7168]{1,0:T(8,128)(2,1)S(1)} collective-permute-done((bf16[8,7168]{1,0:T(8,128)(2,1)S(1)}, bf16[8,7168]{1,0:T(8,128)(2,1)S(1)}, u32[]{:S(2)}, u32[]{:S(2)}) %collective-permute-start.5) | collective-permute-done | bytes 114720 | tf_op jit(solution)/shard_map/ppermute | solution.py:32
  37.4 0.0 collective-permute-start.6
  37.4 7.3 %collective-permute-done.6 = bf16[8,7168]{1,0:T(8,128)(2,1)S(1)} collective-permute-done((bf16[8,7168]{1,0:T(8,128)(2,1)S(1)}, bf16[8,7168]{1,0:T(8,128)(2,1)S(1)}, u32[]{:S(2)}, u32[]{:S(2)}) %collective-permute-start.6) | collective-permute-done | bytes 114720 | tf_op jit(solution)/shard_map/ppermute | solution.py:32
  44.7 6.6 %collective-permute-done.7 = bf16[8,7168]{1,0:T(8,128)(2,1)S(1)} collective-permute-done((bf16[8,7168]{1,0:T(8,128)(2,1)S(1)}, bf16[8,7168]{1,0:T(8,128)(2,1)S(1)}, u32[]{:S(2)}, u32[]{:S(2)}) %collective-permute-start.7) | collective-permute-done | bytes 114720 | tf_op jit(solution)/shard_map/ppermute | solution.py:32
  51.3 4.5 %fusion.1 = f32[64,512]{1,0:T(8,128)S(1)} fusion(bf16[64,7168]{1,0:T(8,128)(2,1)S(1)} %constant_dynamic-update-slice_fusion, bf16[1,7168,512]{2,1,0:T(8,128)(2,1)} %param.10), kind=kOutput, calls=%fused_computation.4 | convolution fusion | flops 469762048 | bytes 8388608 | tf_op jit(solution)/shard_map/dot_general | solution.py:79
  55.8 7.9 %convolution_convert_fusion = bf16[64,7168]{1,0:T(8,128)(2,1)S(1)} fusion(bf16[1,512,7168]{2,1,0:T(8,128)(2,1)} %param.11, f32[64,512]{1,0:T(8,128)S(1)} %fusion.1, bf16[64,7168]{1,0:T(8,128)(2,1)S(1)} %constant_dynamic-update-slice_fusion, bf16[1,7168,512]{2,1,0:T(8,128)(2,1)} %param.9), kind=kOutput, calls=%fused_computation | convolution fusion | flops 940179456 | bytes 16646144 | tf_op jit(solution)/shard_map/dot_general | solution.py:81
  63.7 0.1 collective-permute-start.11
  63.8 0.1 collective-permute-start.8
  63.8 7.8 %collective-permute-done.11 = bf16[8,7168]{1,0:T(8,128)(2,1)S(1)} collective-permute-done((bf16[8,7168]{1,0:T(8,128)(2,1)S(1)}, bf16[8,7168]{1,0:T(8,128)(2,1)S(1)}, u32[]{:S(2)}, u32[]{:S(2)}) %collective-permute-start.11) | collective-permute-done | bytes 114720 | tf_op jit(solution)/shard_map/ppermute | solution.py:39
  71.6 1.3 %collective-permute-done.8 = bf16[8,7168]{1,0:T(8,128)(2,1)S(1)} collective-permute-done((bf16[8,7168]{1,0:T(8,128)(2,1)S(1)}, bf16[8,7168]{1,0:T(8,128)(2,1)S(1)}, u32[]{:S(2)}, u32[]{:S(2)}) %collective-permute-start.8) | collective-permute-done | bytes 114720 | tf_op jit(solution)/shard_map/ppermute | solution.py:39
  72.9 0.1 add_convert_fusion.5
  73.0 0.1 collective-permute-start.12
  73.0 0.1 collective-permute-start.9
  73.1 6.9 %collective-permute-done.12 = bf16[8,7168]{1,0:T(8,128)(2,1)S(1)} collective-permute-done((bf16[8,7168]{1,0:T(8,128)(2,1)S(1)}, bf16[8,7168]{1,0:T(8,128)(2,1)S(1)}, u32[]{:S(2)}, u32[]{:S(2)}) %collective-permute-start.12) | collective-permute-done | bytes 114720 | tf_op jit(solution)/shard_map/ppermute | solution.py:39
  80.0 1.2 %collective-permute-done.9 = bf16[8,7168]{1,0:T(8,128)(2,1)S(1)} collective-permute-done((bf16[8,7168]{1,0:T(8,128)(2,1)S(1)}, bf16[8,7168]{1,0:T(8,128)(2,1)S(1)}, u32[]{:S(2)}, u32[]{:S(2)}) %collective-permute-start.9) | collective-permute-done | bytes 114720 | tf_op jit(solution)/shard_map/ppermute | solution.py:39
  81.3 0.1 add_convert_fusion.4
  81.3 0.1 collective-permute-start.10
  81.4 0.1 collective-permute-start.13
  81.5 6.5 %collective-permute-done.10 = bf16[8,7168]{1,0:T(8,128)(2,1)S(1)} collective-permute-done((bf16[8,7168]{1,0:T(8,128)(2,1)S(1)}, bf16[8,7168]{1,0:T(8,128)(2,1)S(1)}, u32[]{:S(2)}, u32[]{:S(2)}) %collective-permute-start.10) | collective-permute-done | bytes 114720 | tf_op jit(solution)/shard_map/ppermute | solution.py:39
  88.0 1.2 %collective-permute-done.13 = bf16[8,7168]{1,0:T(8,128)(2,1)S(1)} collective-permute-done((bf16[8,7168]{1,0:T(8,128)(2,1)S(1)}, bf16[8,7168]{1,0:T(8,128)(2,1)S(1)}, u32[]{:S(2)}, u32[]{:S(2)}) %collective-permute-start.13) | collective-permute-done | bytes 114720 | tf_op jit(solution)/shard_map/ppermute | solution.py:39
  89.2 0.1 fusion.12
  89.3 1.0 %collective-permute-start.14 = (bf16[8,7168]{1,0:T(8,128)(2,1)S(1)}, bf16[8,7168]{1,0:T(8,128)(2,1)S(1)}, u32[]{:S(2)}, u32[]{:S(2)}) collective-permute-start(bf16[8,7168]{1,0:T(8,128)(2,1)S(1)} %get-tuple-element.10), channel_id=1, source_target_pairs={{0,8},{4,12},{8,0},{12,4},{1,9},{5,13},{9,1},{13,5},{2,10},{6,14},... | collective-permute-start | bytes 344072 | tf_op jit(solution)/shard_map/ppermute | solution.py:92
  90.3 3.8 %collective-permute-done.14 = bf16[8,7168]{1,0:T(8,128)(2,1)S(1)} collective-permute-done((bf16[8,7168]{1,0:T(8,128)(2,1)S(1)}, bf16[8,7168]{1,0:T(8,128)(2,1)S(1)}, u32[]{:S(2)}, u32[]{:S(2)}) %collective-permute-start.14) | collective-permute-done | bytes 114720 | tf_op jit(solution)/shard_map/ppermute | solution.py:92
  94.1 0.1 fusion.13
  94.2 0.1 collective-permute-start.15
  94.4 1.3 %collective-permute-done.15 = bf16[8,7168]{1,0:T(8,128)(2,1)S(1)} collective-permute-done((bf16[8,7168]{1,0:T(8,128)(2,1)S(1)}, bf16[8,7168]{1,0:T(8,128)(2,1)S(1)}, u32[]{:S(2)}, u32[]{:S(2)}) %collective-permute-start.15) | collective-permute-done | bytes 114720 | tf_op jit(solution)/shard_map/ppermute | solution.py:98
  95.6 1.3 %convolution_convert_fusion.1 = bf16[64,7168]{1,0:T(8,128)(2,1)} fusion(bf16[8,7168]{1,0:T(8,128)(2,1)S(1)} %collective-permute-done.15, bf16[8,7168]{1,0:T(8,128)(2,1)S(1)} %reshape.74, bf16[16,64]{1,0:T(8,128)(2,1)S(1)} %fusion.23, bf16[16,64]{1,0:T(8,128)(2,1)S(1)} %get-tuple-element.5), kind=kOutput, calls=%fused_computation.1 | convolution fusion | flops 31662080 | bytes 1150976 | tf_op jit(solution)/shard_map/ct,cd->td/dot_general | solution.py:104
  (20 shorter events, 0.2 us)
Async XLA Ops:
  0.0 2.0 %copy-start = (bf16[64,7168]{1,0:T(8,128)(2,1)S(1)}, bf16[64,7168]{1,0:T(8,128)(2,1)}, u32[]{:S(2)}) copy-start(bf16[64,7168]{1,0:T(8,128)(2,1)} %param.6) | copy-start | bytes 2752516
  2.3 1.5 %collective-permute-start = (bf16[8,7168]{1,0:T(8,128)(2,1)S(1)}, bf16[8,7168]{1,0:T(8,128)(2,1)S(1)}, u32[]{:S(2)}, u32[]{:S(2)}) collective-permute-start(bf16[8,7168]{1,0:T(8,128)(2,1)S(1)} %get-tuple-element.19), channel_id=1, source_target_pairs={{0,4},{4,0},{8,12},{12,8},{1,5},{5,1},{9,13},{13,9},{2,6},{6,2},{1... | collective-permute-start | bytes 344072 | tf_op jit(solution)/shard_map/ppermute | solution.py:69
  3.9 6.4 %collective-permute-start.1 = (bf16[8,7168]{1,0:T(8,128)(2,1)S(1)}, bf16[8,7168]{1,0:T(8,128)(2,1)S(1)}, u32[]{:S(2)}, u32[]{:S(2)}) collective-permute-start(bf16[8,7168]{1,0:T(8,128)(2,1)S(1)} %fusion.15), channel_id=1, source_target_pairs={{0,8},{4,12},{8,0},{12,4},{1,9},{5,13},{9,1},{13,5},{2,10},{6,14},... | collective-permute-start | bytes 344072 | tf_op jit(solution)/shard_map/ppermute | solution.py:72
  10.2 6.6 %collective-permute-start.2 = (bf16[8,7168]{1,0:T(8,128)(2,1)S(1)}, bf16[8,7168]{1,0:T(8,128)(2,1)S(1)}, u32[]{:S(2)}, u32[]{:S(2)}) collective-permute-start(bf16[8,7168]{1,0:T(8,128)(2,1)S(1)} %collective-permute-done.1), channel_id=1, source_target_pairs={{0,1},{1,2},{2,3},{3,0},{4,5},{5,6},{6,7},{7,4},{8,9},{9,10},{10,1... | collective-permute-start | bytes 344072 | tf_op jit(solution)/shard_map/ppermute | solution.py:32
  16.9 6.6 %collective-permute-start.3 = (bf16[8,7168]{1,0:T(8,128)(2,1)S(1)}, bf16[8,7168]{1,0:T(8,128)(2,1)S(1)}, u32[]{:S(2)}, u32[]{:S(2)}) collective-permute-start(bf16[8,7168]{1,0:T(8,128)(2,1)S(1)} %collective-permute-done.2), channel_id=1, source_target_pairs={{0,1},{1,2},{2,3},{3,0},{4,5},{5,6},{6,7},{7,4},{8,9},{9,10},{10,1... | collective-permute-start | bytes 344072 | tf_op jit(solution)/shard_map/ppermute | solution.py:32
  23.4 6.6 %collective-permute-start.4 = (bf16[8,7168]{1,0:T(8,128)(2,1)S(1)}, bf16[8,7168]{1,0:T(8,128)(2,1)S(1)}, u32[]{:S(2)}, u32[]{:S(2)}) collective-permute-start(bf16[8,7168]{1,0:T(8,128)(2,1)S(1)} %collective-permute-done.3), channel_id=1, source_target_pairs={{0,1},{1,2},{2,3},{3,0},{4,5},{5,6},{6,7},{7,4},{8,9},{9,10},{10,1... | collective-permute-start | bytes 344072 | tf_op jit(solution)/shard_map/ppermute | solution.py:32
  30.1 7.3 %collective-permute-start.5 = (bf16[8,7168]{1,0:T(8,128)(2,1)S(1)}, bf16[8,7168]{1,0:T(8,128)(2,1)S(1)}, u32[]{:S(2)}, u32[]{:S(2)}) collective-permute-start(bf16[8,7168]{1,0:T(8,128)(2,1)S(1)} %get-tuple-element.8), channel_id=1, source_target_pairs={{0,1},{1,2},{2,3},{3,0},{4,5},{5,6},{6,7},{7,4},{8,9},{9,10},{10,1... | collective-permute-start | bytes 344072 | tf_op jit(solution)/shard_map/ppermute | solution.py:32
  37.4 7.3 %collective-permute-start.6 = (bf16[8,7168]{1,0:T(8,128)(2,1)S(1)}, bf16[8,7168]{1,0:T(8,128)(2,1)S(1)}, u32[]{:S(2)}, u32[]{:S(2)}) collective-permute-start(bf16[8,7168]{1,0:T(8,128)(2,1)S(1)} %collective-permute-done.5), channel_id=1, source_target_pairs={{0,1},{1,2},{2,3},{3,0},{4,5},{5,6},{6,7},{7,4},{8,9},{9,10},{10,1... | collective-permute-start | bytes 344072 | tf_op jit(solution)/shard_map/ppermute | solution.py:32
  44.7 6.6 %collective-permute-start.7 = (bf16[8,7168]{1,0:T(8,128)(2,1)S(1)}, bf16[8,7168]{1,0:T(8,128)(2,1)S(1)}, u32[]{:S(2)}, u32[]{:S(2)}) collective-permute-start(bf16[8,7168]{1,0:T(8,128)(2,1)S(1)} %collective-permute-done.6), channel_id=1, source_target_pairs={{0,1},{1,2},{2,3},{3,0},{4,5},{5,6},{6,7},{7,4},{8,9},{9,10},{10,1... | collective-permute-start | bytes 344072 | tf_op jit(solution)/shard_map/ppermute | solution.py:32
  63.7 7.9 %collective-permute-start.11 = (bf16[8,7168]{1,0:T(8,128)(2,1)S(1)}, bf16[8,7168]{1,0:T(8,128)(2,1)S(1)}, u32[]{:S(2)}, u32[]{:S(2)}) collective-permute-start(bf16[8,7168]{1,0:T(8,128)(2,1)S(1)} %get-tuple-element.16), channel_id=1, source_target_pairs={{0,1},{1,2},{2,3},{3,0},{4,5},{5,6},{6,7},{7,4},{8,9},{9,10},{10,1... | collective-permute-start | bytes 344072 | tf_op jit(solution)/shard_map/ppermute | solution.py:39
  63.8 9.1 %collective-permute-start.8 = (bf16[8,7168]{1,0:T(8,128)(2,1)S(1)}, bf16[8,7168]{1,0:T(8,128)(2,1)S(1)}, u32[]{:S(2)}, u32[]{:S(2)}) collective-permute-start(bf16[8,7168]{1,0:T(8,128)(2,1)S(1)} %get-tuple-element.15), channel_id=1, source_target_pairs={{0,1},{1,2},{2,3},{3,0},{4,5},{5,6},{6,7},{7,4},{8,9},{9,10},{10,1... | collective-permute-start | bytes 344072 | tf_op jit(solution)/shard_map/ppermute | solution.py:39
  73.0 7.1 %collective-permute-start.12 = (bf16[8,7168]{1,0:T(8,128)(2,1)S(1)}, bf16[8,7168]{1,0:T(8,128)(2,1)S(1)}, u32[]{:S(2)}, u32[]{:S(2)}) collective-permute-start(bf16[8,7168]{1,0:T(8,128)(2,1)S(1)} %get-tuple-element.14), channel_id=1, source_target_pairs={{0,1},{1,2},{2,3},{3,0},{4,5},{5,6},{6,7},{7,4},{8,9},{9,10},{10,1... | collective-permute-start | bytes 344072 | tf_op jit(solution)/shard_map/ppermute | solution.py:39
  73.0 8.2 %collective-permute-start.9 = (bf16[8,7168]{1,0:T(8,128)(2,1)S(1)}, bf16[8,7168]{1,0:T(8,128)(2,1)S(1)}, u32[]{:S(2)}, u32[]{:S(2)}) collective-permute-start(bf16[8,7168]{1,0:T(8,128)(2,1)S(1)} %get-tuple-element.13), channel_id=1, source_target_pairs={{0,1},{1,2},{2,3},{3,0},{4,5},{5,6},{6,7},{7,4},{8,9},{9,10},{10,1... | collective-permute-start | bytes 344072 | tf_op jit(solution)/shard_map/ppermute | solution.py:39
  81.3 6.6 %collective-permute-start.10 = (bf16[8,7168]{1,0:T(8,128)(2,1)S(1)}, bf16[8,7168]{1,0:T(8,128)(2,1)S(1)}, u32[]{:S(2)}, u32[]{:S(2)}) collective-permute-start(bf16[8,7168]{1,0:T(8,128)(2,1)S(1)} %get-tuple-element.11), channel_id=1, source_target_pairs={{0,1},{1,2},{2,3},{3,0},{4,5},{5,6},{6,7},{7,4},{8,9},{9,10},{10,1... | collective-permute-start | bytes 344072 | tf_op jit(solution)/shard_map/ppermute | solution.py:39
  81.4 7.8 %collective-permute-start.13 = (bf16[8,7168]{1,0:T(8,128)(2,1)S(1)}, bf16[8,7168]{1,0:T(8,128)(2,1)S(1)}, u32[]{:S(2)}, u32[]{:S(2)}) collective-permute-start(bf16[8,7168]{1,0:T(8,128)(2,1)S(1)} %get-tuple-element.12), channel_id=1, source_target_pairs={{0,1},{1,2},{2,3},{3,0},{4,5},{5,6},{6,7},{7,4},{8,9},{9,10},{10,1... | collective-permute-start | bytes 344072 | tf_op jit(solution)/shard_map/ppermute | solution.py:39
  89.3 4.9 %collective-permute-start.14 = (bf16[8,7168]{1,0:T(8,128)(2,1)S(1)}, bf16[8,7168]{1,0:T(8,128)(2,1)S(1)}, u32[]{:S(2)}, u32[]{:S(2)}) collective-permute-start(bf16[8,7168]{1,0:T(8,128)(2,1)S(1)} %get-tuple-element.10), channel_id=1, source_target_pairs={{0,8},{4,12},{8,0},{12,4},{1,9},{5,13},{9,1},{13,5},{2,10},{6,14},... | collective-permute-start | bytes 344072 | tf_op jit(solution)/shard_map/ppermute | solution.py:92
  94.2 1.4 %collective-permute-start.15 = (bf16[8,7168]{1,0:T(8,128)(2,1)S(1)}, bf16[8,7168]{1,0:T(8,128)(2,1)S(1)}, u32[]{:S(2)}, u32[]{:S(2)}) collective-permute-start(bf16[8,7168]{1,0:T(8,128)(2,1)S(1)} %reshape.75), channel_id=1, source_target_pairs={{0,4},{4,0},{8,12},{12,8},{1,5},{5,1},{9,13},{13,9},{2,6},{6,2},{1... | collective-permute-start | bytes 344072 | tf_op jit(solution)/shard_map/ppermute | solution.py:98

commit v2 on v1

--- a/solution.py
+++ b/solution.py
@@ -1,6 +1,10 @@
+import functools
+
 import jax
 import jax.numpy as jnp
 from jax import lax
+from jax.experimental import pallas as pl
+from jax.experimental.pallas import tpu as pltpu
 from jax.sharding import PartitionSpec as P
 
 CAP = 4
@@ -22,23 +26,53 @@
     return select, weight
 
 
-def ring(n):
-    return [(i, (i + 1) % n) for i in range(n)]
+def ffn_kernel(rows_ref, gate_ref, up_ref, down_ref, out_ref):
+    rows = rows_ref[...]
+    gate = jnp.dot(rows, gate_ref[0], preferred_element_type=jnp.float32)
+    up = jnp.dot(rows, up_ref[0], preferred_element_type=jnp.float32)
+    hidden = (gate / (1.0 + jnp.exp(-gate)) * up).astype(jnp.bfloat16)
+    width = out_ref.shape[1]
+    tile = 1024
+    for start in range(0, width, tile):
+        out_ref[:, start:start + tile] = jnp.dot(
+            hidden, down_ref[0, :, start:start + tile], preferred_element_type=jnp.float32
+        ).astype(out_ref.dtype)
 
 
-def gather_ring(block, n):
-    parts = [block]
-    for _ in range(n - 1):
-        parts.append(lax.ppermute(parts[-1], "dp", ring(n)))
-    return parts
+def hold_kernel(from_ref, to_ref, sem):
+    copy = pltpu.make_async_copy(from_ref, to_ref, sem)
+    copy.start()
+    copy.wait()
 
 
-def scatter_ring(parts, n):
-    total = parts[1 % n]
-    for step in range(1, n):
-        arrived = lax.ppermute(total, "dp", ring(n))
-        total = (arrived.astype(jnp.float32) + parts[(step + 1) % n].astype(jnp.float32)).astype(jnp.bfloat16)
-    return total
+def hold(weight):
+    return pl.pallas_call(
+        hold_kernel,
+        out_shape=pltpu.VMEM(weight.shape, weight.dtype),
+        in_specs=[pl.BlockSpec(memory_space=pltpu.HBM)],
+        out_specs=pl.BlockSpec(memory_space=pltpu.VMEM),
+        scratch_shapes=[pltpu.SemaphoreType.DMA],
+        compiler_params=pltpu.CompilerParams(vmem_limit_bytes=1024 * 1024),
+        cost_estimate=pl.CostEstimate(flops=0, bytes_accessed=4 * weight.size, transcendentals=0),
+    )(weight)
+
+
+def ffn(rows, w_gate, w_up, w_down):
+    vmem = pl.BlockSpec(memory_space=pltpu.VMEM)
+    held = [pltpu.with_memory_space_constraint(w, pltpu.VMEM) for w in (w_gate, w_up, w_down)]
+    units = w_gate.shape[2]
+    return pl.pallas_call(
+        ffn_kernel,
+        out_shape=jax.ShapeDtypeStruct(rows.shape, jnp.bfloat16),
+        in_specs=[vmem] * 4,
+        out_specs=vmem,
+        compiler_params=pltpu.CompilerParams(vmem_limit_bytes=8 * 1024 * 1024),
+        cost_estimate=pl.CostEstimate(
+            flops=6 * rows.shape[0] * rows.shape[1] * units,
+            bytes_accessed=2 * (3 * rows.shape[1] * units),
+            transcendentals=rows.shape[0] * units,
+        ),
+    )(rows, *held)
 
 
 def local(tokens, expert_ids, gate_weights, w_gate, w_up, w_down):
@@ -64,28 +98,41 @@
             (c * CORES + k, ((c + shift) % chips) * CORES + k) for c in range(chips) for k in range(CORES)
         ]
 
+    def along_dp(block, shift):
+        return lax.ppermute(block, "dp", [(i, (i + shift) % shards) for i in range(shards)])
+
+    shifts = sorted(range(1, shards), key=lambda s: abs(s - shards / 2))
+
     half = chips * CAP
     kept = outgoing[:half].reshape(chips, CAP, width)
     swapped = lax.ppermute(outgoing[half:], "expert", core_pairs).reshape(chips, CAP, width)
     blocks = jnp.concatenate([kept, swapped], axis=1)
     chunk_a = blocks[0]
     chunk_b = [lax.ppermute(blocks[shift], "expert", chip_pairs(shift)) for shift in range(1, chips)]
+    parts_a = {0: chunk_a}
+    for shift in shifts:
+        parts_a[shift] = along_dp(chunk_a, shift)
     chunk_b = jnp.concatenate(chunk_b, axis=0)
-    parts_a = gather_ring(chunk_a, shards)
-    parts_b = gather_ring(chunk_b, shards)
-    rows = jnp.concatenate(parts_b + parts_a, axis=0)
+    parts_b = {0: chunk_b}
+    for shift in shifts:
+        parts_b[shift] = along_dp(chunk_b, shift)
+    order = [0] + shifts
+    rows = jnp.concatenate([parts_a[s] for s in order] + [parts_b[s] for s in order], axis=0)
 
-    gate_proj = jnp.dot(rows, w_gate[0], preferred_element_type=jnp.float32)
-    up_proj = jnp.dot(rows, w_up[0], preferred_element_type=jnp.float32)
-    hidden = (jax.nn.silu(gate_proj) * up_proj).astype(jnp.bfloat16)
-    partial = jnp.dot(hidden, w_down[0], preferred_element_type=jnp.float32).astype(jnp.bfloat16)
+    w_gate, w_up, w_down, _ = lax.optimization_barrier((w_gate, w_up, w_down, chunk_b))
+    partial = ffn(rows, hold(w_gate), hold(w_up), hold(w_down))
 
     size_b, size_a = chunk_b.shape[0], chunk_a.shape[0]
-    back_b = [partial[i * size_b:(i + 1) * size_b] for i in range(shards)]
-    rest = partial[shards * size_b:]
-    back_a = [rest[i * size_a:(i + 1) * size_a] for i in range(shards)]
-    sum_b = scatter_ring(back_b, shards)
-    sum_a = scatter_ring(back_a, shards)
+
+    def sum_over_dp(parts, size):
+        arrived = [along_dp(parts[i * size:(i + 1) * size], shards - s) for i, s in enumerate(order) if s]
+        total = parts[:size].astype(jnp.float32)
+        for block in arrived:
+            total = total + block.astype(jnp.float32)
+        return total.astype(jnp.bfloat16)
+
+    sum_b = sum_over_dp(partial[shards * size_a:], size_b)
+    sum_a = sum_over_dp(partial[:shards * size_a], size_a)
     home = [sum_a]
     for shift in range(1, chips):
         home.append(

time: 97.3 us -> 67.4 us (0.69)
  waiting for transfers between devices: 73.4 us -> 28.1 us
  starting transfers between devices: 6.79 us -> 20.6 us
  matrix products: 14.1 us -> 1.72 us
  local copies, waits for them, and re-layouts: 0.37 us -> 8.65 us
  Pallas kernels: 0 us -> 5.49 us
    ppermute x12, waiting for transfers between devices: 64 us -> 22.6 us  [along_dp(): lax.ppermute(block, 'dp', [(i, (i + shift) % shards) for i in range(shard...]
    ppermute x12, starting transfers between devices: 2.25 us -> 15.4 us  [along_dp(): lax.ppermute(block, 'dp', [(i, (i + shift) % shards) for i in range(shard...]
    dot_general x2 -> x0, matrix products: 12.4 us -> none  [the longest x1 7.93 us: local(): jnp.dot(hidden, w_down[0], preferred_element_type=jnp.float32)]
    unnamed x8 -> x14, local copies, waits for them, and re-layouts: 0.05 us -> 8.3 us
    pallas_call x0 -> x4, Pallas kernels: none -> 5.49 us  [the longest x1 4 us: ffn(): pl.pallas_call(ffn_kernel, out_shape=jax.ShapeDtypeStruct(rows.shape, jnp...]
    ppermute x1, waiting for transfers between devices: 3.46 us -> 0.01 us  [local(): lax.ppermute(blocks[shift], 'expert', chip_pairs(shift))]
  transfers between devices with their start and end apart: 16 -> 16, of which waited for: 16 -> 6; matrix products, arithmetic and copies ran while one was open for 0% -> 0% of each run, Pallas kernels for 0% -> 2%
where the time goes in v2:
time: 67.4 us; the launch traced here: 66.9 us
  waiting for transfers between devices  28.1 us (42%)
  starting transfers between devices  20.6 us (31%)
  local copies, waits for them, and re-layouts  8.65 us (13%)
  Pallas kernels  5.49 us (8%)
  other arithmetic  2.06 us (3%)
  matrix products  1.72 us (3%)
    ppermute x12, waiting for transfers between devices, along_dp(): lax.ppermute(block, 'dp', [(i, (i + shift) % shards) for i in range(shard...  22.6 us
    ppermute x12, starting transfers between devices, along_dp(): lax.ppermute(block, 'dp', [(i, (i + shift) % shards) for i in range(shard...  15.4 us
    unnamed x14, local copies, waits for them, and re-layouts  8.3 us
    pallas_call x1, Pallas kernels, ffn(): pl.pallas_call(ffn_kernel, out_shape=jax.ShapeDtypeStruct(rows.shape, jnp...  4 us
    ppermute x1, waiting for transfers between devices, local(): lax.ppermute(sum_b[(shift - 1) * 2 * CAP:shift * 2 * CAP], 'expert', chip...  3.27 us
    ppermute x1, starting transfers between devices, local(): lax.ppermute(blocks[shift], 'expert', chip_pairs(shift))  2.91 us
    ppermute x1, starting transfers between devices, local(): lax.ppermute(sum_b[(shift - 1) * 2 * CAP:shift * 2 * CAP], 'expert', chip...  1.76 us
    pallas_call x3, Pallas kernels, hold(): pl.pallas_call(hold_kernel, out_shape=pltpu.VMEM(weight.shape, weight.dty...  1.49 us
  transfers between devices with their start and end apart: 16, of which 6 were waited for; matrix products, arithmetic and copies ran while one was open for 0% of the time, Pallas kernels for 2%

profile of v2, /device:TPU:0, one launch (start us, length us, event | category | flops | bytes accessed | tf_op | source)
XLA Modules:
  0.0 66.9 jit_solution(1044833935784714592)
XLA Ops:
  0.0 0.9 %compare_reduce_fusion = pred[64,4]{0,1:T(4,128)(4,1)S(1)} fusion(s32[64,8]{0,1:T(8,128)} %param.7, s32[4]{0:T(128)S(1)} %fusion.17), kind=kLoop, calls=%fused_computation.25 | loop fusion | flops 3840 | bytes 2320 | tf_op jit(solution)/shard_map/reduce_or | solution.py:16
  0.9 0.8 %fusion.12 = f32[64,4]{0,1:T(4,128)S(1)} fusion(f32[64,8]{0,1:T(8,128)} %param.8, s32[64,8]{0,1:T(8,128)} %param.7, s32[4]{0:T(128)S(1)} %fusion.17), kind=kLoop, calls=%fused_computation.34 | loop fusion | flops 5888 | bytes 5136 | tf_op jit(solution)/shard_map/reduce_sum | solution.py:17
  1.7 0.1 convolution_convert_fusion.2
  1.8 0.1 eq.46
  1.9 0.1 reduce-precision_convert_fusion
  2.0 0.2 convolution_convert_fusion.1
  2.3 0.5 collective-permute-start
  2.8 0.1 reshape.72
  2.8 0.9 %collective-permute-done = bf16[8,7168]{1,0:T(8,128)(2,1)S(1)} collective-permute-done((bf16[8,7168]{1,0:T(8,128)(2,1)S(1)}, bf16[8,7168]{1,0:T(8,128)(2,1)S(1)}, u32[]{:S(2)}, u32[]{:S(2)}) %collective-permute-start) | collective-permute-done | bytes 114720 | tf_op jit(solution)/shard_map/ppermute | solution.py:108
  3.7 0.1 reshape.73
  3.8 0.1 fusion.11
  3.9 2.9 %collective-permute-start.4 = (bf16[8,7168]{1,0:T(8,128)(2,1)S(1)}, bf16[8,7168]{1,0:T(8,128)(2,1)S(1)}, u32[]{:S(2)}, u32[]{:S(2)}) collective-permute-start(bf16[8,7168]{1,0:T(8,128)(2,1)S(1)} %fusion.11), channel_id=1, source_target_pairs={{0,8},{4,12},{8,0},{12,4},{1,9},{5,13},{9,1},{13,5},{2,10},{6,14},... | collective-permute-start | bytes 344072 | tf_op jit(solution)/shard_map/ppermute | solution.py:111
  6.8 0.1 constant_dynamic-update-slice_fusion.7
  6.8 2.7 %collective-permute-start.1 = (bf16[8,7168]{1,0:T(8,128)(2,1)S(1)}, bf16[8,7168]{1,0:T(8,128)(2,1)S(1)}, u32[]{:S(2)}, u32[]{:S(2)}) collective-permute-start(bf16[8,7168]{1,0:T(8,128)(2,1)S(1)} %get-tuple-element.14), channel_id=1, source_target_pairs={{0,2},{1,3},{2,0},{3,1},{4,6},{5,7},{6,4},{7,5},{8,10},{9,11},{10,... | collective-permute-start | bytes 344072 | tf_op jit(solution)/shard_map/ppermute | solution.py:102
  9.5 1.3 %collective-permute-start.3 = (bf16[8,7168]{1,0:T(8,128)(2,1)S(1)}, bf16[8,7168]{1,0:T(8,128)(2,1)S(1)}, u32[]{:S(2)}, u32[]{:S(2)}) collective-permute-start(bf16[8,7168]{1,0:T(8,128)(2,1)S(1)} %get-tuple-element.14), channel_id=1, source_target_pairs={{0,3},{1,0},{2,1},{3,2},{4,7},{5,4},{6,5},{7,6},{8,11},{9,8},{10,9... | collective-permute-start | bytes 344072 | tf_op jit(solution)/shard_map/ppermute | solution.py:102
  10.8 0.7 %collective-permute-start.2 = (bf16[8,7168]{1,0:T(8,128)(2,1)S(1)}, bf16[8,7168]{1,0:T(8,128)(2,1)S(1)}, u32[]{:S(2)}, u32[]{:S(2)}) collective-permute-start(bf16[8,7168]{1,0:T(8,128)(2,1)S(1)} %get-tuple-element.14), channel_id=1, source_target_pairs={{0,1},{1,2},{2,3},{3,0},{4,5},{5,6},{6,7},{7,4},{8,9},{9,10},{10,1... | collective-permute-start | bytes 344072 | tf_op jit(solution)/shard_map/ppermute | solution.py:102
  11.5 0.0 collective-permute-done.4
  11.5 3.1 %copy-done.1 = bf16[1,7168,512]{2,1,0:T(8,128)(2,1)S(1)} copy-done((bf16[1,7168,512]{2,1,0:T(8,128)(2,1)S(1)}, bf16[1,7168,512]{2,1,0:T(8,128)(2,1)}, u32[]{:S(2)}) %copy-start.1) | copy-done | bytes 7340056
  14.6 0.5 shard_map.64.gate_ref
  15.1 2.6 %copy-done.2 = bf16[1,7168,512]{2,1,0:T(8,128)(2,1)S(1)} copy-done((bf16[1,7168,512]{2,1,0:T(8,128)(2,1)S(1)}, bf16[1,7168,512]{2,1,0:T(8,128)(2,1)}, u32[]{:S(2)}) %copy-start.2) | copy-done | bytes 7340056
  17.7 0.5 shard_map.65.up_ref
  18.2 2.6 %copy-done.3 = bf16[1,512,7168]{2,1,0:T(8,128)(2,1)S(1)} copy-done((bf16[1,512,7168]{2,1,0:T(8,128)(2,1)S(1)}, bf16[1,512,7168]{2,1,0:T(8,128)(2,1)}, u32[]{:S(2)}) %copy-start.3) | copy-done | bytes 7340056
  20.8 0.5 shard_map.66.down_ref
  21.3 3.2 %collective-permute-start.7 = (bf16[8,7168]{1,0:T(8,128)(2,1)S(1)}, bf16[8,7168]{1,0:T(8,128)(2,1)S(1)}, u32[]{:S(2)}, u32[]{:S(2)}) collective-permute-start(bf16[8,7168]{1,0:T(8,128)(2,1)S(1)} %collective-permute-done.4), channel_id=1, source_target_pairs={{0,3},{1,0},{2,1},{3,2},{4,7},{5,4},{6,5},{7,6},{8,11},{9,8},{10,9... | collective-permute-start | bytes 344072 | tf_op jit(solution)/shard_map/ppermute | solution.py:102
  24.5 0.0 collective-permute-start.6
  24.5 0.0 collective-permute-done.1
  24.5 0.6 collective-permute-start.5
  25.2 9.3 %collective-permute-done.5 = bf16[8,7168]{1,0:T(8,128)(2,1)S(1)} collective-permute-done((bf16[8,7168]{1,0:T(8,128)(2,1)S(1)}, bf16[8,7168]{1,0:T(8,128)(2,1)S(1)}, u32[]{:S(2)}, u32[]{:S(2)}) %collective-permute-start.5) | collective-permute-done | bytes 114720 | tf_op jit(solution)/shard_map/ppermute | solution.py:102
  34.6 4.0 %shard_map.67 = bf16[64,7168]{1,0:T(8,128)(2,1)S(1)} custom-call(bf16[64,7168]{1,0:T(8,128)(2,1)S(1)} %constant_dynamic-update-slice_fusion.rows_ref, bf16[1,7168,512]{2,1,0:T(8,128)(2,1)S(1)} %shard_map.64.gate_ref, bf16[1,7168,512]{2,1,0:T(8,128)(2,1)S(1)} %shard_map.65.up_ref, bf16[1,512,7168]{2,1,0:T(8,128)(2,1)S(1)} %shard_map.66.down_ref), custom_call_target="tpu_custom_call" | custom-call | flops 1409286144 | bytes 22020096 | tf_op jit(solution)/shard_map/pallas_call | solution.py:64
  38.6 0.1 collective-permute-start.8
  38.7 2.5 %collective-permute-start.13 = (bf16[8,7168]{1,0:T(8,128)(2,1)S(1)}, bf16[8,7168]{1,0:T(8,128)(2,1)S(1)}, u32[]{:S(2)}, u32[]{:S(2)}) collective-permute-start(bf16[8,7168]{1,0:T(8,128)(2,1)S(1)} %get-tuple-element.18), channel_id=1, source_target_pairs={{0,1},{1,2},{2,3},{3,0},{4,5},{5,6},{6,7},{7,4},{8,9},{9,10},{10,1... | collective-permute-start | bytes 344072 | tf_op jit(solution)/shard_map/ppermute | solution.py:102
  41.3 1.3 %collective-permute-start.12 = (bf16[8,7168]{1,0:T(8,128)(2,1)S(1)}, bf16[8,7168]{1,0:T(8,128)(2,1)S(1)}, u32[]{:S(2)}, u32[]{:S(2)}) collective-permute-start(bf16[8,7168]{1,0:T(8,128)(2,1)S(1)} %get-tuple-element.19), channel_id=1, source_target_pairs={{0,3},{1,0},{2,1},{3,2},{4,7},{5,4},{6,5},{7,6},{8,11},{9,8},{10,9... | collective-permute-start | bytes 344072 | tf_op jit(solution)/shard_map/ppermute | solution.py:102
  42.6 1.1 %collective-permute-start.11 = (bf16[8,7168]{1,0:T(8,128)(2,1)S(1)}, bf16[8,7168]{1,0:T(8,128)(2,1)S(1)}, u32[]{:S(2)}, u32[]{:S(2)}) collective-permute-start(bf16[8,7168]{1,0:T(8,128)(2,1)S(1)} %get-tuple-element.20), channel_id=1, source_target_pairs={{0,2},{1,3},{2,0},{3,1},{4,6},{5,7},{6,4},{7,5},{8,10},{9,11},{10,... | collective-permute-start | bytes 344072 | tf_op jit(solution)/shard_map/ppermute | solution.py:102
  43.7 0.0 collective-permute-start.10
  43.7 6.1 %collective-permute-done.8 = bf16[8,7168]{1,0:T(8,128)(2,1)S(1)} collective-permute-done((bf16[8,7168]{1,0:T(8,128)(2,1)S(1)}, bf16[8,7168]{1,0:T(8,128)(2,1)S(1)}, u32[]{:S(2)}, u32[]{:S(2)}) %collective-permute-start.8) | collective-permute-done | bytes 114720 | tf_op jit(solution)/shard_map/ppermute | solution.py:102
  49.7 1.9 %collective-permute-start.9 = (bf16[8,7168]{1,0:T(8,128)(2,1)S(1)}, bf16[8,7168]{1,0:T(8,128)(2,1)S(1)}, u32[]{:S(2)}, u32[]{:S(2)}) collective-permute-start(bf16[8,7168]{1,0:T(8,128)(2,1)S(1)} %get-tuple-element.22), channel_id=1, source_target_pairs={{0,3},{1,0},{2,1},{3,2},{4,7},{5,4},{6,5},{7,6},{8,11},{9,8},{10,9... | collective-permute-start | bytes 344072 | tf_op jit(solution)/shard_map/ppermute | solution.py:102
  51.6 0.0 collective-permute-done.13
  51.6 0.0 collective-permute-done.12
  51.6 7.2 %collective-permute-done.11 = bf16[8,7168]{1,0:T(8,128)(2,1)S(1)} collective-permute-done((bf16[8,7168]{1,0:T(8,128)(2,1)S(1)}, bf16[8,7168]{1,0:T(8,128)(2,1)S(1)}, u32[]{:S(2)}, u32[]{:S(2)}) %collective-permute-start.11) | collective-permute-done | bytes 114720 | tf_op jit(solution)/shard_map/ppermute | solution.py:102
  58.8 0.0 collective-permute-done.10
  58.8 0.0 collective-permute-done.9
  58.8 0.1 fusion.7
  59.0 1.8 %collective-permute-start.14 = (bf16[8,7168]{1,0:T(8,128)(2,1)S(1)}, bf16[8,7168]{1,0:T(8,128)(2,1)S(1)}, u32[]{:S(2)}, u32[]{:S(2)}) collective-permute-start(bf16[8,7168]{1,0:T(8,128)(2,1)S(1)} %get-tuple-element.16), channel_id=1, source_target_pairs={{0,8},{4,12},{8,0},{12,4},{1,9},{5,13},{9,1},{13,5},{2,10},{6,14},... | collective-permute-start | bytes 344072 | tf_op jit(solution)/shard_map/ppermute | solution.py:139
  60.7 3.3 %collective-permute-done.14 = bf16[8,7168]{1,0:T(8,128)(2,1)S(1)} collective-permute-done((bf16[8,7168]{1,0:T(8,128)(2,1)S(1)}, bf16[8,7168]{1,0:T(8,128)(2,1)S(1)}, u32[]{:S(2)}, u32[]{:S(2)}) %collective-permute-start.14) | collective-permute-done | bytes 114720 | tf_op jit(solution)/shard_map/ppermute | solution.py:139
  64.0 0.1 fusion.8
  64.1 0.1 collective-permute-start.15
  64.2 1.3 %collective-permute-done.15 = bf16[8,7168]{1,0:T(8,128)(2,1)S(1)} collective-permute-done((bf16[8,7168]{1,0:T(8,128)(2,1)S(1)}, bf16[8,7168]{1,0:T(8,128)(2,1)S(1)}, u32[]{:S(2)}, u32[]{:S(2)}) %collective-permute-start.15) | collective-permute-done | bytes 114720 | tf_op jit(solution)/shard_map/ppermute | solution.py:145
  65.5 1.4 %convolution_convert_fusion = bf16[64,7168]{1,0:T(8,128)(2,1)} fusion(bf16[8,7168]{1,0:T(8,128)(2,1)S(1)} %collective-permute-done.15, bf16[8,7168]{1,0:T(8,128)(2,1)S(1)} %reshape.74, bf16[16,64]{1,0:T(8,128)(2,1)S(1)} %fusion.13, bf16[16,64]{1,0:T(8,128)(2,1)S(1)} %get-tuple-element.11), kind=kOutput, calls=%fused_computation | convolution fusion | flops 31662080 | bytes 1150976 | tf_op jit(solution)/shard_map/ct,cd->td/dot_general | solution.py:151
  (26 shorter events, 0.3 us)
Async XLA Ops:
  0.0 2.0 %copy-start = (bf16[64,7168]{1,0:T(8,128)(2,1)S(1)}, bf16[64,7168]{1,0:T(8,128)(2,1)}, u32[]{:S(2)}) copy-start(bf16[64,7168]{1,0:T(8,128)(2,1)} %param.6) | copy-start | bytes 2752516
  2.3 1.5 %collective-permute-start = (bf16[8,7168]{1,0:T(8,128)(2,1)S(1)}, bf16[8,7168]{1,0:T(8,128)(2,1)S(1)}, u32[]{:S(2)}, u32[]{:S(2)}) collective-permute-start(bf16[8,7168]{1,0:T(8,128)(2,1)S(1)} %get-tuple-element.26), channel_id=1, source_target_pairs={{0,4},{4,0},{8,12},{12,8},{1,5},{5,1},{9,13},{13,9},{2,6},{6,2},{1... | collective-permute-start | bytes 344072 | tf_op jit(solution)/shard_map/ppermute | solution.py:108
  3.9 7.7 %collective-permute-start.4 = (bf16[8,7168]{1,0:T(8,128)(2,1)S(1)}, bf16[8,7168]{1,0:T(8,128)(2,1)S(1)}, u32[]{:S(2)}, u32[]{:S(2)}) collective-permute-start(bf16[8,7168]{1,0:T(8,128)(2,1)S(1)} %fusion.11), channel_id=1, source_target_pairs={{0,8},{4,12},{8,0},{12,4},{1,9},{5,13},{9,1},{13,5},{2,10},{6,14},... | collective-permute-start | bytes 344072 | tf_op jit(solution)/shard_map/ppermute | solution.py:111
  6.8 17.6 %collective-permute-start.1 = (bf16[8,7168]{1,0:T(8,128)(2,1)S(1)}, bf16[8,7168]{1,0:T(8,128)(2,1)S(1)}, u32[]{:S(2)}, u32[]{:S(2)}) collective-permute-start(bf16[8,7168]{1,0:T(8,128)(2,1)S(1)} %get-tuple-element.14), channel_id=1, source_target_pairs={{0,2},{1,3},{2,0},{3,1},{4,6},{5,7},{6,4},{7,5},{8,10},{9,11},{10,... | collective-permute-start | bytes 344072 | tf_op jit(solution)/shard_map/ppermute | solution.py:102
  9.5 15.7 %collective-permute-start.3 = (bf16[8,7168]{1,0:T(8,128)(2,1)S(1)}, bf16[8,7168]{1,0:T(8,128)(2,1)S(1)}, u32[]{:S(2)}, u32[]{:S(2)}) collective-permute-start(bf16[8,7168]{1,0:T(8,128)(2,1)S(1)} %get-tuple-element.14), channel_id=1, source_target_pairs={{0,3},{1,0},{2,1},{3,2},{4,7},{5,4},{6,5},{7,6},{8,11},{9,8},{10,9... | collective-permute-start | bytes 344072 | tf_op jit(solution)/shard_map/ppermute | solution.py:102
  10.8 14.3 %collective-permute-start.2 = (bf16[8,7168]{1,0:T(8,128)(2,1)S(1)}, bf16[8,7168]{1,0:T(8,128)(2,1)S(1)}, u32[]{:S(2)}, u32[]{:S(2)}) collective-permute-start(bf16[8,7168]{1,0:T(8,128)(2,1)S(1)} %get-tuple-element.14), channel_id=1, source_target_pairs={{0,1},{1,2},{2,3},{3,0},{4,5},{5,6},{6,7},{7,4},{8,9},{9,10},{10,1... | collective-permute-start | bytes 344072 | tf_op jit(solution)/shard_map/ppermute | solution.py:102
  11.5 3.1 %copy-start.1 = (bf16[1,7168,512]{2,1,0:T(8,128)(2,1)S(1)}, bf16[1,7168,512]{2,1,0:T(8,128)(2,1)}, u32[]{:S(2)}) copy-start(bf16[1,7168,512]{2,1,0:T(8,128)(2,1)} %from_ref) | copy-start | bytes 22020100
  14.6 3.1 %copy-start.2 = (bf16[1,7168,512]{2,1,0:T(8,128)(2,1)S(1)}, bf16[1,7168,512]{2,1,0:T(8,128)(2,1)}, u32[]{:S(2)}) copy-start(bf16[1,7168,512]{2,1,0:T(8,128)(2,1)} %from_ref.1) | copy-start | bytes 22020100
  17.7 3.1 %copy-start.3 = (bf16[1,512,7168]{2,1,0:T(8,128)(2,1)S(1)}, bf16[1,512,7168]{2,1,0:T(8,128)(2,1)}, u32[]{:S(2)}) copy-start(bf16[1,512,7168]{2,1,0:T(8,128)(2,1)} %from_ref.2) | copy-start | bytes 22020100
  21.3 13.3 %collective-permute-start.7 = (bf16[8,7168]{1,0:T(8,128)(2,1)S(1)}, bf16[8,7168]{1,0:T(8,128)(2,1)S(1)}, u32[]{:S(2)}, u32[]{:S(2)}) collective-permute-start(bf16[8,7168]{1,0:T(8,128)(2,1)S(1)} %collective-permute-done.4), channel_id=1, source_target_pairs={{0,3},{1,0},{2,1},{3,2},{4,7},{5,4},{6,5},{7,6},{8,11},{9,8},{10,9... | collective-permute-start | bytes 344072 | tf_op jit(solution)/shard_map/ppermute | solution.py:102
  24.5 10.0 %collective-permute-start.6 = (bf16[8,7168]{1,0:T(8,128)(2,1)S(1)}, bf16[8,7168]{1,0:T(8,128)(2,1)S(1)}, u32[]{:S(2)}, u32[]{:S(2)}) collective-permute-start(bf16[8,7168]{1,0:T(8,128)(2,1)S(1)} %collective-permute-done.4), channel_id=1, source_target_pairs={{0,1},{1,2},{2,3},{3,0},{4,5},{5,6},{6,7},{7,4},{8,9},{9,10},{10,1... | collective-permute-start | bytes 344072 | tf_op jit(solution)/shard_map/ppermute | solution.py:102
  24.5 10.0 %collective-permute-start.5 = (bf16[8,7168]{1,0:T(8,128)(2,1)S(1)}, bf16[8,7168]{1,0:T(8,128)(2,1)S(1)}, u32[]{:S(2)}, u32[]{:S(2)}) collective-permute-start(bf16[8,7168]{1,0:T(8,128)(2,1)S(1)} %collective-permute-done.4), channel_id=1, source_target_pairs={{0,2},{1,3},{2,0},{3,1},{4,6},{5,7},{6,4},{7,5},{8,10},{9,11},{10,... | collective-permute-start | bytes 344072 | tf_op jit(solution)/shard_map/ppermute | solution.py:102
  38.6 11.1 %collective-permute-start.8 = (bf16[8,7168]{1,0:T(8,128)(2,1)S(1)}, bf16[8,7168]{1,0:T(8,128)(2,1)S(1)}, u32[]{:S(2)}, u32[]{:S(2)}) collective-permute-start(bf16[8,7168]{1,0:T(8,128)(2,1)S(1)} %get-tuple-element.17), channel_id=1, source_target_pairs={{0,2},{1,3},{2,0},{3,1},{4,6},{5,7},{6,4},{7,5},{8,10},{9,11},{10,... | collective-permute-start | bytes 344072 | tf_op jit(solution)/shard_map/ppermute | solution.py:102
  38.7 12.9 %collective-permute-start.13 = (bf16[8,7168]{1,0:T(8,128)(2,1)S(1)}, bf16[8,7168]{1,0:T(8,128)(2,1)S(1)}, u32[]{:S(2)}, u32[]{:S(2)}) collective-permute-start(bf16[8,7168]{1,0:T(8,128)(2,1)S(1)} %get-tuple-element.18), channel_id=1, source_target_pairs={{0,1},{1,2},{2,3},{3,0},{4,5},{5,6},{6,7},{7,4},{8,9},{9,10},{10,1... | collective-permute-start | bytes 344072 | tf_op jit(solution)/shard_map/ppermute | solution.py:102
  41.3 10.3 %collective-permute-start.12 = (bf16[8,7168]{1,0:T(8,128)(2,1)S(1)}, bf16[8,7168]{1,0:T(8,128)(2,1)S(1)}, u32[]{:S(2)}, u32[]{:S(2)}) collective-permute-start(bf16[8,7168]{1,0:T(8,128)(2,1)S(1)} %get-tuple-element.19), channel_id=1, source_target_pairs={{0,3},{1,0},{2,1},{3,2},{4,7},{5,4},{6,5},{7,6},{8,11},{9,8},{10,9... | collective-permute-start | bytes 344072 | tf_op jit(solution)/shard_map/ppermute | solution.py:102
  42.6 16.2 %collective-permute-start.11 = (bf16[8,7168]{1,0:T(8,128)(2,1)S(1)}, bf16[8,7168]{1,0:T(8,128)(2,1)S(1)}, u32[]{:S(2)}, u32[]{:S(2)}) collective-permute-start(bf16[8,7168]{1,0:T(8,128)(2,1)S(1)} %get-tuple-element.20), channel_id=1, source_target_pairs={{0,2},{1,3},{2,0},{3,1},{4,6},{5,7},{6,4},{7,5},{8,10},{9,11},{10,... | collective-permute-start | bytes 344072 | tf_op jit(solution)/shard_map/ppermute | solution.py:102
  43.7 15.2 %collective-permute-start.10 = (bf16[8,7168]{1,0:T(8,128)(2,1)S(1)}, bf16[8,7168]{1,0:T(8,128)(2,1)S(1)}, u32[]{:S(2)}, u32[]{:S(2)}) collective-permute-start(bf16[8,7168]{1,0:T(8,128)(2,1)S(1)} %get-tuple-element.21), channel_id=1, source_target_pairs={{0,1},{1,2},{2,3},{3,0},{4,5},{5,6},{6,7},{7,4},{8,9},{9,10},{10,1... | collective-permute-start | bytes 344072 | tf_op jit(solution)/shard_map/ppermute | solution.py:102
  49.7 9.1 %collective-permute-start.9 = (bf16[8,7168]{1,0:T(8,128)(2,1)S(1)}, bf16[8,7168]{1,0:T(8,128)(2,1)S(1)}, u32[]{:S(2)}, u32[]{:S(2)}) collective-permute-start(bf16[8,7168]{1,0:T(8,128)(2,1)S(1)} %get-tuple-element.22), channel_id=1, source_target_pairs={{0,3},{1,0},{2,1},{3,2},{4,7},{5,4},{6,5},{7,6},{8,11},{9,8},{10,9... | collective-permute-start | bytes 344072 | tf_op jit(solution)/shard_map/ppermute | solution.py:102
  59.0 5.0 %collective-permute-start.14 = (bf16[8,7168]{1,0:T(8,128)(2,1)S(1)}, bf16[8,7168]{1,0:T(8,128)(2,1)S(1)}, u32[]{:S(2)}, u32[]{:S(2)}) collective-permute-start(bf16[8,7168]{1,0:T(8,128)(2,1)S(1)} %get-tuple-element.16), channel_id=1, source_target_pairs={{0,8},{4,12},{8,0},{12,4},{1,9},{5,13},{9,1},{13,5},{2,10},{6,14},... | collective-permute-start | bytes 344072 | tf_op jit(solution)/shard_map/ppermute | solution.py:139
  64.1 1.4 %collective-permute-start.15 = (bf16[8,7168]{1,0:T(8,128)(2,1)S(1)}, bf16[8,7168]{1,0:T(8,128)(2,1)S(1)}, u32[]{:S(2)}, u32[]{:S(2)}) collective-permute-start(bf16[8,7168]{1,0:T(8,128)(2,1)S(1)} %reshape.75), channel_id=1, source_target_pairs={{0,4},{4,0},{8,12},{12,8},{1,5},{5,1},{9,13},{13,9},{2,6},{6,2},{1... | collective-permute-start | bytes 344072 | tf_op jit(solution)/shard_map/ppermute | solution.py:145

commit v3 on v1

--- a/solution.py
+++ b/solution.py
@@ -1,6 +1,10 @@
+import functools
+
 import jax
 import jax.numpy as jnp
 from jax import lax
+from jax.experimental import pallas as pl
+from jax.experimental.pallas import tpu as pltpu
 from jax.sharding import PartitionSpec as P
 
 CAP = 4
@@ -22,23 +26,95 @@
     return select, weight
 
 
-def ring(n):
-    return [(i, (i + 1) % n) for i in range(n)]
-
-
-def gather_ring(block, n):
-    parts = [block]
-    for _ in range(n - 1):
-        parts.append(lax.ppermute(parts[-1], "dp", ring(n)))
-    return parts
-
-
-def scatter_ring(parts, n):
-    total = parts[1 % n]
-    for step in range(1, n):
-        arrived = lax.ppermute(total, "dp", ring(n))
-        total = (arrived.astype(jnp.float32) + parts[(step + 1) % n].astype(jnp.float32)).astype(jnp.bfloat16)
-    return total
+PIECES = 4
+STEPS = 4
+
+
+def hold_kernel(gate_from, up_from, gate_to, up_to, sems):
+    copies = []
+    for which, (source, target) in enumerate(((gate_from, gate_to), (up_from, up_to))):
+        rows = source.shape[1] // PIECES
+        for piece in range(PIECES):
+            at = pl.ds(piece * rows, rows)
+            copies.append(
+                pltpu.make_async_copy(source.at[:, at], target.at[:, at], sems.at[which, piece])
+            )
+    for copy in copies:
+        copy.start()
+    for copy in copies:
+        copy.wait()
+
+
+def hold(w_gate, w_up):
+    in_hbm = [pltpu.with_memory_space_constraint(w, pltpu.HBM) for w in (w_gate, w_up)]
+    return pl.pallas_call(
+        hold_kernel,
+        out_shape=[pltpu.VMEM(w.shape, w.dtype) for w in (w_gate, w_up)],
+        in_specs=[pl.BlockSpec(memory_space=pltpu.HBM)] * 2,
+        out_specs=[pl.BlockSpec(memory_space=pltpu.VMEM)] * 2,
+        scratch_shapes=[pltpu.SemaphoreType.DMA((2, PIECES))],
+        compiler_params=pltpu.CompilerParams(vmem_limit_bytes=1024 * 1024),
+        cost_estimate=pl.CostEstimate(flops=0, bytes_accessed=4 * w_gate.size, transcendentals=0),
+    )(*in_hbm)
+
+
+def ffn_kernel(rows_ref, gate_ref, up_ref, down_hbm, out_ref, down_ref, gate_sum, up_sum, sems):
+    units = down_hbm.shape[1] // PIECES
+    copies = []
+    for piece in range(PIECES):
+        at = pl.ds(piece * units, units)
+        copies.append(pltpu.make_async_copy(down_hbm.at[0, at], down_ref.at[at], sems.at[piece]))
+    for copy in copies:
+        copy.start()
+    depth = rows_ref.shape[1] // STEPS
+    gate_sum[...] = jnp.zeros_like(gate_sum)
+    up_sum[...] = jnp.zeros_like(up_sum)
+
+    @pl.loop(0, STEPS)
+    def _(step):
+        at = pl.ds(pl.multiple_of(step * depth, 128), depth)
+        rows = rows_ref[:, at]
+        gate_sum[...] += jnp.dot(rows, gate_ref[0, at], preferred_element_type=jnp.float32)
+        up_sum[...] += jnp.dot(rows, up_ref[0, at], preferred_element_type=jnp.float32)
+
+    gate, up = gate_sum[...], up_sum[...]
+    hidden = (gate / (1.0 + jnp.exp(-gate)) * up).astype(jnp.bfloat16)
+    for copy in copies:
+        copy.wait()
+    width = out_ref.shape[1]
+    tile = 1024
+    for start in range(0, width, tile):
+        out_ref[:, start:start + tile] = jnp.dot(
+            hidden, down_ref[:, start:start + tile], preferred_element_type=jnp.float32
+        ).astype(out_ref.dtype)
+
+
+def ffn(rows, gate, up, w_down):
+    vmem = pl.BlockSpec(memory_space=pltpu.VMEM)
+    units, width = w_down.shape[1:]
+    return pl.pallas_call(
+        ffn_kernel,
+        out_shape=jax.ShapeDtypeStruct(rows.shape, jnp.bfloat16),
+        in_specs=[vmem] * 3 + [pl.BlockSpec(memory_space=pltpu.HBM)],
+        out_specs=vmem,
+        scratch_shapes=[
+            pltpu.VMEM((units, width), w_down.dtype),
+            pltpu.VMEM((rows.shape[0], units), jnp.float32),
+            pltpu.VMEM((rows.shape[0], units), jnp.float32),
+            pltpu.SemaphoreType.DMA((PIECES,)),
+        ],
+        compiler_params=pltpu.CompilerParams(vmem_limit_bytes=16 * 1024 * 1024),
+        cost_estimate=pl.CostEstimate(
+            flops=6 * rows.shape[0] * width * units,
+            bytes_accessed=2 * width * units,
+            transcendentals=rows.shape[0] * units,
+        ),
+    )(
+        rows,
+        pltpu.with_memory_space_constraint(gate, pltpu.VMEM),
+        pltpu.with_memory_space_constraint(up, pltpu.VMEM),
+        pltpu.with_memory_space_constraint(w_down, pltpu.HBM),
+    )
 
 
 def local(tokens, expert_ids, gate_weights, w_gate, w_up, w_down):
@@ -59,40 +135,38 @@
 
     core_pairs = [(i, i ^ 1) for i in range(window)]
 
-    def chip_pairs(shift):
-        return [
-            (c * CORES + k, ((c + shift) % chips) * CORES + k) for c in range(chips) for k in range(CORES)
-        ]
+    def travel(block, chip_shift, dp_shift):
+        pairs = []
+        for c in range(chips):
+            for k in range(CORES):
+                for z in range(shards):
+                    to_chip, to_shard = (c + chip_shift) % chips, (z + dp_shift) % shards
+                    pairs.append(((c * CORES + k) * shards + z, (to_chip * CORES + k) * shards + to_shard))
+        return lax.ppermute(block, ("expert", "dp"), pairs)
+
+    ways = [(x, z) for z in sorted(range(shards), key=lambda z: -min(z, shards - z)) for x in range(chips)]
 
     half = chips * CAP
     kept = outgoing[:half].reshape(chips, CAP, width)
     swapped = lax.ppermute(outgoing[half:], "expert", core_pairs).reshape(chips, CAP, width)
     blocks = jnp.concatenate([kept, swapped], axis=1)
-    chunk_a = blocks[0]
-    chunk_b = [lax.ppermute(blocks[shift], "expert", chip_pairs(shift)) for shift in range(1, chips)]
-    chunk_b = jnp.concatenate(chunk_b, axis=0)
-    parts_a = gather_ring(chunk_a, shards)
-    parts_b = gather_ring(chunk_b, shards)
-    rows = jnp.concatenate(parts_b + parts_a, axis=0)
-
-    gate_proj = jnp.dot(rows, w_gate[0], preferred_element_type=jnp.float32)
-    up_proj = jnp.dot(rows, w_up[0], preferred_element_type=jnp.float32)
-    hidden = (jax.nn.silu(gate_proj) * up_proj).astype(jnp.bfloat16)
-    partial = jnp.dot(hidden, w_down[0], preferred_element_type=jnp.float32).astype(jnp.bfloat16)
-
-    size_b, size_a = chunk_b.shape[0], chunk_a.shape[0]
-    back_b = [partial[i * size_b:(i + 1) * size_b] for i in range(shards)]
-    rest = partial[shards * size_b:]
-    back_a = [rest[i * size_a:(i + 1) * size_a] for i in range(shards)]
-    sum_b = scatter_ring(back_b, shards)
-    sum_a = scatter_ring(back_a, shards)
-    home = [sum_a]
-    for shift in range(1, chips):
-        home.append(
-            lax.ppermute(
-                sum_b[(shift - 1) * 2 * CAP:shift * 2 * CAP], "expert", chip_pairs(chips - shift)
-            )
-        )
+    arrived = [travel(blocks[x], x, z) if (x, z) != (0, 0) else blocks[0] for x, z in ways]
+    rows = jnp.concatenate(arrived, axis=0)
+
+    w_gate, w_up, _ = lax.optimization_barrier((w_gate, w_up, swapped))
+    partial = ffn(rows, *hold(w_gate, w_up), w_down)
+
+    partial = partial.reshape(len(ways), CORES * CAP, width)
+    returned = {
+        way: travel(partial[i], (chips - way[0]) % chips, (shards - way[1]) % shards) if way != (0, 0) else partial[i]
+        for i, way in enumerate(ways)
+    }
+    home = []
+    for x in range(chips):
+        total = returned[x, 0].astype(jnp.float32)
+        for z in range(1, shards):
+            total = total + returned[x, z].astype(jnp.float32)
+        home.append(total.astype(jnp.bfloat16))
     home = jnp.stack(home)
     mine = home[:, :CAP].reshape(half, width)
     other = lax.ppermute(home[:, CAP:].reshape(half, width), "expert", core_pairs)

time: 97.3 us -> 62 us (0.64)
  waiting for transfers between devices: 73.4 us -> 21.2 us
  starting transfers between devices: 6.79 us -> 26.3 us
  matrix products: 14.1 us -> 1.72 us
  Pallas kernels: 0 us -> 9.88 us
    ppermute x14, waiting for transfers between devices: 71.2 us -> 19 us  [travel(): return lax.ppermute(block, ('expert', 'dp'), pairs)]
    ppermute x14, starting transfers between devices: 6.2 us -> 25.7 us  [travel(): return lax.ppermute(block, ('expert', 'dp'), pairs)]
    dot_general x2 -> x0, matrix products: 12.4 us -> none  [the longest x1 7.93 us: local(): jnp.dot(hidden, w_down[0], preferred_element_type=jnp.float32)]
    pallas_call x0 -> x2, Pallas kernels: none -> 9.88 us  [the longest x1 5.31 us: hold(): pl.pallas_call(hold_kernel, out_shape=[pltpu.VMEM(w.shape, w.dtype) for w...]
  transfers between devices with their start and end apart: 16 -> 16, of which waited for: 16 -> 7; matrix products, arithmetic and copies ran while one was open for 0% -> 0% of each run, Pallas kernels for 0% -> 9%
where the time goes in v3:
time: 62 us; the launch traced here: 61.8 us
  starting transfers between devices  26.3 us (42%)
  waiting for transfers between devices  21.2 us (34%)
  Pallas kernels  9.88 us (16%)
  other arithmetic  2.06 us (3%)
  matrix products  1.72 us (3%)
    ppermute x14, starting transfers between devices, travel(): return lax.ppermute(block, ('expert', 'dp'), pairs)  25.7 us
    ppermute x14, waiting for transfers between devices, travel(): return lax.ppermute(block, ('expert', 'dp'), pairs)  19 us
    pallas_call x1, Pallas kernels, hold(): pl.pallas_call(hold_kernel, out_shape=[pltpu.VMEM(w.shape, w.dtype) for w...  5.31 us
    pallas_call x1, Pallas kernels, ffn(): pl.pallas_call(ffn_kernel, out_shape=jax.ShapeDtypeStruct(rows.shape, jnp...  4.57 us
    dot_general x1, matrix products, local(): jnp.einsum('ct,cd->td', jnp.concatenate([high, low], axis=0).astype(jnp.b...  1.35 us
    ppermute x1, waiting for transfers between devices, local(): lax.ppermute(home[:, CAP:].reshape(half, width), 'expert', core_pairs)  1.26 us
  transfers between devices with their start and end apart: 16, of which 7 were waited for; matrix products, arithmetic and copies ran while one was open for 0% of the time, Pallas kernels for 9%

profile of v3, /device:TPU:0, one launch (start us, length us, event | category | flops | bytes accessed | tf_op | source)
XLA Modules:
  0.0 61.8 jit_solution(8402959165430240190)
XLA Ops:
  0.0 0.9 %compare_reduce_fusion = pred[64,4]{0,1:T(4,128)(4,1)S(1)} fusion(s32[64,8]{0,1:T(8,128)} %param.7, s32[4]{0:T(128)S(1)} %fusion.18), kind=kLoop, calls=%fused_computation.26 | loop fusion | flops 3840 | bytes 2320 | tf_op jit(solution)/shard_map/reduce_or | solution.py:16
  0.9 0.8 %fusion.13 = f32[64,4]{0,1:T(4,128)S(1)} fusion(f32[64,8]{0,1:T(8,128)} %param.8, s32[64,8]{0,1:T(8,128)} %param.7, s32[4]{0:T(128)S(1)} %fusion.18), kind=kLoop, calls=%fused_computation.35 | loop fusion | flops 5888 | bytes 5136 | tf_op jit(solution)/shard_map/reduce_sum | solution.py:17
  1.7 0.1 convolution_convert_fusion.2
  1.8 0.1 eq.46
  1.9 0.1 reduce-precision_convert_fusion
  2.0 0.2 convolution_convert_fusion.1
  2.3 0.5 collective-permute-start
  2.8 0.1 reshape.89
  2.8 0.9 %collective-permute-done = bf16[8,7168]{1,0:T(8,128)(2,1)S(1)} collective-permute-done((bf16[8,7168]{1,0:T(8,128)(2,1)S(1)}, bf16[8,7168]{1,0:T(8,128)(2,1)S(1)}, u32[]{:S(2)}, u32[]{:S(2)}) %collective-permute-start) | collective-permute-done | bytes 114720 | tf_op jit(solution)/shard_map/ppermute | solution.py:151
  3.7 0.1 reshape.90
  3.8 0.1 fusion.12
  3.9 4.0 %collective-permute-start.1 = (bf16[8,7168]{1,0:T(8,128)(2,1)S(1)}, bf16[8,7168]{1,0:T(8,128)(2,1)S(1)}, u32[]{:S(2)}, u32[]{:S(2)}) collective-permute-start(bf16[8,7168]{1,0:T(8,128)(2,1)S(1)} %get-tuple-element.25), channel_id=1, source_target_pairs={{0,2},{1,3},{2,0},{3,1},{4,6},{5,7},{6,4},{7,5},{8,10},{9,11},{10,... | collective-permute-start | bytes 344072 | tf_op jit(solution)/shard_map/ppermute | solution.py:145
  7.9 1.5 %collective-permute-start.7 = (bf16[8,7168]{1,0:T(8,128)(2,1)S(1)}, bf16[8,7168]{1,0:T(8,128)(2,1)S(1)}, u32[]{:S(2)}, u32[]{:S(2)}) collective-permute-start(bf16[8,7168]{1,0:T(8,128)(2,1)S(1)} %get-tuple-element.24), channel_id=1, source_target_pairs={{0,8},{1,9},{2,10},{3,11},{4,12},{5,13},{6,14},{7,15},{8,0},{9,1},... | collective-permute-start | bytes 344072 | tf_op jit(solution)/shard_map/ppermute | solution.py:145
  9.4 1.3 %collective-permute-start.6 = (bf16[8,7168]{1,0:T(8,128)(2,1)S(1)}, bf16[8,7168]{1,0:T(8,128)(2,1)S(1)}, u32[]{:S(2)}, u32[]{:S(2)}) collective-permute-start(bf16[8,7168]{1,0:T(8,128)(2,1)S(1)} %get-tuple-element.24), channel_id=1, source_target_pairs={{0,11},{1,8},{2,9},{3,10},{4,15},{5,12},{6,13},{7,14},{8,3},{9,0},... | collective-permute-start | bytes 344072 | tf_op jit(solution)/shard_map/ppermute | solution.py:145
  10.7 1.6 %collective-permute-start.4 = (bf16[8,7168]{1,0:T(8,128)(2,1)S(1)}, bf16[8,7168]{1,0:T(8,128)(2,1)S(1)}, u32[]{:S(2)}, u32[]{:S(2)}) collective-permute-start(bf16[8,7168]{1,0:T(8,128)(2,1)S(1)} %get-tuple-element.24), channel_id=1, source_target_pairs={{0,9},{1,10},{2,11},{3,8},{4,13},{5,14},{6,15},{7,12},{8,1},{9,2},... | collective-permute-start | bytes 344072 | tf_op jit(solution)/shard_map/ppermute | solution.py:145
  12.3 1.0 %collective-permute-start.2 = (bf16[8,7168]{1,0:T(8,128)(2,1)S(1)}, bf16[8,7168]{1,0:T(8,128)(2,1)S(1)}, u32[]{:S(2)}, u32[]{:S(2)}) collective-permute-start(bf16[8,7168]{1,0:T(8,128)(2,1)S(1)} %get-tuple-element.24), channel_id=1, source_target_pairs={{0,10},{1,11},{2,8},{3,9},{4,14},{5,15},{6,12},{7,13},{8,2},{9,3},... | collective-permute-start | bytes 344072 | tf_op jit(solution)/shard_map/ppermute | solution.py:145
  13.4 5.3 %shard_map.64 = (bf16[1,7168,512]{2,1,0:T(8,128)(2,1)S(1)}, bf16[1,7168,512]{2,1,0:T(8,128)(2,1)S(1)}) custom-call(bf16[1,7168,512]{2,1,0:T(8,128)(2,1)} %gate_from, bf16[1,7168,512]{2,1,0:T(8,128)(2,1)} %up_from), custom_call_target="tpu_custom_call" | custom-call | bytes 14680064 | tf_op jit(solution)/shard_map/pallas_call | solution.py:50
  18.7 0.0 collective-permute-done.1
  18.7 3.7 %collective-permute-start.5 = (bf16[8,7168]{1,0:T(8,128)(2,1)S(1)}, bf16[8,7168]{1,0:T(8,128)(2,1)S(1)}, u32[]{:S(2)}, u32[]{:S(2)}) collective-permute-start(bf16[8,7168]{1,0:T(8,128)(2,1)S(1)} %get-tuple-element.25), channel_id=1, source_target_pairs={{0,3},{1,0},{2,1},{3,2},{4,7},{5,4},{6,5},{7,6},{8,11},{9,8},{10,9... | collective-permute-start | bytes 344072 | tf_op jit(solution)/shard_map/ppermute | solution.py:145
  22.4 3.1 %collective-permute-done.2 = bf16[8,7168]{1,0:T(8,128)(2,1)S(1)} collective-permute-done((bf16[8,7168]{1,0:T(8,128)(2,1)S(1)}, bf16[8,7168]{1,0:T(8,128)(2,1)S(1)}, u32[]{:S(2)}, u32[]{:S(2)}) %collective-permute-start.2) | collective-permute-done | bytes 114720 | tf_op jit(solution)/shard_map/ppermute | solution.py:145
  25.4 1.5 %collective-permute-start.3 = (bf16[8,7168]{1,0:T(8,128)(2,1)S(1)}, bf16[8,7168]{1,0:T(8,128)(2,1)S(1)}, u32[]{:S(2)}, u32[]{:S(2)}) collective-permute-start(bf16[8,7168]{1,0:T(8,128)(2,1)S(1)} %get-tuple-element.25), channel_id=1, source_target_pairs={{0,1},{1,2},{2,3},{3,0},{4,5},{5,6},{6,7},{7,4},{8,9},{9,10},{10,1... | collective-permute-start | bytes 344072 | tf_op jit(solution)/shard_map/ppermute | solution.py:145
  26.9 7.1 %collective-permute-done.3 = bf16[8,7168]{1,0:T(8,128)(2,1)S(1)} collective-permute-done((bf16[8,7168]{1,0:T(8,128)(2,1)S(1)}, bf16[8,7168]{1,0:T(8,128)(2,1)S(1)}, u32[]{:S(2)}, u32[]{:S(2)}) %collective-permute-start.3) | collective-permute-done | bytes 114720 | tf_op jit(solution)/shard_map/ppermute | solution.py:145
  34.0 0.0 collective-permute-done.4
  34.0 0.0 collective-permute-done.5
  34.1 0.0 collective-permute-done.6
  34.1 0.0 collective-permute-done.7
  34.1 4.6 %shard_map.65 = bf16[64,7168]{1,0:T(8,128)(2,1)S(1)} custom-call(bf16[64,7168]{1,0:T(8,128)(2,1)S(1)} %constant_dynamic-update-slice_fusion.rows_ref, bf16[1,7168,512]{2,1,0:T(8,128)(2,1)S(1)} %get-tuple-element.11.gate_ref, bf16[1,7168,512]{2,1,0:T(8,128)(2,1)S(1)} %get-tuple-element.12.up_ref, bf16[1,512,7168]{2,1,0:T(8,128)(2,1)} %down_hbm.1), custom_call_target="tpu_custom_call" | custom-call | flops 1409286144 | bytes 7340032 | tf_op jit(solution)/shard_map/pallas_call | solution.py:95
  38.7 0.1 fusion.25
  38.8 1.8 %collective-permute-start.8 = (bf16[8,7168]{1,0:T(8,128)(2,1)S(1)}, bf16[8,7168]{1,0:T(8,128)(2,1)S(1)}, u32[]{:S(2)}, u32[]{:S(2)}) collective-permute-start(bf16[8,7168]{1,0:T(8,128)(2,1)S(1)} %get-tuple-element.15), channel_id=1, source_target_pairs={{0,3},{1,0},{2,1},{3,2},{4,7},{5,4},{6,5},{7,6},{8,11},{9,8},{10,9... | collective-permute-start | bytes 344072 | tf_op jit(solution)/shard_map/ppermute | solution.py:145
  40.6 0.3 collective-permute-start.10
  40.9 0.3 collective-permute-start.9
  41.2 3.7 %collective-permute-start.14 = (bf16[8,7168]{1,0:T(8,128)(2,1)S(1)}, bf16[8,7168]{1,0:T(8,128)(2,1)S(1)}, u32[]{:S(2)}, u32[]{:S(2)}) collective-permute-start(bf16[8,7168]{1,0:T(8,128)(2,1)S(1)} %get-tuple-element.16), channel_id=1, source_target_pairs={{0,9},{1,10},{2,11},{3,8},{4,13},{5,14},{6,15},{7,12},{8,1},{9,2},... | collective-permute-start | bytes 344072 | tf_op jit(solution)/shard_map/ppermute | solution.py:145
  44.9 1.0 %collective-permute-start.13 = (bf16[8,7168]{1,0:T(8,128)(2,1)S(1)}, bf16[8,7168]{1,0:T(8,128)(2,1)S(1)}, u32[]{:S(2)}, u32[]{:S(2)}) collective-permute-start(bf16[8,7168]{1,0:T(8,128)(2,1)S(1)} %get-tuple-element.17), channel_id=1, source_target_pairs={{0,10},{1,11},{2,8},{3,9},{4,14},{5,15},{6,12},{7,13},{8,2},{9,3},... | collective-permute-start | bytes 344072 | tf_op jit(solution)/shard_map/ppermute | solution.py:145
  45.9 0.0 collective-permute-done.8
  45.9 2.6 %collective-permute-start.12 = (bf16[8,7168]{1,0:T(8,128)(2,1)S(1)}, bf16[8,7168]{1,0:T(8,128)(2,1)S(1)}, u32[]{:S(2)}, u32[]{:S(2)}) collective-permute-start(bf16[8,7168]{1,0:T(8,128)(2,1)S(1)} %get-tuple-element.18), channel_id=1, source_target_pairs={{0,11},{1,8},{2,9},{3,10},{4,15},{5,12},{6,13},{7,14},{8,3},{9,0},... | collective-permute-start | bytes 344072 | tf_op jit(solution)/shard_map/ppermute | solution.py:145
  48.5 0.1 collective-permute-done.10
  48.6 1.4 %collective-permute-start.11 = (bf16[8,7168]{1,0:T(8,128)(2,1)S(1)}, bf16[8,7168]{1,0:T(8,128)(2,1)S(1)}, u32[]{:S(2)}, u32[]{:S(2)}) collective-permute-start(bf16[8,7168]{1,0:T(8,128)(2,1)S(1)} %get-tuple-element.19), channel_id=1, source_target_pairs={{0,8},{1,9},{2,10},{3,11},{4,12},{5,13},{6,14},{7,15},{8,0},{9,1},... | collective-permute-start | bytes 344072 | tf_op jit(solution)/shard_map/ppermute | solution.py:145
  50.0 6.4 %collective-permute-done.9 = bf16[8,7168]{1,0:T(8,128)(2,1)S(1)} collective-permute-done((bf16[8,7168]{1,0:T(8,128)(2,1)S(1)}, bf16[8,7168]{1,0:T(8,128)(2,1)S(1)}, u32[]{:S(2)}, u32[]{:S(2)}) %collective-permute-start.9) | collective-permute-done | bytes 114720 | tf_op jit(solution)/shard_map/ppermute | solution.py:145
  56.4 0.1 fusion.7
  56.5 0.0 collective-permute-done.14
  56.5 2.3 %collective-permute-done.13 = bf16[8,7168]{1,0:T(8,128)(2,1)S(1)} collective-permute-done((bf16[8,7168]{1,0:T(8,128)(2,1)S(1)}, bf16[8,7168]{1,0:T(8,128)(2,1)S(1)}, u32[]{:S(2)}, u32[]{:S(2)}) %collective-permute-start.13) | collective-permute-done | bytes 114720 | tf_op jit(solution)/shard_map/ppermute | solution.py:145
  58.8 0.0 collective-permute-done.12
  58.8 0.0 collective-permute-done.11
  58.8 0.1 fusion.8
  58.9 0.1 fusion.9
  59.0 0.1 collective-permute-start.15
  59.1 1.3 %collective-permute-done.15 = bf16[8,7168]{1,0:T(8,128)(2,1)S(1)} collective-permute-done((bf16[8,7168]{1,0:T(8,128)(2,1)S(1)}, bf16[8,7168]{1,0:T(8,128)(2,1)S(1)}, u32[]{:S(2)}, u32[]{:S(2)}) %collective-permute-start.15) | collective-permute-done | bytes 114720 | tf_op jit(solution)/shard_map/ppermute | solution.py:172
  60.4 1.4 %convolution_convert_fusion = bf16[64,7168]{1,0:T(8,128)(2,1)} fusion(bf16[8,7168]{1,0:T(8,128)(2,1)S(1)} %collective-permute-done.15, bf16[8,7168]{1,0:T(8,128)(2,1)S(1)} %reshape.91, bf16[16,64]{1,0:T(8,128)(2,1)S(1)} %fusion.14, bf16[16,64]{1,0:T(8,128)(2,1)S(1)} %get-tuple-element.13), kind=kOutput, calls=%fused_computation | convolution fusion | flops 31662080 | bytes 1150976 | tf_op jit(solution)/shard_map/ct,cd->td/dot_general | solution.py:178
  (19 shorter events, 0.2 us)
Async XLA Ops:
  0.0 2.0 %copy-start = (bf16[64,7168]{1,0:T(8,128)(2,1)S(1)}, bf16[64,7168]{1,0:T(8,128)(2,1)}, u32[]{:S(2)}) copy-start(bf16[64,7168]{1,0:T(8,128)(2,1)} %param.6) | copy-start | bytes 2752516
  2.3 1.5 %collective-permute-start = (bf16[8,7168]{1,0:T(8,128)(2,1)S(1)}, bf16[8,7168]{1,0:T(8,128)(2,1)S(1)}, u32[]{:S(2)}, u32[]{:S(2)}) collective-permute-start(bf16[8,7168]{1,0:T(8,128)(2,1)S(1)} %get-tuple-element.26), channel_id=1, source_target_pairs={{0,4},{4,0},{8,12},{12,8},{1,5},{5,1},{9,13},{13,9},{2,6},{6,2},{1... | collective-permute-start | bytes 344072 | tf_op jit(solution)/shard_map/ppermute | solution.py:151
  3.9 14.8 %collective-permute-start.1 = (bf16[8,7168]{1,0:T(8,128)(2,1)S(1)}, bf16[8,7168]{1,0:T(8,128)(2,1)S(1)}, u32[]{:S(2)}, u32[]{:S(2)}) collective-permute-start(bf16[8,7168]{1,0:T(8,128)(2,1)S(1)} %get-tuple-element.25), channel_id=1, source_target_pairs={{0,2},{1,3},{2,0},{3,1},{4,6},{5,7},{6,4},{7,5},{8,10},{9,11},{10,... | collective-permute-start | bytes 344072 | tf_op jit(solution)/shard_map/ppermute | solution.py:145
  7.9 26.2 %collective-permute-start.7 = (bf16[8,7168]{1,0:T(8,128)(2,1)S(1)}, bf16[8,7168]{1,0:T(8,128)(2,1)S(1)}, u32[]{:S(2)}, u32[]{:S(2)}) collective-permute-start(bf16[8,7168]{1,0:T(8,128)(2,1)S(1)} %get-tuple-element.24), channel_id=1, source_target_pairs={{0,8},{1,9},{2,10},{3,11},{4,12},{5,13},{6,14},{7,15},{8,0},{9,1},... | collective-permute-start | bytes 344072 | tf_op jit(solution)/shard_map/ppermute | solution.py:145
  9.4 24.6 %collective-permute-start.6 = (bf16[8,7168]{1,0:T(8,128)(2,1)S(1)}, bf16[8,7168]{1,0:T(8,128)(2,1)S(1)}, u32[]{:S(2)}, u32[]{:S(2)}) collective-permute-start(bf16[8,7168]{1,0:T(8,128)(2,1)S(1)} %get-tuple-element.24), channel_id=1, source_target_pairs={{0,11},{1,8},{2,9},{3,10},{4,15},{5,12},{6,13},{7,14},{8,3},{9,0},... | collective-permute-start | bytes 344072 | tf_op jit(solution)/shard_map/ppermute | solution.py:145
  10.7 23.3 %collective-permute-start.4 = (bf16[8,7168]{1,0:T(8,128)(2,1)S(1)}, bf16[8,7168]{1,0:T(8,128)(2,1)S(1)}, u32[]{:S(2)}, u32[]{:S(2)}) collective-permute-start(bf16[8,7168]{1,0:T(8,128)(2,1)S(1)} %get-tuple-element.24), channel_id=1, source_target_pairs={{0,9},{1,10},{2,11},{3,8},{4,13},{5,14},{6,15},{7,12},{8,1},{9,2},... | collective-permute-start | bytes 344072 | tf_op jit(solution)/shard_map/ppermute | solution.py:145
  12.3 13.1 %collective-permute-start.2 = (bf16[8,7168]{1,0:T(8,128)(2,1)S(1)}, bf16[8,7168]{1,0:T(8,128)(2,1)S(1)}, u32[]{:S(2)}, u32[]{:S(2)}) collective-permute-start(bf16[8,7168]{1,0:T(8,128)(2,1)S(1)} %get-tuple-element.24), channel_id=1, source_target_pairs={{0,10},{1,11},{2,8},{3,9},{4,14},{5,15},{6,12},{7,13},{8,2},{9,3},... | collective-permute-start | bytes 344072 | tf_op jit(solution)/shard_map/ppermute | solution.py:145
  18.7 15.4 %collective-permute-start.5 = (bf16[8,7168]{1,0:T(8,128)(2,1)S(1)}, bf16[8,7168]{1,0:T(8,128)(2,1)S(1)}, u32[]{:S(2)}, u32[]{:S(2)}) collective-permute-start(bf16[8,7168]{1,0:T(8,128)(2,1)S(1)} %get-tuple-element.25), channel_id=1, source_target_pairs={{0,3},{1,0},{2,1},{3,2},{4,7},{5,4},{6,5},{7,6},{8,11},{9,8},{10,9... | collective-permute-start | bytes 344072 | tf_op jit(solution)/shard_map/ppermute | solution.py:145
  25.4 8.6 %collective-permute-start.3 = (bf16[8,7168]{1,0:T(8,128)(2,1)S(1)}, bf16[8,7168]{1,0:T(8,128)(2,1)S(1)}, u32[]{:S(2)}, u32[]{:S(2)}) collective-permute-start(bf16[8,7168]{1,0:T(8,128)(2,1)S(1)} %get-tuple-element.25), channel_id=1, source_target_pairs={{0,1},{1,2},{2,3},{3,0},{4,5},{5,6},{6,7},{7,4},{8,9},{9,10},{10,1... | collective-permute-start | bytes 344072 | tf_op jit(solution)/shard_map/ppermute | solution.py:145
  38.8 7.1 %collective-permute-start.8 = (bf16[8,7168]{1,0:T(8,128)(2,1)S(1)}, bf16[8,7168]{1,0:T(8,128)(2,1)S(1)}, u32[]{:S(2)}, u32[]{:S(2)}) collective-permute-start(bf16[8,7168]{1,0:T(8,128)(2,1)S(1)} %get-tuple-element.15), channel_id=1, source_target_pairs={{0,3},{1,0},{2,1},{3,2},{4,7},{5,4},{6,5},{7,6},{8,11},{9,8},{10,9... | collective-permute-start | bytes 344072 | tf_op jit(solution)/shard_map/ppermute | solution.py:145
  40.6 8.0 %collective-permute-start.10 = (bf16[8,7168]{1,0:T(8,128)(2,1)S(1)}, bf16[8,7168]{1,0:T(8,128)(2,1)S(1)}, u32[]{:S(2)}, u32[]{:S(2)}) collective-permute-start(bf16[8,7168]{1,0:T(8,128)(2,1)S(1)} %get-tuple-element.20), channel_id=1, source_target_pairs={{0,1},{1,2},{2,3},{3,0},{4,5},{5,6},{6,7},{7,4},{8,9},{9,10},{10,1... | collective-permute-start | bytes 344072 | tf_op jit(solution)/shard_map/ppermute | solution.py:145
  40.9 15.6 %collective-permute-start.9 = (bf16[8,7168]{1,0:T(8,128)(2,1)S(1)}, bf16[8,7168]{1,0:T(8,128)(2,1)S(1)}, u32[]{:S(2)}, u32[]{:S(2)}) collective-permute-start(bf16[8,7168]{1,0:T(8,128)(2,1)S(1)} %get-tuple-element.21), channel_id=1, source_target_pairs={{0,2},{1,3},{2,0},{3,1},{4,6},{5,7},{6,4},{7,5},{8,10},{9,11},{10,... | collective-permute-start | bytes 344072 | tf_op jit(solution)/shard_map/ppermute | solution.py:145
  41.2 15.3 %collective-permute-start.14 = (bf16[8,7168]{1,0:T(8,128)(2,1)S(1)}, bf16[8,7168]{1,0:T(8,128)(2,1)S(1)}, u32[]{:S(2)}, u32[]{:S(2)}) collective-permute-start(bf16[8,7168]{1,0:T(8,128)(2,1)S(1)} %get-tuple-element.16), channel_id=1, source_target_pairs={{0,9},{1,10},{2,11},{3,8},{4,13},{5,14},{6,15},{7,12},{8,1},{9,2},... | collective-permute-start | bytes 344072 | tf_op jit(solution)/shard_map/ppermute | solution.py:145
  44.9 13.9 %collective-permute-start.13 = (bf16[8,7168]{1,0:T(8,128)(2,1)S(1)}, bf16[8,7168]{1,0:T(8,128)(2,1)S(1)}, u32[]{:S(2)}, u32[]{:S(2)}) collective-permute-start(bf16[8,7168]{1,0:T(8,128)(2,1)S(1)} %get-tuple-element.17), channel_id=1, source_target_pairs={{0,10},{1,11},{2,8},{3,9},{4,14},{5,15},{6,12},{7,13},{8,2},{9,3},... | collective-permute-start | bytes 344072 | tf_op jit(solution)/shard_map/ppermute | solution.py:145
  45.9 12.9 %collective-permute-start.12 = (bf16[8,7168]{1,0:T(8,128)(2,1)S(1)}, bf16[8,7168]{1,0:T(8,128)(2,1)S(1)}, u32[]{:S(2)}, u32[]{:S(2)}) collective-permute-start(bf16[8,7168]{1,0:T(8,128)(2,1)S(1)} %get-tuple-element.18), channel_id=1, source_target_pairs={{0,11},{1,8},{2,9},{3,10},{4,15},{5,12},{6,13},{7,14},{8,3},{9,0},... | collective-permute-start | bytes 344072 | tf_op jit(solution)/shard_map/ppermute | solution.py:145
  48.6 10.2 %collective-permute-start.11 = (bf16[8,7168]{1,0:T(8,128)(2,1)S(1)}, bf16[8,7168]{1,0:T(8,128)(2,1)S(1)}, u32[]{:S(2)}, u32[]{:S(2)}) collective-permute-start(bf16[8,7168]{1,0:T(8,128)(2,1)S(1)} %get-tuple-element.19), channel_id=1, source_target_pairs={{0,8},{1,9},{2,10},{3,11},{4,12},{5,13},{6,14},{7,15},{8,0},{9,1},... | collective-permute-start | bytes 344072 | tf_op jit(solution)/shard_map/ppermute | solution.py:145
  59.0 1.4 %collective-permute-start.15 = (bf16[8,7168]{1,0:T(8,128)(2,1)S(1)}, bf16[8,7168]{1,0:T(8,128)(2,1)S(1)}, u32[]{:S(2)}, u32[]{:S(2)}) collective-permute-start(bf16[8,7168]{1,0:T(8,128)(2,1)S(1)} %reshape.92), channel_id=1, source_target_pairs={{0,4},{4,0},{8,12},{12,8},{1,5},{5,1},{9,13},{13,9},{2,6},{6,2},{1... | collective-permute-start | bytes 344072 | tf_op jit(solution)/shard_map/ppermute | solution.py:172

commit v4 on v3

--- a/solution.py
+++ b/solution.py
@@ -58,7 +58,8 @@
     )(*in_hbm)
 
 
-def ffn_kernel(rows_ref, gate_ref, up_ref, down_hbm, out_ref, down_ref, gate_sum, up_sum, sems):
+def ffn_kernel(rows_ref, gate_ref, up_ref, down_hbm, *refs):
+    out_refs, (down_ref, gate_sum, up_sum, sems) = refs[:-4], refs[-4:]
     units = down_hbm.shape[1] // PIECES
     copies = []
     for piece in range(PIECES):
@@ -81,22 +82,22 @@
     hidden = (gate / (1.0 + jnp.exp(-gate)) * up).astype(jnp.bfloat16)
     for copy in copies:
         copy.wait()
-    width = out_ref.shape[1]
+    part, width = out_refs[0].shape
     tile = 1024
     for start in range(0, width, tile):
-        out_ref[:, start:start + tile] = jnp.dot(
-            hidden, down_ref[:, start:start + tile], preferred_element_type=jnp.float32
-        ).astype(out_ref.dtype)
-
-
-def ffn(rows, gate, up, w_down):
+        product = jnp.dot(hidden, down_ref[:, start:start + tile], preferred_element_type=jnp.float32)
+        for i, out_ref in enumerate(out_refs):
+            out_ref[:, start:start + tile] = product[i * part:(i + 1) * part].astype(out_ref.dtype)
+
+
+def ffn(rows, gate, up, w_down, part):
     vmem = pl.BlockSpec(memory_space=pltpu.VMEM)
     units, width = w_down.shape[1:]
     return pl.pallas_call(
         ffn_kernel,
-        out_shape=jax.ShapeDtypeStruct(rows.shape, jnp.bfloat16),
+        out_shape=[jax.ShapeDtypeStruct((part, width), jnp.bfloat16)] * (rows.shape[0] // part),
         in_specs=[vmem] * 3 + [pl.BlockSpec(memory_space=pltpu.HBM)],
-        out_specs=vmem,
+        out_specs=[vmem] * (rows.shape[0] // part),
         scratch_shapes=[
             pltpu.VMEM((units, width), w_down.dtype),
             pltpu.VMEM((rows.shape[0], units), jnp.float32),
@@ -135,39 +136,64 @@
 
     core_pairs = [(i, i ^ 1) for i in range(window)]
 
-    def travel(block, chip_shift, dp_shift):
+    def travel(block, chip_shift, dp_bit):
         pairs = []
         for c in range(chips):
             for k in range(CORES):
                 for z in range(shards):
-                    to_chip, to_shard = (c + chip_shift) % chips, (z + dp_shift) % shards
-                    pairs.append(((c * CORES + k) * shards + z, (to_chip * CORES + k) * shards + to_shard))
+                    to_chip = (c + chip_shift) % chips
+                    pairs.append(((c * CORES + k) * shards + z, (to_chip * CORES + k) * shards + (z ^ dp_bit)))
         return lax.ppermute(block, ("expert", "dp"), pairs)
 
-    ways = [(x, z) for z in sorted(range(shards), key=lambda z: -min(z, shards - z)) for x in range(chips)]
+    bits = [1 << i for i in range((shards - 1).bit_length())]
 
     half = chips * CAP
     kept = outgoing[:half].reshape(chips, CAP, width)
     swapped = lax.ppermute(outgoing[half:], "expert", core_pairs).reshape(chips, CAP, width)
     blocks = jnp.concatenate([kept, swapped], axis=1)
-    arrived = [travel(blocks[x], x, z) if (x, z) != (0, 0) else blocks[0] for x, z in ways]
-    rows = jnp.concatenate(arrived, axis=0)
-
-    w_gate, w_up, _ = lax.optimization_barrier((w_gate, w_up, swapped))
-    partial = ffn(rows, *hold(w_gate, w_up), w_down)
-
-    partial = partial.reshape(len(ways), CORES * CAP, width)
-    returned = {
-        way: travel(partial[i], (chips - way[0]) % chips, (shards - way[1]) % shards) if way != (0, 0) else partial[i]
-        for i, way in enumerate(ways)
-    }
-    home = []
-    for x in range(chips):
-        total = returned[x, 0].astype(jnp.float32)
-        for z in range(1, shards):
-            total = total + returned[x, z].astype(jnp.float32)
-        home.append(total.astype(jnp.bfloat16))
-    home = jnp.stack(home)
+    size = CORES * CAP
+    others = [travel(blocks[x], x, 0) for x in range(1, chips)]
+    own = jnp.concatenate([blocks[0]] + others, axis=0)
+    held = [{0: own[x * size:(x + 1) * size] if x else blocks[0]} for x in range(chips)]
+    for bit in reversed(bits[1:]):
+        for blocks_of in held:
+            blocks_of.update({offset ^ bit: travel(blocks_of[offset], 0, bit) for offset in list(blocks_of)})
+    near = travel(own, 0, 1) if shards > 1 else None
+    passed = [
+        (x, offset ^ 1, travel(held[x][offset], 0, 1)) for x in range(chips) for offset in held[x] if offset and shards > 1
+    ]
+    ways = [(x, 0) for x in range(chips)] + [(x, 1) for x in range(chips) if shards > 1]
+    ways += [(x, offset) for x in range(chips) for offset in held[x] if offset]
+    ways += [(x, offset) for x, offset, _ in passed]
+    pieces = [own] + ([near] if shards > 1 else [])
+    pieces += [held[x][offset] for x in range(chips) for offset in held[x] if offset]
+    rows = jnp.concatenate(pieces + [block for _, _, block in passed], axis=0)
+
+    w_gate, w_up, _ = lax.optimization_barrier((w_gate, w_up, own))
+    partial = ffn(rows, *hold(w_gate, w_up), w_down, size)
+
+    parts = dict(zip(ways, partial))
+    home = {x: [] for x in range(chips)}
+    relayed = []
+    last = [(x, 0, 0) for x in range(chips)]
+    for bit in bits:
+        for x in reversed(range(chips)):
+            for offset in [o for o in reversed(range(shards)) if (x, o) in parts and o & bit]:
+                if offset == bit:
+                    last.append((x, offset, bit))
+                else:
+                    arrived = travel(parts.pop((x, offset)), 0, bit)
+                    onward = (x, offset ^ bit)
+                    parts[onward] = (parts[onward].astype(jnp.float32) + arrived.astype(jnp.float32)).astype(jnp.bfloat16)
+                    relayed.append(arrived)
+    plain = [(x, offset) for x, offset, bit in last if offset <= 1 and relayed and (x or offset)]
+    waited, _ = lax.optimization_barrier(([parts[way] for way in plain], relayed))
+    parts.update(zip(plain, waited))
+    for x, offset, bit in last:
+        shift = (chips - x) % chips
+        block = parts[x, offset]
+        home[x].append(travel(block, shift, bit) if shift or bit else block)
+    home = jnp.stack([sum(block.astype(jnp.float32) for block in home[x]).astype(jnp.bfloat16) for x in range(chips)])
     mine = home[:, :CAP].reshape(half, width)
     other = lax.ppermute(home[:, CAP:].reshape(half, width), "expert", core_pairs)
     expert_out = jnp.concatenate([mine, other], axis=0)

time: 62 us -> 54.5 us (0.88)
  waiting for transfers between devices: 21.2 us -> 14.4 us
  starting transfers between devices: 26.3 us -> 25.6 us
    ppermute x14 -> x13, waiting for transfers between devices: 19 us -> 12.3 us  [travel(): return lax.ppermute(block, ('expert', 'dp'), pairs)]
    ppermute x14 -> x13, starting transfers between devices: 25.7 us -> 25 us  [travel(): return lax.ppermute(block, ('expert', 'dp'), pairs)]
  transfers between devices with their start and end apart: 16 -> 15, of which waited for: 7 -> 9; matrix products, arithmetic and copies ran while one was open for 0% -> 1% of each run, Pallas kernels for 9% -> 10%
where the time goes in v4:
time: 54.5 us; the launch traced here: 54.3 us
  starting transfers between devices  25.6 us (47%)
  waiting for transfers between devices  14.4 us (26%)
  Pallas kernels  9.89 us (18%)
  other arithmetic  2.11 us (4%)
  matrix products  1.71 us (3%)
    ppermute x13, starting transfers between devices, travel(): return lax.ppermute(block, ('expert', 'dp'), pairs)  25 us
    ppermute x13, waiting for transfers between devices, travel(): return lax.ppermute(block, ('expert', 'dp'), pairs)  12.3 us
    pallas_call x1, Pallas kernels, hold(): pl.pallas_call(hold_kernel, out_shape=[pltpu.VMEM(w.shape, w.dtype) for w...  5.31 us
    pallas_call x1, Pallas kernels, ffn(): pl.pallas_call(ffn_kernel, out_shape=[jax.ShapeDtypeStruct((part, width),...  4.57 us
    dot_general x1, matrix products, local(): jnp.einsum('ct,cd->td', jnp.concatenate([high, low], axis=0).astype(jnp.b...  1.34 us
    ppermute x1, waiting for transfers between devices, local(): lax.ppermute(home[:, CAP:].reshape(half, width), 'expert', core_pairs)  1.26 us
  transfers between devices with their start and end apart: 15, of which 9 were waited for; matrix products, arithmetic and copies ran while one was open for 1% of the time, Pallas kernels for 10%

profile of v4, /device:TPU:0, one launch (start us, length us, event | category | flops | bytes accessed | tf_op | source)
XLA Modules:
  0.0 54.3 jit_solution(766639704577046886)
XLA Ops:
  0.0 0.0 copy-start
  0.0 0.9 %compare_reduce_fusion = pred[64,4]{0,1:T(4,128)(4,1)S(1)} fusion(s32[64,8]{0,1:T(8,128)} %param.7, s32[4]{0:T(128)S(1)} %fusion.18), kind=kLoop, calls=%fused_computation.29 | loop fusion | flops 3840 | bytes 2320 | tf_op jit(solution)/shard_map/reduce_or | solution.py:16
  0.9 0.8 %fusion.13 = f32[64,4]{0,1:T(4,128)S(1)} fusion(f32[64,8]{0,1:T(8,128)} %param.8, s32[64,8]{0,1:T(8,128)} %param.7, s32[4]{0:T(128)S(1)} %fusion.18), kind=kLoop, calls=%fused_computation.30 | loop fusion | flops 5888 | bytes 5136 | tf_op jit(solution)/shard_map/reduce_sum | solution.py:17
  1.7 0.1 convolution_convert_fusion.2
  1.8 0.1 eq.46
  1.9 0.1 reduce-precision_convert_fusion
  2.0 0.0 copy-done
  2.0 0.2 convolution_convert_fusion.1
  2.3 0.5 collective-permute-start
  2.8 0.1 reshape.72
  2.8 0.9 %collective-permute-done = bf16[8,7168]{1,0:T(8,128)(2,1)S(1)} collective-permute-done((bf16[8,7168]{1,0:T(8,128)(2,1)S(1)}, bf16[8,7168]{1,0:T(8,128)(2,1)S(1)}, u32[]{:S(2)}, u32[]{:S(2)}) %collective-permute-start) | collective-permute-done | bytes 114720 | tf_op jit(solution)/shard_map/ppermute | solution.py:152
  3.7 0.1 reshape.73
  3.8 0.1 fusion.12
  3.9 2.9 %collective-permute-start.1 = (bf16[8,7168]{1,0:T(8,128)(2,1)S(1)}, bf16[8,7168]{1,0:T(8,128)(2,1)S(1)}, u32[]{:S(2)}, u32[]{:S(2)}) collective-permute-start(bf16[8,7168]{1,0:T(8,128)(2,1)S(1)} %fusion.12), channel_id=1, source_target_pairs={{0,8},{1,9},{2,10},{3,11},{4,12},{5,13},{6,14},{7,15},{8,0},{9,1},... | collective-permute-start | bytes 344072 | tf_op jit(solution)/shard_map/ppermute | solution.py:146
  6.8 0.1 constant_dynamic-update-slice_fusion.6
  6.8 2.7 %collective-permute-start.3 = (bf16[8,7168]{1,0:T(8,128)(2,1)S(1)}, bf16[8,7168]{1,0:T(8,128)(2,1)S(1)}, u32[]{:S(2)}, u32[]{:S(2)}) collective-permute-start(bf16[8,7168]{1,0:T(8,128)(2,1)S(1)} %get-tuple-element.38), channel_id=1, source_target_pairs={{0,2},{1,3},{2,0},{3,1},{4,6},{5,7},{6,4},{7,5},{8,10},{9,11},{10,... | collective-permute-start | bytes 344072 | tf_op jit(solution)/shard_map/ppermute | solution.py:146
  9.5 0.7 %collective-permute-done.1 = bf16[8,7168]{1,0:T(8,128)(2,1)S(1)} collective-permute-done((bf16[8,7168]{1,0:T(8,128)(2,1)S(1)}, bf16[8,7168]{1,0:T(8,128)(2,1)S(1)}, u32[]{:S(2)}, u32[]{:S(2)}) %collective-permute-start.1) | collective-permute-done | bytes 114720 | tf_op jit(solution)/shard_map/ppermute | solution.py:146
  10.3 1.9 %collective-permute-start.2 = (bf16[16,7168]{1,0:T(8,128)(2,1)S(1)}, bf16[16,7168]{1,0:T(8,128)(2,1)S(1)}, u32[]{:S(2)}, u32[]{:S(2)}) collective-permute-start(bf16[16,7168]{1,0:T(8,128)(2,1)S(1)} %pad_maximum_fusion), channel_id=1, source_target_pairs={{0,1},{1,0},{2,3},{3,2},{4,5},{5,4},{6,7},{7,6},{8,9},{9,8},{10,11... | collective-permute-start | bytes 688136 | tf_op jit(solution)/shard_map/ppermute | solution.py:146
  12.1 2.6 %collective-permute-start.4 = (bf16[8,7168]{1,0:T(8,128)(2,1)S(1)}, bf16[8,7168]{1,0:T(8,128)(2,1)S(1)}, u32[]{:S(2)}, u32[]{:S(2)}) collective-permute-start(bf16[8,7168]{1,0:T(8,128)(2,1)S(1)} %collective-permute-done.1), channel_id=1, source_target_pairs={{0,2},{1,3},{2,0},{3,1},{4,6},{5,7},{6,4},{7,5},{8,10},{9,11},{10,... | collective-permute-start | bytes 344072 | tf_op jit(solution)/shard_map/ppermute | solution.py:146
  14.7 5.3 %shard_map.64 = (bf16[1,7168,512]{2,1,0:T(8,128)(2,1)S(1)}, bf16[1,7168,512]{2,1,0:T(8,128)(2,1)S(1)}) custom-call(bf16[1,7168,512]{2,1,0:T(8,128)(2,1)} %gate_from, bf16[1,7168,512]{2,1,0:T(8,128)(2,1)} %up_from), custom_call_target="tpu_custom_call" | custom-call | bytes 14680064 | tf_op jit(solution)/shard_map/pallas_call | solution.py:50
  20.1 0.0 collective-permute-done.3
  20.1 0.5 collective-permute-start.5
  20.6 0.0 collective-permute-done.4
  20.6 2.4 %collective-permute-start.6 = (bf16[8,7168]{1,0:T(8,128)(2,1)S(1)}, bf16[8,7168]{1,0:T(8,128)(2,1)S(1)}, u32[]{:S(2)}, u32[]{:S(2)}) collective-permute-start(bf16[8,7168]{1,0:T(8,128)(2,1)S(1)} %collective-permute-done.4), channel_id=1, source_target_pairs={{0,1},{1,0},{2,3},{3,2},{4,5},{5,4},{6,7},{7,6},{8,9},{9,8},{10,11... | collective-permute-start | bytes 344072 | tf_op jit(solution)/shard_map/ppermute | solution.py:146
  23.0 0.0 collective-permute-done.2
  23.0 2.1 %collective-permute-done.5 = bf16[8,7168]{1,0:T(8,128)(2,1)S(1)} collective-permute-done((bf16[8,7168]{1,0:T(8,128)(2,1)S(1)}, bf16[8,7168]{1,0:T(8,128)(2,1)S(1)}, u32[]{:S(2)}, u32[]{:S(2)}) %collective-permute-start.5) | collective-permute-done | bytes 114720 | tf_op jit(solution)/shard_map/ppermute | solution.py:146
  25.2 1.2 %collective-permute-done.6 = bf16[8,7168]{1,0:T(8,128)(2,1)S(1)} collective-permute-done((bf16[8,7168]{1,0:T(8,128)(2,1)S(1)}, bf16[8,7168]{1,0:T(8,128)(2,1)S(1)}, u32[]{:S(2)}, u32[]{:S(2)}) %collective-permute-start.6) | collective-permute-done | bytes 114720 | tf_op jit(solution)/shard_map/ppermute | solution.py:146
  26.4 4.6 %shard_map.65 = (bf16[8,7168]{1,0:T(8,128)(2,1)S(1)}, bf16[8,7168]{1,0:T(8,128)(2,1)S(1)}, bf16[8,7168]{1,0:T(8,128)(2,1)S(1)}, bf16[8,7168]{1,0:T(8,128)(2,1)S(...) custom-call(bf16[64,7168]{1,0:T(8,128)(2,1)S(1)} %constant_dynamic-u, ...), custom_call_target="tpu_custom_call" | custom-call | flops 1409286144 | bytes 7340032 | tf_op jit(solution)/shard_map/pallas_call | solution.py:96
  31.0 1.4 %collective-permute-start.7 = (bf16[8,7168]{1,0:T(8,128)(2,1)S(1)}, bf16[8,7168]{1,0:T(8,128)(2,1)S(1)}, u32[]{:S(2)}, u32[]{:S(2)}) collective-permute-start(bf16[8,7168]{1,0:T(8,128)(2,1)S(1)} %get-tuple-element.28), channel_id=1, source_target_pairs={{0,1},{1,0},{2,3},{3,2},{4,5},{5,4},{6,7},{7,6},{8,9},{9,8},{10,11... | collective-permute-start | bytes 344072 | tf_op jit(solution)/shard_map/ppermute | solution.py:146
  32.4 0.7 %collective-permute-start.8 = (bf16[8,7168]{1,0:T(8,128)(2,1)S(1)}, bf16[8,7168]{1,0:T(8,128)(2,1)S(1)}, u32[]{:S(2)}, u32[]{:S(2)}) collective-permute-start(bf16[8,7168]{1,0:T(8,128)(2,1)S(1)} %get-tuple-element.29), channel_id=1, source_target_pairs={{0,1},{1,0},{2,3},{3,2},{4,5},{5,4},{6,7},{7,6},{8,9},{9,8},{10,11... | collective-permute-start | bytes 344072 | tf_op jit(solution)/shard_map/ppermute | solution.py:146
  33.1 2.8 %collective-permute-done.7 = bf16[8,7168]{1,0:T(8,128)(2,1)S(1)} collective-permute-done((bf16[8,7168]{1,0:T(8,128)(2,1)S(1)}, bf16[8,7168]{1,0:T(8,128)(2,1)S(1)}, u32[]{:S(2)}, u32[]{:S(2)}) %collective-permute-start.7) | collective-permute-done | bytes 114720 | tf_op jit(solution)/shard_map/ppermute | solution.py:146
  35.9 4.3 %collective-permute-start.13 = (bf16[8,7168]{1,0:T(8,128)(2,1)S(1)}, bf16[8,7168]{1,0:T(8,128)(2,1)S(1)}, u32[]{:S(2)}, u32[]{:S(2)}) collective-permute-start(bf16[8,7168]{1,0:T(8,128)(2,1)S(1)} %add_convert_fusion.1), channel_id=1, source_target_pairs={{0,10},{1,11},{2,8},{3,9},{4,14},{5,15},{6,12},{7,13},{8,2},{9,3},... | collective-permute-start | bytes 344072 | tf_op jit(solution)/shard_map/ppermute | solution.py:146
  40.2 0.0 collective-permute-done.8
  40.2 2.1 %collective-permute-start.9 = (bf16[8,7168]{1,0:T(8,128)(2,1)S(1)}, bf16[8,7168]{1,0:T(8,128)(2,1)S(1)}, u32[]{:S(2)}, u32[]{:S(2)}) collective-permute-start(bf16[8,7168]{1,0:T(8,128)(2,1)S(1)} %get-tuple-element.30), channel_id=1, source_target_pairs={{0,1},{1,0},{2,3},{3,2},{4,5},{5,4},{6,7},{7,6},{8,9},{9,8},{10,11... | collective-permute-start | bytes 344072 | tf_op jit(solution)/shard_map/ppermute | solution.py:146
  42.3 1.1 %collective-permute-start.11 = (bf16[8,7168]{1,0:T(8,128)(2,1)S(1)}, bf16[8,7168]{1,0:T(8,128)(2,1)S(1)}, u32[]{:S(2)}, u32[]{:S(2)}) collective-permute-start(bf16[8,7168]{1,0:T(8,128)(2,1)S(1)} %get-tuple-element.32), channel_id=1, source_target_pairs={{0,8},{1,9},{2,10},{3,11},{4,12},{5,13},{6,14},{7,15},{8,0},{9,1},... | collective-permute-start | bytes 344072 | tf_op jit(solution)/shard_map/ppermute | solution.py:146
  43.4 0.3 collective-permute-start.12
  43.8 2.2 %collective-permute-start.10 = (bf16[8,7168]{1,0:T(8,128)(2,1)S(1)}, bf16[8,7168]{1,0:T(8,128)(2,1)S(1)}, u32[]{:S(2)}, u32[]{:S(2)}) collective-permute-start(bf16[8,7168]{1,0:T(8,128)(2,1)S(1)} %add_convert_fusion.3), channel_id=1, source_target_pairs={{0,2},{1,3},{2,0},{3,1},{4,6},{5,7},{6,4},{7,5},{8,10},{9,11},{10,... | collective-permute-start | bytes 344072 | tf_op jit(solution)/shard_map/ppermute | solution.py:146
  45.9 0.0 collective-permute-done.13
  45.9 1.3 %collective-permute-done.11 = bf16[8,7168]{1,0:T(8,128)(2,1)S(1)} collective-permute-done((bf16[8,7168]{1,0:T(8,128)(2,1)S(1)}, bf16[8,7168]{1,0:T(8,128)(2,1)S(1)}, u32[]{:S(2)}, u32[]{:S(2)}) %collective-permute-start.11) | collective-permute-done | bytes 114720 | tf_op jit(solution)/shard_map/ppermute | solution.py:146
  47.3 2.0 %collective-permute-done.12 = bf16[8,7168]{1,0:T(8,128)(2,1)S(1)} collective-permute-done((bf16[8,7168]{1,0:T(8,128)(2,1)S(1)}, bf16[8,7168]{1,0:T(8,128)(2,1)S(1)}, u32[]{:S(2)}, u32[]{:S(2)}) %collective-permute-start.12) | collective-permute-done | bytes 114720 | tf_op jit(solution)/shard_map/ppermute | solution.py:146
  49.3 0.0 collective-permute-done.9
  49.3 2.0 %collective-permute-done.10 = bf16[8,7168]{1,0:T(8,128)(2,1)S(1)} collective-permute-done((bf16[8,7168]{1,0:T(8,128)(2,1)S(1)}, bf16[8,7168]{1,0:T(8,128)(2,1)S(1)}, u32[]{:S(2)}, u32[]{:S(2)}) %collective-permute-start.10) | collective-permute-done | bytes 114720 | tf_op jit(solution)/shard_map/ppermute | solution.py:146
  51.4 0.1 fusion.9
  51.5 0.1 collective-permute-start.14
  51.7 1.3 %collective-permute-done.14 = bf16[8,7168]{1,0:T(8,128)(2,1)S(1)} collective-permute-done((bf16[8,7168]{1,0:T(8,128)(2,1)S(1)}, bf16[8,7168]{1,0:T(8,128)(2,1)S(1)}, u32[]{:S(2)}, u32[]{:S(2)}) %collective-permute-start.14) | collective-permute-done | bytes 114720 | tf_op jit(solution)/shard_map/ppermute | solution.py:198
  52.9 1.3 %convolution_convert_fusion = bf16[64,7168]{1,0:T(8,128)(2,1)} fusion(bf16[8,7168]{1,0:T(8,128)(2,1)S(1)} %collective-permute-done.14, bf16[8,7168]{1,0:T(8,128)(2,1)S(1)} %reshape.74, bf16[16,64]{1,0:T(8,128)(2,1)S(1)} %fusion.14, bf16[16,64]{1,0:T(8,128)(2,1)S(1)} %get-tuple-element.35), kind=kOutput, calls=%fused_computation | convolution fusion | flops 31662080 | bytes 1150976 | tf_op jit(solution)/shard_map/ct,cd->td/dot_general | solution.py:204
  (20 shorter events, 0.3 us)
Async XLA Ops:
  0.0 2.0 %copy-start = (bf16[64,7168]{1,0:T(8,128)(2,1)S(1)}, bf16[64,7168]{1,0:T(8,128)(2,1)}, u32[]{:S(2)}) copy-start(bf16[64,7168]{1,0:T(8,128)(2,1)} %param.6) | copy-start | bytes 2752516
  2.3 1.5 %collective-permute-start = (bf16[8,7168]{1,0:T(8,128)(2,1)S(1)}, bf16[8,7168]{1,0:T(8,128)(2,1)S(1)}, u32[]{:S(2)}, u32[]{:S(2)}) collective-permute-start(bf16[8,7168]{1,0:T(8,128)(2,1)S(1)} %get-tuple-element.42), channel_id=1, source_target_pairs={{0,4},{4,0},{8,12},{12,8},{1,5},{5,1},{9,13},{13,9},{2,6},{6,2},{1... | collective-permute-start | bytes 344072 | tf_op jit(solution)/shard_map/ppermute | solution.py:152
  3.9 6.4 %collective-permute-start.1 = (bf16[8,7168]{1,0:T(8,128)(2,1)S(1)}, bf16[8,7168]{1,0:T(8,128)(2,1)S(1)}, u32[]{:S(2)}, u32[]{:S(2)}) collective-permute-start(bf16[8,7168]{1,0:T(8,128)(2,1)S(1)} %fusion.12), channel_id=1, source_target_pairs={{0,8},{1,9},{2,10},{3,11},{4,12},{5,13},{6,14},{7,15},{8,0},{9,1},... | collective-permute-start | bytes 344072 | tf_op jit(solution)/shard_map/ppermute | solution.py:146
  6.8 13.2 %collective-permute-start.3 = (bf16[8,7168]{1,0:T(8,128)(2,1)S(1)}, bf16[8,7168]{1,0:T(8,128)(2,1)S(1)}, u32[]{:S(2)}, u32[]{:S(2)}) collective-permute-start(bf16[8,7168]{1,0:T(8,128)(2,1)S(1)} %get-tuple-element.38), channel_id=1, source_target_pairs={{0,2},{1,3},{2,0},{3,1},{4,6},{5,7},{6,4},{7,5},{8,10},{9,11},{10,... | collective-permute-start | bytes 344072 | tf_op jit(solution)/shard_map/ppermute | solution.py:146
  10.3 12.7 %collective-permute-start.2 = (bf16[16,7168]{1,0:T(8,128)(2,1)S(1)}, bf16[16,7168]{1,0:T(8,128)(2,1)S(1)}, u32[]{:S(2)}, u32[]{:S(2)}) collective-permute-start(bf16[16,7168]{1,0:T(8,128)(2,1)S(1)} %pad_maximum_fusion), channel_id=1, source_target_pairs={{0,1},{1,0},{2,3},{3,2},{4,5},{5,4},{6,7},{7,6},{8,9},{9,8},{10,11... | collective-permute-start | bytes 688136 | tf_op jit(solution)/shard_map/ppermute | solution.py:146
  12.1 8.5 %collective-permute-start.4 = (bf16[8,7168]{1,0:T(8,128)(2,1)S(1)}, bf16[8,7168]{1,0:T(8,128)(2,1)S(1)}, u32[]{:S(2)}, u32[]{:S(2)}) collective-permute-start(bf16[8,7168]{1,0:T(8,128)(2,1)S(1)} %collective-permute-done.1), channel_id=1, source_target_pairs={{0,2},{1,3},{2,0},{3,1},{4,6},{5,7},{6,4},{7,5},{8,10},{9,11},{10,... | collective-permute-start | bytes 344072 | tf_op jit(solution)/shard_map/ppermute | solution.py:146
  20.1 5.1 %collective-permute-start.5 = (bf16[8,7168]{1,0:T(8,128)(2,1)S(1)}, bf16[8,7168]{1,0:T(8,128)(2,1)S(1)}, u32[]{:S(2)}, u32[]{:S(2)}) collective-permute-start(bf16[8,7168]{1,0:T(8,128)(2,1)S(1)} %collective-permute-done.3), channel_id=1, source_target_pairs={{0,1},{1,0},{2,3},{3,2},{4,5},{5,4},{6,7},{7,6},{8,9},{9,8},{10,11... | collective-permute-start | bytes 344072 | tf_op jit(solution)/shard_map/ppermute | solution.py:146
  20.6 5.8 %collective-permute-start.6 = (bf16[8,7168]{1,0:T(8,128)(2,1)S(1)}, bf16[8,7168]{1,0:T(8,128)(2,1)S(1)}, u32[]{:S(2)}, u32[]{:S(2)}) collective-permute-start(bf16[8,7168]{1,0:T(8,128)(2,1)S(1)} %collective-permute-done.4), channel_id=1, source_target_pairs={{0,1},{1,0},{2,3},{3,2},{4,5},{5,4},{6,7},{7,6},{8,9},{9,8},{10,11... | collective-permute-start | bytes 344072 | tf_op jit(solution)/shard_map/ppermute | solution.py:146
  31.0 4.9 %collective-permute-start.7 = (bf16[8,7168]{1,0:T(8,128)(2,1)S(1)}, bf16[8,7168]{1,0:T(8,128)(2,1)S(1)}, u32[]{:S(2)}, u32[]{:S(2)}) collective-permute-start(bf16[8,7168]{1,0:T(8,128)(2,1)S(1)} %get-tuple-element.28), channel_id=1, source_target_pairs={{0,1},{1,0},{2,3},{3,2},{4,5},{5,4},{6,7},{7,6},{8,9},{9,8},{10,11... | collective-permute-start | bytes 344072 | tf_op jit(solution)/shard_map/ppermute | solution.py:146
  32.4 7.8 %collective-permute-start.8 = (bf16[8,7168]{1,0:T(8,128)(2,1)S(1)}, bf16[8,7168]{1,0:T(8,128)(2,1)S(1)}, u32[]{:S(2)}, u32[]{:S(2)}) collective-permute-start(bf16[8,7168]{1,0:T(8,128)(2,1)S(1)} %get-tuple-element.29), channel_id=1, source_target_pairs={{0,1},{1,0},{2,3},{3,2},{4,5},{5,4},{6,7},{7,6},{8,9},{9,8},{10,11... | collective-permute-start | bytes 344072 | tf_op jit(solution)/shard_map/ppermute | solution.py:146
  35.9 10.0 %collective-permute-start.13 = (bf16[8,7168]{1,0:T(8,128)(2,1)S(1)}, bf16[8,7168]{1,0:T(8,128)(2,1)S(1)}, u32[]{:S(2)}, u32[]{:S(2)}) collective-permute-start(bf16[8,7168]{1,0:T(8,128)(2,1)S(1)} %add_convert_fusion.1), channel_id=1, source_target_pairs={{0,10},{1,11},{2,8},{3,9},{4,14},{5,15},{6,12},{7,13},{8,2},{9,3},... | collective-permute-start | bytes 344072 | tf_op jit(solution)/shard_map/ppermute | solution.py:146
  40.2 9.1 %collective-permute-start.9 = (bf16[8,7168]{1,0:T(8,128)(2,1)S(1)}, bf16[8,7168]{1,0:T(8,128)(2,1)S(1)}, u32[]{:S(2)}, u32[]{:S(2)}) collective-permute-start(bf16[8,7168]{1,0:T(8,128)(2,1)S(1)} %get-tuple-element.30), channel_id=1, source_target_pairs={{0,1},{1,0},{2,3},{3,2},{4,5},{5,4},{6,7},{7,6},{8,9},{9,8},{10,11... | collective-permute-start | bytes 344072 | tf_op jit(solution)/shard_map/ppermute | solution.py:146
  42.3 5.0 %collective-permute-start.11 = (bf16[8,7168]{1,0:T(8,128)(2,1)S(1)}, bf16[8,7168]{1,0:T(8,128)(2,1)S(1)}, u32[]{:S(2)}, u32[]{:S(2)}) collective-permute-start(bf16[8,7168]{1,0:T(8,128)(2,1)S(1)} %get-tuple-element.32), channel_id=1, source_target_pairs={{0,8},{1,9},{2,10},{3,11},{4,12},{5,13},{6,14},{7,15},{8,0},{9,1},... | collective-permute-start | bytes 344072 | tf_op jit(solution)/shard_map/ppermute | solution.py:146
  43.4 5.9 %collective-permute-start.12 = (bf16[8,7168]{1,0:T(8,128)(2,1)S(1)}, bf16[8,7168]{1,0:T(8,128)(2,1)S(1)}, u32[]{:S(2)}, u32[]{:S(2)}) collective-permute-start(bf16[8,7168]{1,0:T(8,128)(2,1)S(1)} %get-tuple-element.33), channel_id=1, source_target_pairs={{0,9},{1,8},{2,11},{3,10},{4,13},{5,12},{6,15},{7,14},{8,1},{9,0},... | collective-permute-start | bytes 344072 | tf_op jit(solution)/shard_map/ppermute | solution.py:146
  43.8 7.6 %collective-permute-start.10 = (bf16[8,7168]{1,0:T(8,128)(2,1)S(1)}, bf16[8,7168]{1,0:T(8,128)(2,1)S(1)}, u32[]{:S(2)}, u32[]{:S(2)}) collective-permute-start(bf16[8,7168]{1,0:T(8,128)(2,1)S(1)} %add_convert_fusion.3), channel_id=1, source_target_pairs={{0,2},{1,3},{2,0},{3,1},{4,6},{5,7},{6,4},{7,5},{8,10},{9,11},{10,... | collective-permute-start | bytes 344072 | tf_op jit(solution)/shard_map/ppermute | solution.py:146
  51.5 1.4 %collective-permute-start.14 = (bf16[8,7168]{1,0:T(8,128)(2,1)S(1)}, bf16[8,7168]{1,0:T(8,128)(2,1)S(1)}, u32[]{:S(2)}, u32[]{:S(2)}) collective-permute-start(bf16[8,7168]{1,0:T(8,128)(2,1)S(1)} %reshape.75), channel_id=1, source_target_pairs={{0,4},{4,0},{8,12},{12,8},{1,5},{5,1},{9,13},{13,9},{2,6},{6,2},{1... | collective-permute-start | bytes 344072 | tf_op jit(solution)/shard_map/ppermute | solution.py:198

commit v5 on v4

--- a/solution.py
+++ b/solution.py
@@ -11,51 +11,100 @@
 CORES = 2
 
 
-def routing(expert_ids, gate_weights, experts):
-    matches = expert_ids[:, :, None] == experts[None, None, :]
-    chosen = jnp.any(matches, axis=1)
-    weight = jnp.sum(jnp.where(matches, gate_weights[:, :, None], jnp.float32(0.0)), axis=1)
-    count = chosen.astype(jnp.int32)
-    tokens = count.shape[0]
-    before = lax.broadcasted_iota(jnp.int32, (tokens, tokens), 0) > lax.broadcasted_iota(jnp.int32, (tokens, tokens), 1)
+def route_kernel(chips, *refs):
+    sources, (kept_ref, sent_ref, mix_ref), (ids_ref, weights_ref, tokens_ref, sems) = refs[:3], refs[3:6], refs[6:]
+    copies = [
+        pltpu.make_async_copy(source, target, sems.at[i])
+        for i, (source, target) in enumerate(zip(sources, (ids_ref, weights_ref, tokens_ref)))
+    ]
+    for copy in copies:
+        copy.start()
+    me = lax.axis_index("expert")
+    chip, core = me // CORES, me % CORES
+    slots = CORES * chips * CAP
+    topk, tokens = ids_ref.shape
+    row = lax.broadcasted_iota(jnp.int32, (slots, tokens), 0)
+    expert = jnp.zeros_like(row)
+    for i in range(CORES * chips):
+        core_offset, chip_offset = i // chips, i % chips
+        named = lax.rem(chip + chip_offset, chips) * CORES + lax.rem(core + core_offset, CORES)
+        expert = jnp.where((row >= i * CAP) & (row < (i + 1) * CAP), named, expert)
+    copies[0].wait()
+    copies[1].wait()
+    chosen = jnp.zeros((slots, tokens), jnp.float32)
+    weight = jnp.zeros((slots, tokens), jnp.float32)
+    for k in range(topk):
+        hit = ids_ref[k:k + 1, :] == expert
+        chosen = jnp.where(hit, 1.0, chosen)
+        weight = weight + jnp.where(hit, weights_ref[k:k + 1, :], 0.0)
+    before = lax.broadcasted_iota(jnp.int32, (tokens, tokens), 0) < lax.broadcasted_iota(jnp.int32, (tokens, tokens), 1)
     position = jnp.dot(
-        before.astype(jnp.bfloat16), count.astype(jnp.bfloat16), preferred_element_type=jnp.float32
-    ).astype(jnp.int32)
-    slot = jnp.arange(CAP, dtype=jnp.int32)
-    select = (position.T[:, None, :] == slot[None, :, None]) & chosen.T[:, None, :]
-    return select, weight
+        chosen.astype(jnp.bfloat16), jnp.where(before, 1.0, 0.0).astype(jnp.bfloat16), preferred_element_type=jnp.float32
+    )
+    slot = (row & (CAP - 1)).astype(jnp.float32)
+    select = jnp.where(position == slot, chosen, 0.0)
+    combine = select * weight
+    high = combine.astype(jnp.bfloat16)
+    mix_ref[:slots] = high
+    mix_ref[slots:] = (combine - high.astype(jnp.float32)).astype(jnp.bfloat16)
+    select = select.astype(jnp.bfloat16)
+    copies[2].wait()
+    half, width = kept_ref.shape
+    tile = 1024
+    for start in range(0, width, tile):
+        picked = jnp.dot(select, tokens_ref[:, start:start + tile], preferred_element_type=jnp.float32)
+        kept_ref[:, start:start + tile] = picked[:half].astype(jnp.bfloat16)
+        sent_ref[:, start:start + tile] = picked[half:].astype(jnp.bfloat16)
+
+
+def route(tokens, expert_ids, gate_weights, chips):
+    vmem = pl.BlockSpec(memory_space=pltpu.VMEM)
+    count, width = tokens.shape
+    half = chips * CAP
+    arrays = (expert_ids.T, gate_weights.T, tokens)
+    return pl.pallas_call(
+        functools.partial(route_kernel, chips),
+        out_shape=[
+            jax.ShapeDtypeStruct((half, width), jnp.bfloat16),
+            jax.ShapeDtypeStruct((half, width), jnp.bfloat16),
+            jax.ShapeDtypeStruct((2 * CORES * half, count), jnp.bfloat16),
+        ],
+        in_specs=[pl.BlockSpec(memory_space=pltpu.HBM)] * 3,
+        out_specs=[vmem] * 3,
+        scratch_shapes=[pltpu.VMEM(array.shape, array.dtype) for array in arrays] + [pltpu.SemaphoreType.DMA((3,))],
+        compiler_params=pltpu.CompilerParams(vmem_limit_bytes=8 * 1024 * 1024),
+        cost_estimate=pl.CostEstimate(
+            flops=4 * half * CORES * count * width, bytes_accessed=4 * count * width, transcendentals=0
+        ),
+    )(*[pltpu.with_memory_space_constraint(array, pltpu.HBM) for array in arrays])
 
 
 PIECES = 4
 STEPS = 4
 
 
-def hold_kernel(gate_from, up_from, gate_to, up_to, sems):
+def hold_kernel(source, target, sems):
+    rows = source.shape[1] // PIECES
     copies = []
-    for which, (source, target) in enumerate(((gate_from, gate_to), (up_from, up_to))):
-        rows = source.shape[1] // PIECES
-        for piece in range(PIECES):
-            at = pl.ds(piece * rows, rows)
-            copies.append(
-                pltpu.make_async_copy(source.at[:, at], target.at[:, at], sems.at[which, piece])
-            )
+    for piece in range(PIECES):
+        at = pl.ds(piece * rows, rows)
+        copies.append(pltpu.make_async_copy(source.at[:, at], target.at[:, at], sems.at[piece]))
     for copy in copies:
         copy.start()
     for copy in copies:
         copy.wait()
 
 
-def hold(w_gate, w_up):
-    in_hbm = [pltpu.with_memory_space_constraint(w, pltpu.HBM) for w in (w_gate, w_up)]
+def hold(weight):
     return pl.pallas_call(
         hold_kernel,
-        out_shape=[pltpu.VMEM(w.shape, w.dtype) for w in (w_gate, w_up)],
-        in_specs=[pl.BlockSpec(memory_space=pltpu.HBM)] * 2,
-        out_specs=[pl.BlockSpec(memory_space=pltpu.VMEM)] * 2,
-        scratch_shapes=[pltpu.SemaphoreType.DMA((2, PIECES))],
+        out_shape=pltpu.VMEM(weight.shape, weight.dtype),
+        in_specs=[pl.BlockSpec(memory_space=pltpu.HBM)],
+        out_specs=pl.BlockSpec(memory_space=pltpu.VMEM),
+        scratch_shapes=[pltpu.SemaphoreType.DMA((PIECES,))],
         compiler_params=pltpu.CompilerParams(vmem_limit_bytes=1024 * 1024),
-        cost_estimate=pl.CostEstimate(flops=0, bytes_accessed=4 * w_gate.size, transcendentals=0),
-    )(*in_hbm)
+        cost_estimate=pl.CostEstimate(flops=0, bytes_accessed=4 * weight.size, transcendentals=0),
+    )(pltpu.with_memory_space_constraint(weight, pltpu.HBM))
 
 
 def ffn_kernel(rows_ref, gate_ref, up_ref, down_hbm, *refs):
@@ -123,16 +172,7 @@
     shards = lax.axis_size("dp")
     chips = window // CORES
     width = tokens.shape[1]
-    me = lax.axis_index("expert")
-    chip, core = me // CORES, me % CORES
-    offset = jnp.arange(window, dtype=jnp.int32)
-    core_offset, chip_offset = offset // chips, offset % chips
-    experts = ((chip + chip_offset) % chips) * CORES + (core + core_offset) % CORES
-    select, route_weight = routing(expert_ids, gate_weights, experts)
-    flat_select = select.reshape(window * CAP, -1)
-    outgoing = jnp.dot(
-        flat_select.astype(jnp.bfloat16), tokens, preferred_element_type=jnp.float32
-    ).astype(jnp.bfloat16)
+    kept, sent, mix = route(tokens, expert_ids, gate_weights, chips)
 
     core_pairs = [(i, i ^ 1) for i in range(window)]
 
@@ -148,9 +188,8 @@
     bits = [1 << i for i in range((shards - 1).bit_length())]
 
     half = chips * CAP
-    kept = outgoing[:half].reshape(chips, CAP, width)
-    swapped = lax.ppermute(outgoing[half:], "expert", core_pairs).reshape(chips, CAP, width)
-    blocks = jnp.concatenate([kept, swapped], axis=1)
+    swapped = lax.ppermute(sent, "expert", core_pairs).reshape(chips, CAP, width)
+    blocks = jnp.concatenate([kept.reshape(chips, CAP, width), swapped], axis=1)
     size = CORES * CAP
     others = [travel(blocks[x], x, 0) for x in range(1, chips)]
     own = jnp.concatenate([blocks[0]] + others, axis=0)
@@ -169,8 +208,8 @@
     pieces += [held[x][offset] for x in range(chips) for offset in held[x] if offset]
     rows = jnp.concatenate(pieces + [block for _, _, block in passed], axis=0)
 
-    w_gate, w_up, _ = lax.optimization_barrier((w_gate, w_up, own))
-    partial = ffn(rows, *hold(w_gate, w_up), w_down, size)
+    w_up, _ = lax.optimization_barrier((w_up, own))
+    partial = ffn(rows, w_gate, hold(w_up), w_down, size)
 
     parts = dict(zip(ways, partial))
     home = {x: [] for x in range(chips)}
@@ -198,14 +237,8 @@
     other = lax.ppermute(home[:, CAP:].reshape(half, width), "expert", core_pairs)
     expert_out = jnp.concatenate([mine, other], axis=0)
 
-    combine = (select.astype(jnp.float32) * route_weight.T[:, None, :]).reshape(window * CAP, -1)
-    high = lax.reduce_precision(combine, 8, 7)
-    low = combine - high
     mixed = jnp.einsum(
-        "ct,cd->td",
-        jnp.concatenate([high, low], axis=0).astype(jnp.bfloat16),
-        jnp.concatenate([expert_out, expert_out], axis=0),
-        preferred_element_type=jnp.float32,
+        "ct,cd->td", mix, jnp.concatenate([expert_out, expert_out], axis=0), preferred_element_type=jnp.float32
     )
     return mixed.astype(jnp.bfloat16)
 

time: 54.5 us -> 53.7 us (0.985)
  other arithmetic: 2.11 us -> 0.37 us
  waiting for transfers between devices: 14.4 us -> 15.7 us
  starting transfers between devices: 25.6 us -> 26.4 us
    ppermute x13, waiting for transfers between devices: 12.3 us -> 13.5 us  [travel(): return lax.ppermute(block, ('expert', 'dp'), pairs)]
    reduce_or x1 -> x0, other arithmetic: 0.85 us -> none  [routing(): chosen = jnp.any(matches, axis=1)]
    reduce_sum x1 -> x0, other arithmetic: 0.79 us -> none  [routing(): jnp.sum(jnp.where(matches, gate_weights[:, :, None], jnp.float32(0.0)), a...]
    ppermute x13, starting transfers between devices: 25 us -> 25.8 us  [travel(): return lax.ppermute(block, ('expert', 'dp'), pairs)]
    pallas_call x1 -> x2, Pallas kernels: 5.31 us -> 4.81 us  [the longest x1 3.33 us: hold(): pl.pallas_call(hold_kernel, out_shape=pltpu.VMEM(weight.shape, weight.dty...]
    dot_general x3 -> x1, matrix products: 1.71 us -> 1.34 us  [local(): jnp.einsum('ct,cd->td', mix, jnp.concatenate([expert_out, expert_out], ax...]
  transfers between devices with their start and end apart: 15 -> 15, of which waited for: 9 -> 10; matrix products, arithmetic and copies ran while one was open for 1% -> 1% of each run, Pallas kernels for 10% -> 6%
where the time goes in v5:
time: 53.7 us; the launch traced here: 53.5 us
  starting transfers between devices  26.4 us (49%)
  waiting for transfers between devices  15.7 us (29%)
  Pallas kernels  9.38 us (17%)
  matrix products  1.34 us (2%)
    ppermute x13, starting transfers between devices, travel(): return lax.ppermute(block, ('expert', 'dp'), pairs)  25.8 us
    ppermute x13, waiting for transfers between devices, travel(): return lax.ppermute(block, ('expert', 'dp'), pairs)  13.5 us
    pallas_call x1, Pallas kernels, ffn(): pl.pallas_call(ffn_kernel, out_shape=[jax.ShapeDtypeStruct((part, width),...  4.57 us
    pallas_call x1, Pallas kernels, hold(): pl.pallas_call(hold_kernel, out_shape=pltpu.VMEM(weight.shape, weight.dty...  3.33 us
    pallas_call x1, Pallas kernels, route(): pl.pallas_call(functools.partial(route_kernel, chips), out_shape=[jax.Sha...  1.48 us
    dot_general x1, matrix products, local(): jnp.einsum('ct,cd->td', mix, jnp.concatenate([expert_out, expert_out], ax...  1.34 us
    ppermute x1, waiting for transfers between devices, local(): lax.ppermute(home[:, CAP:].reshape(half, width), 'expert', core_pairs)  1.27 us
  transfers between devices with their start and end apart: 15, of which 10 were waited for; matrix products, arithmetic and copies ran while one was open for 1% of the time, Pallas kernels for 6%

profile of v5, /device:TPU:0, one launch (start us, length us, event | category | flops | bytes accessed | tf_op | source)
XLA Modules:
  0.0 53.5 jit_solution(32233584486718516)
XLA Ops:
  0.0 1.5 %shard_map.64 = (bf16[8,7168]{1,0:T(8,128)(2,1)S(1)}, bf16[8,7168]{1,0:T(8,128)(2,1)S(1)}, bf16[32,64]{1,0:T(8,128)(2,1)S(1)}) custom-call(s32[8,64]{1,0:T(8,128)} %bitcast.14, f32[8,64]{1,0:T(8,128)} %bitcast.15, bf16[64,7168]{1,0:T(8,128)(2,1)} %refs_2_.1), custom_call_target="tpu_custom_call" | custom-call | flops 29360128 | bytes 1835008 | tf_op jit(solution)/shard_map/pallas_call | solution.py:65
  1.5 0.5 collective-permute-start
  2.0 0.1 reshape.12
  2.1 0.9 %collective-permute-done = bf16[8,7168]{1,0:T(8,128)(2,1)S(1)} collective-permute-done((bf16[8,7168]{1,0:T(8,128)(2,1)S(1)}, bf16[8,7168]{1,0:T(8,128)(2,1)S(1)}, u32[]{:S(2)}, u32[]{:S(2)}) %collective-permute-start) | collective-permute-done | bytes 114720 | tf_op jit(solution)/shard_map/ppermute | solution.py:191
  3.0 0.1 reshape.13
  3.0 0.1 fusion.12
  3.1 2.9 %collective-permute-start.1 = (bf16[8,7168]{1,0:T(8,128)(2,1)S(1)}, bf16[8,7168]{1,0:T(8,128)(2,1)S(1)}, u32[]{:S(2)}, u32[]{:S(2)}) collective-permute-start(bf16[8,7168]{1,0:T(8,128)(2,1)S(1)} %fusion.12), channel_id=1, source_target_pairs={{0,8},{1,9},{2,10},{3,11},{4,12},{5,13},{6,14},{7,15},{8,0},{9,1},... | collective-permute-start | bytes 344072 | tf_op jit(solution)/shard_map/ppermute | solution.py:186
  6.0 0.1 constant_dynamic-update-slice_fusion.6
  6.1 2.7 %collective-permute-start.3 = (bf16[8,7168]{1,0:T(8,128)(2,1)S(1)}, bf16[8,7168]{1,0:T(8,128)(2,1)S(1)}, u32[]{:S(2)}, u32[]{:S(2)}) collective-permute-start(bf16[8,7168]{1,0:T(8,128)(2,1)S(1)} %get-tuple-element.36), channel_id=1, source_target_pairs={{0,2},{1,3},{2,0},{3,1},{4,6},{5,7},{6,4},{7,5},{8,10},{9,11},{10,... | collective-permute-start | bytes 344072 | tf_op jit(solution)/shard_map/ppermute | solution.py:186
  8.7 0.7 %collective-permute-done.1 = bf16[8,7168]{1,0:T(8,128)(2,1)S(1)} collective-permute-done((bf16[8,7168]{1,0:T(8,128)(2,1)S(1)}, bf16[8,7168]{1,0:T(8,128)(2,1)S(1)}, u32[]{:S(2)}, u32[]{:S(2)}) %collective-permute-start.1) | collective-permute-done | bytes 114720 | tf_op jit(solution)/shard_map/ppermute | solution.py:186
  9.5 1.9 %collective-permute-start.2 = (bf16[16,7168]{1,0:T(8,128)(2,1)S(1)}, bf16[16,7168]{1,0:T(8,128)(2,1)S(1)}, u32[]{:S(2)}, u32[]{:S(2)}) collective-permute-start(bf16[16,7168]{1,0:T(8,128)(2,1)S(1)} %pad_maximum_fusion), channel_id=1, source_target_pairs={{0,1},{1,0},{2,3},{3,2},{4,5},{5,4},{6,7},{7,6},{8,9},{9,8},{10,11... | collective-permute-start | bytes 688136 | tf_op jit(solution)/shard_map/ppermute | solution.py:186
  11.4 2.6 %collective-permute-start.4 = (bf16[8,7168]{1,0:T(8,128)(2,1)S(1)}, bf16[8,7168]{1,0:T(8,128)(2,1)S(1)}, u32[]{:S(2)}, u32[]{:S(2)}) collective-permute-start(bf16[8,7168]{1,0:T(8,128)(2,1)S(1)} %collective-permute-done.1), channel_id=1, source_target_pairs={{0,2},{1,3},{2,0},{3,1},{4,6},{5,7},{6,4},{7,5},{8,10},{9,11},{10,... | collective-permute-start | bytes 344072 | tf_op jit(solution)/shard_map/ppermute | solution.py:186
  14.0 0.0 slice-start
  14.0 0.0 slice-start.1
  14.0 3.3 %shard_map.65.up_ref = bf16[1,7168,512]{2,1,0:T(8,128)(2,1)S(1)} custom-call(bf16[1,7168,512]{2,1,0:T(8,128)(2,1)} %source), custom_call_target="tpu_custom_call" | custom-call | bytes 14680064 | tf_op jit(solution)/shard_map/pallas_call | solution.py:99
  17.3 0.0 collective-permute-done.3
  17.3 0.5 collective-permute-start.5
  17.9 1.9 %collective-permute-done.4 = bf16[8,7168]{1,0:T(8,128)(2,1)S(1)} collective-permute-done((bf16[8,7168]{1,0:T(8,128)(2,1)S(1)}, bf16[8,7168]{1,0:T(8,128)(2,1)S(1)}, u32[]{:S(2)}, u32[]{:S(2)}) %collective-permute-start.4) | collective-permute-done | bytes 114720 | tf_op jit(solution)/shard_map/ppermute | solution.py:186
  19.8 3.1 %collective-permute-start.6 = (bf16[8,7168]{1,0:T(8,128)(2,1)S(1)}, bf16[8,7168]{1,0:T(8,128)(2,1)S(1)}, u32[]{:S(2)}, u32[]{:S(2)}) collective-permute-start(bf16[8,7168]{1,0:T(8,128)(2,1)S(1)} %collective-permute-done.4), channel_id=1, source_target_pairs={{0,1},{1,0},{2,3},{3,2},{4,5},{5,4},{6,7},{7,6},{8,9},{9,8},{10,11... | collective-permute-start | bytes 344072 | tf_op jit(solution)/shard_map/ppermute | solution.py:186
  22.9 0.0 collective-permute-done.2
  23.0 1.2 %collective-permute-done.5 = bf16[8,7168]{1,0:T(8,128)(2,1)S(1)} collective-permute-done((bf16[8,7168]{1,0:T(8,128)(2,1)S(1)}, bf16[8,7168]{1,0:T(8,128)(2,1)S(1)}, u32[]{:S(2)}, u32[]{:S(2)}) %collective-permute-start.5) | collective-permute-done | bytes 114720 | tf_op jit(solution)/shard_map/ppermute | solution.py:186
  24.2 1.5 %collective-permute-done.6 = bf16[8,7168]{1,0:T(8,128)(2,1)S(1)} collective-permute-done((bf16[8,7168]{1,0:T(8,128)(2,1)S(1)}, bf16[8,7168]{1,0:T(8,128)(2,1)S(1)}, u32[]{:S(2)}, u32[]{:S(2)}) %collective-permute-start.6) | collective-permute-done | bytes 114720 | tf_op jit(solution)/shard_map/ppermute | solution.py:186
  25.7 0.0 slice-done
  25.7 0.0 slice-done.1
  25.7 4.6 %shard_map.66 = (bf16[8,7168]{1,0:T(8,128)(2,1)S(1)}, bf16[8,7168]{1,0:T(8,128)(2,1)S(1)}, bf16[8,7168]{1,0:T(8,128)(2,1)S(1)}, bf16[8,7168]{1,0:T(8,128)(2,1)S(...) custom-call(bf16[64,7168]{1,0:T(8,128)(2,1)S(1)} %constant_dynamic-u, ...), custom_call_target="tpu_custom_call" | custom-call | flops 1409286144 | bytes 7340032 | tf_op jit(solution)/shard_map/pallas_call | solution.py:145
  30.3 2.1 %collective-permute-start.7 = (bf16[8,7168]{1,0:T(8,128)(2,1)S(1)}, bf16[8,7168]{1,0:T(8,128)(2,1)S(1)}, u32[]{:S(2)}, u32[]{:S(2)}) collective-permute-start(bf16[8,7168]{1,0:T(8,128)(2,1)S(1)} %get-tuple-element.28), channel_id=1, source_target_pairs={{0,1},{1,0},{2,3},{3,2},{4,5},{5,4},{6,7},{7,6},{8,9},{9,8},{10,11... | collective-permute-start | bytes 344072 | tf_op jit(solution)/shard_map/ppermute | solution.py:186
  32.4 0.1 collective-permute-start.8
  32.5 2.7 %collective-permute-done.7 = bf16[8,7168]{1,0:T(8,128)(2,1)S(1)} collective-permute-done((bf16[8,7168]{1,0:T(8,128)(2,1)S(1)}, bf16[8,7168]{1,0:T(8,128)(2,1)S(1)}, u32[]{:S(2)}, u32[]{:S(2)}) %collective-permute-start.7) | collective-permute-done | bytes 114720 | tf_op jit(solution)/shard_map/ppermute | solution.py:186
  35.2 4.3 %collective-permute-start.13 = (bf16[8,7168]{1,0:T(8,128)(2,1)S(1)}, bf16[8,7168]{1,0:T(8,128)(2,1)S(1)}, u32[]{:S(2)}, u32[]{:S(2)}) collective-permute-start(bf16[8,7168]{1,0:T(8,128)(2,1)S(1)} %add_convert_fusion.1), channel_id=1, source_target_pairs={{0,10},{1,11},{2,8},{3,9},{4,14},{5,15},{6,12},{7,13},{8,2},{9,3},... | collective-permute-start | bytes 344072 | tf_op jit(solution)/shard_map/ppermute | solution.py:186
  39.5 0.0 collective-permute-done.8
  39.5 2.1 %collective-permute-start.9 = (bf16[8,7168]{1,0:T(8,128)(2,1)S(1)}, bf16[8,7168]{1,0:T(8,128)(2,1)S(1)}, u32[]{:S(2)}, u32[]{:S(2)}) collective-permute-start(bf16[8,7168]{1,0:T(8,128)(2,1)S(1)} %get-tuple-element.30), channel_id=1, source_target_pairs={{0,1},{1,0},{2,3},{3,2},{4,5},{5,4},{6,7},{7,6},{8,9},{9,8},{10,11... | collective-permute-start | bytes 344072 | tf_op jit(solution)/shard_map/ppermute | solution.py:186
  41.5 1.1 %collective-permute-start.11 = (bf16[8,7168]{1,0:T(8,128)(2,1)S(1)}, bf16[8,7168]{1,0:T(8,128)(2,1)S(1)}, u32[]{:S(2)}, u32[]{:S(2)}) collective-permute-start(bf16[8,7168]{1,0:T(8,128)(2,1)S(1)} %get-tuple-element.32), channel_id=1, source_target_pairs={{0,8},{1,9},{2,10},{3,11},{4,12},{5,13},{6,14},{7,15},{8,0},{9,1},... | collective-permute-start | bytes 344072 | tf_op jit(solution)/shard_map/ppermute | solution.py:186
  42.7 0.3 collective-permute-start.12
  43.0 2.1 %collective-permute-start.10 = (bf16[8,7168]{1,0:T(8,128)(2,1)S(1)}, bf16[8,7168]{1,0:T(8,128)(2,1)S(1)}, u32[]{:S(2)}, u32[]{:S(2)}) collective-permute-start(bf16[8,7168]{1,0:T(8,128)(2,1)S(1)} %add_convert_fusion.3), channel_id=1, source_target_pairs={{0,2},{1,3},{2,0},{3,1},{4,6},{5,7},{6,4},{7,5},{8,10},{9,11},{10,... | collective-permute-start | bytes 344072 | tf_op jit(solution)/shard_map/ppermute | solution.py:186
  45.2 0.0 collective-permute-done.13
  45.2 1.3 %collective-permute-done.11 = bf16[8,7168]{1,0:T(8,128)(2,1)S(1)} collective-permute-done((bf16[8,7168]{1,0:T(8,128)(2,1)S(1)}, bf16[8,7168]{1,0:T(8,128)(2,1)S(1)}, u32[]{:S(2)}, u32[]{:S(2)}) %collective-permute-start.11) | collective-permute-done | bytes 114720 | tf_op jit(solution)/shard_map/ppermute | solution.py:186
  46.5 2.0 %collective-permute-done.12 = bf16[8,7168]{1,0:T(8,128)(2,1)S(1)} collective-permute-done((bf16[8,7168]{1,0:T(8,128)(2,1)S(1)}, bf16[8,7168]{1,0:T(8,128)(2,1)S(1)}, u32[]{:S(2)}, u32[]{:S(2)}) %collective-permute-start.12) | collective-permute-done | bytes 114720 | tf_op jit(solution)/shard_map/ppermute | solution.py:186
  48.6 0.0 collective-permute-done.9
  48.6 2.0 %collective-permute-done.10 = bf16[8,7168]{1,0:T(8,128)(2,1)S(1)} collective-permute-done((bf16[8,7168]{1,0:T(8,128)(2,1)S(1)}, bf16[8,7168]{1,0:T(8,128)(2,1)S(1)}, u32[]{:S(2)}, u32[]{:S(2)}) %collective-permute-start.10) | collective-permute-done | bytes 114720 | tf_op jit(solution)/shard_map/ppermute | solution.py:186
  50.7 0.1 fusion.9
  50.8 0.1 collective-permute-start.14
  50.9 1.3 %collective-permute-done.14 = bf16[8,7168]{1,0:T(8,128)(2,1)S(1)} collective-permute-done((bf16[8,7168]{1,0:T(8,128)(2,1)S(1)}, bf16[8,7168]{1,0:T(8,128)(2,1)S(1)}, u32[]{:S(2)}, u32[]{:S(2)}) %collective-permute-start.14) | collective-permute-done | bytes 114720 | tf_op jit(solution)/shard_map/ppermute | solution.py:237
  52.2 1.3 %convolution_convert_fusion = bf16[64,7168]{1,0:T(8,128)(2,1)} fusion(bf16[32,64]{1,0:T(8,128)(2,1)S(1)} %get-tuple-element.20, bf16[8,7168]{1,0:T(8,128)(2,1)S(1)} %collective-permute-done.14, bf16[8,7168]{1,0:T(8,128)(2,1)S(1)} %reshape.14), kind=kOutput, calls=%fused_computation | convolution fusion | flops 31653888 | bytes 1150976 | tf_op jit(solution)/shard_map/ct,cd->td/dot_general | solution.py:240
  (14 shorter events, 0.3 us)
Async XLA Ops:
  1.5 1.5 %collective-permute-start = (bf16[8,7168]{1,0:T(8,128)(2,1)S(1)}, bf16[8,7168]{1,0:T(8,128)(2,1)S(1)}, u32[]{:S(2)}, u32[]{:S(2)}) collective-permute-start(bf16[8,7168]{1,0:T(8,128)(2,1)S(1)} %get-tuple-element.22), channel_id=1, source_target_pairs={{0,4},{4,0},{8,12},{12,8},{1,5},{5,1},{9,13},{13,9},{2,6},{6,2},{1... | collective-permute-start | bytes 344072 | tf_op jit(solution)/shard_map/ppermute | solution.py:191
  3.1 6.4 %collective-permute-start.1 = (bf16[8,7168]{1,0:T(8,128)(2,1)S(1)}, bf16[8,7168]{1,0:T(8,128)(2,1)S(1)}, u32[]{:S(2)}, u32[]{:S(2)}) collective-permute-start(bf16[8,7168]{1,0:T(8,128)(2,1)S(1)} %fusion.12), channel_id=1, source_target_pairs={{0,8},{1,9},{2,10},{3,11},{4,12},{5,13},{6,14},{7,15},{8,0},{9,1},... | collective-permute-start | bytes 344072 | tf_op jit(solution)/shard_map/ppermute | solution.py:186
  6.1 11.3 %collective-permute-start.3 = (bf16[8,7168]{1,0:T(8,128)(2,1)S(1)}, bf16[8,7168]{1,0:T(8,128)(2,1)S(1)}, u32[]{:S(2)}, u32[]{:S(2)}) collective-permute-start(bf16[8,7168]{1,0:T(8,128)(2,1)S(1)} %get-tuple-element.36), channel_id=1, source_target_pairs={{0,2},{1,3},{2,0},{3,1},{4,6},{5,7},{6,4},{7,5},{8,10},{9,11},{10,... | collective-permute-start | bytes 344072 | tf_op jit(solution)/shard_map/ppermute | solution.py:186
  9.5 13.4 %collective-permute-start.2 = (bf16[16,7168]{1,0:T(8,128)(2,1)S(1)}, bf16[16,7168]{1,0:T(8,128)(2,1)S(1)}, u32[]{:S(2)}, u32[]{:S(2)}) collective-permute-start(bf16[16,7168]{1,0:T(8,128)(2,1)S(1)} %pad_maximum_fusion), channel_id=1, source_target_pairs={{0,1},{1,0},{2,3},{3,2},{4,5},{5,4},{6,7},{7,6},{8,9},{9,8},{10,11... | collective-permute-start | bytes 688136 | tf_op jit(solution)/shard_map/ppermute | solution.py:186
  11.4 8.4 %collective-permute-start.4 = (bf16[8,7168]{1,0:T(8,128)(2,1)S(1)}, bf16[8,7168]{1,0:T(8,128)(2,1)S(1)}, u32[]{:S(2)}, u32[]{:S(2)}) collective-permute-start(bf16[8,7168]{1,0:T(8,128)(2,1)S(1)} %collective-permute-done.1), channel_id=1, source_target_pairs={{0,2},{1,3},{2,0},{3,1},{4,6},{5,7},{6,4},{7,5},{8,10},{9,11},{10,... | collective-permute-start | bytes 344072 | tf_op jit(solution)/shard_map/ppermute | solution.py:186
  14.0 11.7 %slice-start = ((s8[7340032]{0:T(1024)(128)(4,1)}), s8[4194304]{0:T(1024)(128)(4,1)S(1)}, s32[]{:S(2)}) async-start(s8[7340032]{0:T(1024)(128)(4,1)} %bitcast.12), calls=%async_computation | async-start | bytes 8388608
  14.0 11.7 %slice-start.1 = ((s8[7340032]{0:T(1024)(128)(4,1)}), s8[3145728]{0:T(1024)(128)(4,1)S(1)}, s32[]{:S(2)}) async-start(s8[7340032]{0:T(1024)(128)(4,1)} %bitcast.12), calls=%async_computation.1 | async-start | bytes 6291456
  17.3 6.8 %collective-permute-start.5 = (bf16[8,7168]{1,0:T(8,128)(2,1)S(1)}, bf16[8,7168]{1,0:T(8,128)(2,1)S(1)}, u32[]{:S(2)}, u32[]{:S(2)}) collective-permute-start(bf16[8,7168]{1,0:T(8,128)(2,1)S(1)} %collective-permute-done.3), channel_id=1, source_target_pairs={{0,1},{1,0},{2,3},{3,2},{4,5},{5,4},{6,7},{7,6},{8,9},{9,8},{10,11... | collective-permute-start | bytes 344072 | tf_op jit(solution)/shard_map/ppermute | solution.py:186
  19.8 5.9 %collective-permute-start.6 = (bf16[8,7168]{1,0:T(8,128)(2,1)S(1)}, bf16[8,7168]{1,0:T(8,128)(2,1)S(1)}, u32[]{:S(2)}, u32[]{:S(2)}) collective-permute-start(bf16[8,7168]{1,0:T(8,128)(2,1)S(1)} %collective-permute-done.4), channel_id=1, source_target_pairs={{0,1},{1,0},{2,3},{3,2},{4,5},{5,4},{6,7},{7,6},{8,9},{9,8},{10,11... | collective-permute-start | bytes 344072 | tf_op jit(solution)/shard_map/ppermute | solution.py:186
  30.3 4.9 %collective-permute-start.7 = (bf16[8,7168]{1,0:T(8,128)(2,1)S(1)}, bf16[8,7168]{1,0:T(8,128)(2,1)S(1)}, u32[]{:S(2)}, u32[]{:S(2)}) collective-permute-start(bf16[8,7168]{1,0:T(8,128)(2,1)S(1)} %get-tuple-element.28), channel_id=1, source_target_pairs={{0,1},{1,0},{2,3},{3,2},{4,5},{5,4},{6,7},{7,6},{8,9},{9,8},{10,11... | collective-permute-start | bytes 344072 | tf_op jit(solution)/shard_map/ppermute | solution.py:186
  32.4 7.1 %collective-permute-start.8 = (bf16[8,7168]{1,0:T(8,128)(2,1)S(1)}, bf16[8,7168]{1,0:T(8,128)(2,1)S(1)}, u32[]{:S(2)}, u32[]{:S(2)}) collective-permute-start(bf16[8,7168]{1,0:T(8,128)(2,1)S(1)} %get-tuple-element.29), channel_id=1, source_target_pairs={{0,1},{1,0},{2,3},{3,2},{4,5},{5,4},{6,7},{7,6},{8,9},{9,8},{10,11... | collective-permute-start | bytes 344072 | tf_op jit(solution)/shard_map/ppermute | solution.py:186
  35.2 10.0 %collective-permute-start.13 = (bf16[8,7168]{1,0:T(8,128)(2,1)S(1)}, bf16[8,7168]{1,0:T(8,128)(2,1)S(1)}, u32[]{:S(2)}, u32[]{:S(2)}) collective-permute-start(bf16[8,7168]{1,0:T(8,128)(2,1)S(1)} %add_convert_fusion.1), channel_id=1, source_target_pairs={{0,10},{1,11},{2,8},{3,9},{4,14},{5,15},{6,12},{7,13},{8,2},{9,3},... | collective-permute-start | bytes 344072 | tf_op jit(solution)/shard_map/ppermute | solution.py:186
  39.5 9.1 %collective-permute-start.9 = (bf16[8,7168]{1,0:T(8,128)(2,1)S(1)}, bf16[8,7168]{1,0:T(8,128)(2,1)S(1)}, u32[]{:S(2)}, u32[]{:S(2)}) collective-permute-start(bf16[8,7168]{1,0:T(8,128)(2,1)S(1)} %get-tuple-element.30), channel_id=1, source_target_pairs={{0,1},{1,0},{2,3},{3,2},{4,5},{5,4},{6,7},{7,6},{8,9},{9,8},{10,11... | collective-permute-start | bytes 344072 | tf_op jit(solution)/shard_map/ppermute | solution.py:186
  41.5 5.0 %collective-permute-start.11 = (bf16[8,7168]{1,0:T(8,128)(2,1)S(1)}, bf16[8,7168]{1,0:T(8,128)(2,1)S(1)}, u32[]{:S(2)}, u32[]{:S(2)}) collective-permute-start(bf16[8,7168]{1,0:T(8,128)(2,1)S(1)} %get-tuple-element.32), channel_id=1, source_target_pairs={{0,8},{1,9},{2,10},{3,11},{4,12},{5,13},{6,14},{7,15},{8,0},{9,1},... | collective-permute-start | bytes 344072 | tf_op jit(solution)/shard_map/ppermute | solution.py:186
  42.7 5.9 %collective-permute-start.12 = (bf16[8,7168]{1,0:T(8,128)(2,1)S(1)}, bf16[8,7168]{1,0:T(8,128)(2,1)S(1)}, u32[]{:S(2)}, u32[]{:S(2)}) collective-permute-start(bf16[8,7168]{1,0:T(8,128)(2,1)S(1)} %get-tuple-element.33), channel_id=1, source_target_pairs={{0,9},{1,8},{2,11},{3,10},{4,13},{5,12},{6,15},{7,14},{8,1},{9,0},... | collective-permute-start | bytes 344072 | tf_op jit(solution)/shard_map/ppermute | solution.py:186
  43.0 7.6 %collective-permute-start.10 = (bf16[8,7168]{1,0:T(8,128)(2,1)S(1)}, bf16[8,7168]{1,0:T(8,128)(2,1)S(1)}, u32[]{:S(2)}, u32[]{:S(2)}) collective-permute-start(bf16[8,7168]{1,0:T(8,128)(2,1)S(1)} %add_convert_fusion.3), channel_id=1, source_target_pairs={{0,2},{1,3},{2,0},{3,1},{4,6},{5,7},{6,4},{7,5},{8,10},{9,11},{10,... | collective-permute-start | bytes 344072 | tf_op jit(solution)/shard_map/ppermute | solution.py:186
  50.8 1.4 %collective-permute-start.14 = (bf16[8,7168]{1,0:T(8,128)(2,1)S(1)}, bf16[8,7168]{1,0:T(8,128)(2,1)S(1)}, u32[]{:S(2)}, u32[]{:S(2)}) collective-permute-start(bf16[8,7168]{1,0:T(8,128)(2,1)S(1)} %reshape.15), channel_id=1, source_target_pairs={{0,4},{4,0},{8,12},{12,8},{1,5},{5,1},{9,13},{13,9},{2,6},{6,2},{1... | collective-permute-start | bytes 344072 | tf_op jit(solution)/shard_map/ppermute | solution.py:237

commit v6 on v5

--- a/solution.py
+++ b/solution.py
@@ -191,24 +191,21 @@
     swapped = lax.ppermute(sent, "expert", core_pairs).reshape(chips, CAP, width)
     blocks = jnp.concatenate([kept.reshape(chips, CAP, width), swapped], axis=1)
     size = CORES * CAP
-    others = [travel(blocks[x], x, 0) for x in range(1, chips)]
-    own = jnp.concatenate([blocks[0]] + others, axis=0)
-    held = [{0: own[x * size:(x + 1) * size] if x else blocks[0]} for x in range(chips)]
+    held = {0: blocks.reshape(chips * size, width)}
     for bit in reversed(bits[1:]):
-        for blocks_of in held:
-            blocks_of.update({offset ^ bit: travel(blocks_of[offset], 0, bit) for offset in list(blocks_of)})
-    near = travel(own, 0, 1) if shards > 1 else None
-    passed = [
-        (x, offset ^ 1, travel(held[x][offset], 0, 1)) for x in range(chips) for offset in held[x] if offset and shards > 1
-    ]
-    ways = [(x, 0) for x in range(chips)] + [(x, 1) for x in range(chips) if shards > 1]
-    ways += [(x, offset) for x in range(chips) for offset in held[x] if offset]
-    ways += [(x, offset) for x, offset, _ in passed]
-    pieces = [own] + ([near] if shards > 1 else [])
-    pieces += [held[x][offset] for x in range(chips) for offset in held[x] if offset]
-    rows = jnp.concatenate(pieces + [block for _, _, block in passed], axis=0)
-
-    w_up, _ = lax.optimization_barrier((w_up, own))
+        for offset in list(held):
+            held[offset ^ bit] = [travel(held[offset][x * size:(x + 1) * size], 0, bit) for x in range(chips)]
+            held[offset ^ bit] = jnp.concatenate(held[offset ^ bit], axis=0)
+    ways, pieces = [], []
+    for offset in list(held):
+        for x in range(chips):
+            block = held[offset][x * size:(x + 1) * size]
+            for bit in [0] + bits[:1]:
+                ways.append((x, offset ^ bit))
+                pieces.append(travel(block, x, bit) if x or bit else block)
+    rows = jnp.concatenate(pieces, axis=0)
+
+    w_up, _ = lax.optimization_barrier((w_up, swapped))
     partial = ffn(rows, w_gate, hold(w_up), w_down, size)
 
     parts = dict(zip(ways, partial))

time: 53.7 us -> 51.8 us (0.965)
  starting transfers between devices: 26.4 us -> 22.5 us
  waiting for transfers between devices: 15.7 us -> 17.7 us
    ppermute x13 -> x15, starting transfers between devices: 25.8 us -> 21.9 us  [travel(): return lax.ppermute(block, ('expert', 'dp'), pairs)]
    ppermute x13 -> x15, waiting for transfers between devices: 13.5 us -> 15.5 us  [travel(): return lax.ppermute(block, ('expert', 'dp'), pairs)]
  transfers between devices with their start and end apart: 15 -> 17, of which waited for: 10 -> 9; matrix products, arithmetic and copies ran while one was open for 1% -> 0% of each run, Pallas kernels for 6% -> 6%
where the time goes in v6:
time: 51.8 us; the launch traced here: 51.6 us
  starting transfers between devices  22.5 us (43%)
  waiting for transfers between devices  17.7 us (34%)
  Pallas kernels  9.24 us (18%)
  matrix products  1.34 us (3%)
    ppermute x15, starting transfers between devices, travel(): return lax.ppermute(block, ('expert', 'dp'), pairs)  21.9 us
    ppermute x15, waiting for transfers between devices, travel(): return lax.ppermute(block, ('expert', 'dp'), pairs)  15.5 us
    pallas_call x1, Pallas kernels, ffn(): pl.pallas_call(ffn_kernel, out_shape=[jax.ShapeDtypeStruct((part, width),...  4.57 us
    pallas_call x1, Pallas kernels, hold(): pl.pallas_call(hold_kernel, out_shape=pltpu.VMEM(weight.shape, weight.dty...  3.18 us
    pallas_call x1, Pallas kernels, route(): pl.pallas_call(functools.partial(route_kernel, chips), out_shape=[jax.Sha...  1.48 us
    dot_general x1, matrix products, local(): jnp.einsum('ct,cd->td', mix, jnp.concatenate([expert_out, expert_out], ax...  1.34 us
    ppermute x1, waiting for transfers between devices, local(): lax.ppermute(home[:, CAP:].reshape(half, width), 'expert', core_pairs)  1.27 us
  transfers between devices with their start and end apart: 17, of which 9 were waited for; matrix products, arithmetic and copies ran while one was open for 0% of the time, Pallas kernels for 6%

profile of v6, /device:TPU:0, one launch (start us, length us, event | category | flops | bytes accessed | tf_op | source)
XLA Modules:
  0.0 51.6 jit_solution(1927263307234012437)
XLA Ops:
  0.0 1.5 %shard_map.64 = (bf16[8,7168]{1,0:T(8,128)(2,1)S(1)}, bf16[8,7168]{1,0:T(8,128)(2,1)S(1)}, bf16[32,64]{1,0:T(8,128)(2,1)S(1)}) custom-call(s32[8,64]{1,0:T(8,128)} %bitcast.14, f32[8,64]{1,0:T(8,128)} %bitcast.15, bf16[64,7168]{1,0:T(8,128)(2,1)} %refs_2_.1), custom_call_target="tpu_custom_call" | custom-call | flops 29360128 | bytes 1835008 | tf_op jit(solution)/shard_map/pallas_call | solution.py:65
  1.5 0.5 %collective-permute-start = (bf16[8,7168]{1,0:T(8,128)(2,1)S(1)}, bf16[8,7168]{1,0:T(8,128)(2,1)S(1)}, u32[]{:S(2)}, u32[]{:S(2)}) collective-permute-start(bf16[8,7168]{1,0:T(8,128)(2,1)S(1)} %get-tuple-element.22), channel_id=1, source_target_pairs={{0,4},{4,0},{8,12},{12,8},{1,5},{5,1},{9,13},{13,9},{2,6},{6,2},{1... | collective-permute-start | bytes 344072 | tf_op jit(solution)/shard_map/ppermute | solution.py:191
  2.0 0.1 reshape.15
  2.1 0.9 %collective-permute-done = bf16[8,7168]{1,0:T(8,128)(2,1)S(1)} collective-permute-done((bf16[8,7168]{1,0:T(8,128)(2,1)S(1)}, bf16[8,7168]{1,0:T(8,128)(2,1)S(1)}, u32[]{:S(2)}, u32[]{:S(2)}) %collective-permute-start) | collective-permute-done | bytes 114720 | tf_op jit(solution)/shard_map/ppermute | solution.py:191
  3.0 0.1 reshape.16
  3.0 0.1 fusion.12
  3.1 0.1 constant_dynamic-update-slice_fusion.7
  3.2 4.0 %collective-permute-start.6 = (bf16[8,7168]{1,0:T(8,128)(2,1)S(1)}, bf16[8,7168]{1,0:T(8,128)(2,1)S(1)}, u32[]{:S(2)}, u32[]{:S(2)}) collective-permute-start(bf16[8,7168]{1,0:T(8,128)(2,1)S(1)} %fusion.12), channel_id=1, source_target_pairs={{0,2},{1,3},{2,0},{3,1},{4,6},{5,7},{6,4},{7,5},{8,10},{9,11},{10,... | collective-permute-start | bytes 344072 | tf_op jit(solution)/shard_map/ppermute | solution.py:186
  7.2 0.0 slice-start
  7.2 0.0 slice-start.1
  7.2 0.1 collective-permute-start.4
  7.3 1.8 %collective-permute-start.1 = (bf16[8,7168]{1,0:T(8,128)(2,1)S(1)}, bf16[8,7168]{1,0:T(8,128)(2,1)S(1)}, u32[]{:S(2)}, u32[]{:S(2)}) collective-permute-start(bf16[8,7168]{1,0:T(8,128)(2,1)S(1)} %get-tuple-element.36), channel_id=1, source_target_pairs={{0,1},{1,0},{2,3},{3,2},{4,5},{5,4},{6,7},{7,6},{8,9},{9,8},{10,11... | collective-permute-start | bytes 344072 | tf_op jit(solution)/shard_map/ppermute | solution.py:186
  9.1 1.4 %collective-permute-start.3 = (bf16[8,7168]{1,0:T(8,128)(2,1)S(1)}, bf16[8,7168]{1,0:T(8,128)(2,1)S(1)}, u32[]{:S(2)}, u32[]{:S(2)}) collective-permute-start(bf16[8,7168]{1,0:T(8,128)(2,1)S(1)} %fusion.12), channel_id=1, source_target_pairs={{0,9},{1,8},{2,11},{3,10},{4,13},{5,12},{6,15},{7,14},{8,1},{9,0},... | collective-permute-start | bytes 344072 | tf_op jit(solution)/shard_map/ppermute | solution.py:186
  10.5 0.3 collective-permute-start.2
  10.8 3.2 %shard_map.65.up_ref = bf16[1,7168,512]{2,1,0:T(8,128)(2,1)S(1)} custom-call(bf16[1,7168,512]{2,1,0:T(8,128)(2,1)} %source), custom_call_target="tpu_custom_call" | custom-call | bytes 14680064 | tf_op jit(solution)/shard_map/pallas_call | solution.py:99
  14.0 2.1 %collective-permute-done.6 = bf16[8,7168]{1,0:T(8,128)(2,1)S(1)} collective-permute-done((bf16[8,7168]{1,0:T(8,128)(2,1)S(1)}, bf16[8,7168]{1,0:T(8,128)(2,1)S(1)}, u32[]{:S(2)}, u32[]{:S(2)}) %collective-permute-start.6) | collective-permute-done | bytes 114720 | tf_op jit(solution)/shard_map/ppermute | solution.py:186
  16.0 1.3 %collective-permute-start.8 = (bf16[8,7168]{1,0:T(8,128)(2,1)S(1)}, bf16[8,7168]{1,0:T(8,128)(2,1)S(1)}, u32[]{:S(2)}, u32[]{:S(2)}) collective-permute-start(bf16[8,7168]{1,0:T(8,128)(2,1)S(1)} %collective-permute-done.6), channel_id=1, source_target_pairs={{0,9},{1,8},{2,11},{3,10},{4,13},{5,12},{6,15},{7,14},{8,1},{9,0},... | collective-permute-start | bytes 344072 | tf_op jit(solution)/shard_map/ppermute | solution.py:186
  17.3 0.7 %collective-permute-done.4 = bf16[8,7168]{1,0:T(8,128)(2,1)S(1)} collective-permute-done((bf16[8,7168]{1,0:T(8,128)(2,1)S(1)}, bf16[8,7168]{1,0:T(8,128)(2,1)S(1)}, u32[]{:S(2)}, u32[]{:S(2)}) %collective-permute-start.4) | collective-permute-done | bytes 114720 | tf_op jit(solution)/shard_map/ppermute | solution.py:186
  18.0 1.6 %collective-permute-start.7 = (bf16[8,7168]{1,0:T(8,128)(2,1)S(1)}, bf16[8,7168]{1,0:T(8,128)(2,1)S(1)}, u32[]{:S(2)}, u32[]{:S(2)}) collective-permute-start(bf16[8,7168]{1,0:T(8,128)(2,1)S(1)} %collective-permute-done.6), channel_id=1, source_target_pairs={{0,8},{1,9},{2,10},{3,11},{4,12},{5,13},{6,14},{7,15},{8,0},{9,1},... | collective-permute-start | bytes 344072 | tf_op jit(solution)/shard_map/ppermute | solution.py:186
  19.6 0.0 collective-permute-done.1
  19.7 0.6 %collective-permute-start.5 = (bf16[8,7168]{1,0:T(8,128)(2,1)S(1)}, bf16[8,7168]{1,0:T(8,128)(2,1)S(1)}, u32[]{:S(2)}, u32[]{:S(2)}) collective-permute-start(bf16[8,7168]{1,0:T(8,128)(2,1)S(1)} %collective-permute-done.4), channel_id=1, source_target_pairs={{0,1},{1,0},{2,3},{3,2},{4,5},{5,4},{6,7},{7,6},{8,9},{9,8},{10,11... | collective-permute-start | bytes 344072 | tf_op jit(solution)/shard_map/ppermute | solution.py:186
  20.3 0.0 collective-permute-done.2
  20.3 0.0 collective-permute-done.3
  20.4 4.3 %collective-permute-done.5 = bf16[8,7168]{1,0:T(8,128)(2,1)S(1)} collective-permute-done((bf16[8,7168]{1,0:T(8,128)(2,1)S(1)}, bf16[8,7168]{1,0:T(8,128)(2,1)S(1)}, u32[]{:S(2)}, u32[]{:S(2)}) %collective-permute-start.5) | collective-permute-done | bytes 114720 | tf_op jit(solution)/shard_map/ppermute | solution.py:186
  24.7 0.0 collective-permute-done.7
  24.7 0.0 collective-permute-done.8
  24.7 0.0 slice-done
  24.7 0.0 slice-done.1
  24.8 4.6 %shard_map.66 = (bf16[8,7168]{1,0:T(8,128)(2,1)S(1)}, bf16[8,7168]{1,0:T(8,128)(2,1)S(1)}, bf16[8,7168]{1,0:T(8,128)(2,1)S(1)}, bf16[8,7168]{1,0:T(8,128)(2,1)S(...) custom-call(bf16[64,7168]{1,0:T(8,128)(2,1)S(1)} %constant_dynamic-u, ...), custom_call_target="tpu_custom_call" | custom-call | flops 1409286144 | bytes 7340032 | tf_op jit(solution)/shard_map/pallas_call | solution.py:145
  29.3 1.0 %collective-permute-start.9 = (bf16[8,7168]{1,0:T(8,128)(2,1)S(1)}, bf16[8,7168]{1,0:T(8,128)(2,1)S(1)}, u32[]{:S(2)}, u32[]{:S(2)}) collective-permute-start(bf16[8,7168]{1,0:T(8,128)(2,1)S(1)} %get-tuple-element.28), channel_id=1, source_target_pairs={{0,1},{1,0},{2,3},{3,2},{4,5},{5,4},{6,7},{7,6},{8,9},{9,8},{10,11... | collective-permute-start | bytes 344072 | tf_op jit(solution)/shard_map/ppermute | solution.py:186
  30.4 1.1 %collective-permute-start.10 = (bf16[8,7168]{1,0:T(8,128)(2,1)S(1)}, bf16[8,7168]{1,0:T(8,128)(2,1)S(1)}, u32[]{:S(2)}, u32[]{:S(2)}) collective-permute-start(bf16[8,7168]{1,0:T(8,128)(2,1)S(1)} %get-tuple-element.29), channel_id=1, source_target_pairs={{0,1},{1,0},{2,3},{3,2},{4,5},{5,4},{6,7},{7,6},{8,9},{9,8},{10,11... | collective-permute-start | bytes 344072 | tf_op jit(solution)/shard_map/ppermute | solution.py:186
  31.4 3.9 %collective-permute-done.9 = bf16[8,7168]{1,0:T(8,128)(2,1)S(1)} collective-permute-done((bf16[8,7168]{1,0:T(8,128)(2,1)S(1)}, bf16[8,7168]{1,0:T(8,128)(2,1)S(1)}, u32[]{:S(2)}, u32[]{:S(2)}) %collective-permute-start.9) | collective-permute-done | bytes 114720 | tf_op jit(solution)/shard_map/ppermute | solution.py:186
  35.4 2.9 %collective-permute-start.15 = (bf16[8,7168]{1,0:T(8,128)(2,1)S(1)}, bf16[8,7168]{1,0:T(8,128)(2,1)S(1)}, u32[]{:S(2)}, u32[]{:S(2)}) collective-permute-start(bf16[8,7168]{1,0:T(8,128)(2,1)S(1)} %add_convert_fusion.1), channel_id=1, source_target_pairs={{0,10},{1,11},{2,8},{3,9},{4,14},{5,15},{6,12},{7,13},{8,2},{9,3},... | collective-permute-start | bytes 344072 | tf_op jit(solution)/shard_map/ppermute | solution.py:186
  38.2 0.0 collective-permute-done.10
  38.2 2.1 %collective-permute-start.11 = (bf16[8,7168]{1,0:T(8,128)(2,1)S(1)}, bf16[8,7168]{1,0:T(8,128)(2,1)S(1)}, u32[]{:S(2)}, u32[]{:S(2)}) collective-permute-start(bf16[8,7168]{1,0:T(8,128)(2,1)S(1)} %get-tuple-element.30), channel_id=1, source_target_pairs={{0,1},{1,0},{2,3},{3,2},{4,5},{5,4},{6,7},{7,6},{8,9},{9,8},{10,11... | collective-permute-start | bytes 344072 | tf_op jit(solution)/shard_map/ppermute | solution.py:186
  40.3 1.4 %collective-permute-start.13 = (bf16[8,7168]{1,0:T(8,128)(2,1)S(1)}, bf16[8,7168]{1,0:T(8,128)(2,1)S(1)}, u32[]{:S(2)}, u32[]{:S(2)}) collective-permute-start(bf16[8,7168]{1,0:T(8,128)(2,1)S(1)} %get-tuple-element.32), channel_id=1, source_target_pairs={{0,8},{1,9},{2,10},{3,11},{4,12},{5,13},{6,14},{7,15},{8,0},{9,1},... | collective-permute-start | bytes 344072 | tf_op jit(solution)/shard_map/ppermute | solution.py:186
  41.7 0.0 collective-permute-start.14
  41.8 2.2 %collective-permute-start.12 = (bf16[8,7168]{1,0:T(8,128)(2,1)S(1)}, bf16[8,7168]{1,0:T(8,128)(2,1)S(1)}, u32[]{:S(2)}, u32[]{:S(2)}) collective-permute-start(bf16[8,7168]{1,0:T(8,128)(2,1)S(1)} %add_convert_fusion.3), channel_id=1, source_target_pairs={{0,2},{1,3},{2,0},{3,1},{4,6},{5,7},{6,4},{7,5},{8,10},{9,11},{10,... | collective-permute-start | bytes 344072 | tf_op jit(solution)/shard_map/ppermute | solution.py:186
  44.1 0.0 collective-permute-done.15
  44.1 1.1 %collective-permute-done.13 = bf16[8,7168]{1,0:T(8,128)(2,1)S(1)} collective-permute-done((bf16[8,7168]{1,0:T(8,128)(2,1)S(1)}, bf16[8,7168]{1,0:T(8,128)(2,1)S(1)}, u32[]{:S(2)}, u32[]{:S(2)}) %collective-permute-start.13) | collective-permute-done | bytes 114720 | tf_op jit(solution)/shard_map/ppermute | solution.py:186
  45.2 2.9 %collective-permute-done.14 = bf16[8,7168]{1,0:T(8,128)(2,1)S(1)} collective-permute-done((bf16[8,7168]{1,0:T(8,128)(2,1)S(1)}, bf16[8,7168]{1,0:T(8,128)(2,1)S(1)}, u32[]{:S(2)}, u32[]{:S(2)}) %collective-permute-start.14) | collective-permute-done | bytes 114720 | tf_op jit(solution)/shard_map/ppermute | solution.py:186
  48.2 0.0 collective-permute-done.11
  48.2 0.5 collective-permute-done.12
  48.7 0.1 fusion.9
  48.9 0.1 collective-permute-start.16
  49.0 1.3 %collective-permute-done.16 = bf16[8,7168]{1,0:T(8,128)(2,1)S(1)} collective-permute-done((bf16[8,7168]{1,0:T(8,128)(2,1)S(1)}, bf16[8,7168]{1,0:T(8,128)(2,1)S(1)}, u32[]{:S(2)}, u32[]{:S(2)}) %collective-permute-start.16) | collective-permute-done | bytes 114720 | tf_op jit(solution)/shard_map/ppermute | solution.py:234
  50.3 1.3 %convolution_convert_fusion = bf16[64,7168]{1,0:T(8,128)(2,1)} fusion(bf16[32,64]{1,0:T(8,128)(2,1)S(1)} %get-tuple-element.20, bf16[8,7168]{1,0:T(8,128)(2,1)S(1)} %collective-permute-done.16, bf16[8,7168]{1,0:T(8,128)(2,1)S(1)} %reshape.17), kind=kOutput, calls=%fused_computation | convolution fusion | flops 31653888 | bytes 1150976 | tf_op jit(solution)/shard_map/ct,cd->td/dot_general | solution.py:237
  (14 shorter events, 0.3 us)
Async XLA Ops:
  1.5 1.5 %collective-permute-start = (bf16[8,7168]{1,0:T(8,128)(2,1)S(1)}, bf16[8,7168]{1,0:T(8,128)(2,1)S(1)}, u32[]{:S(2)}, u32[]{:S(2)}) collective-permute-start(bf16[8,7168]{1,0:T(8,128)(2,1)S(1)} %get-tuple-element.22), channel_id=1, source_target_pairs={{0,4},{4,0},{8,12},{12,8},{1,5},{5,1},{9,13},{13,9},{2,6},{6,2},{1... | collective-permute-start | bytes 344072 | tf_op jit(solution)/shard_map/ppermute | solution.py:191
  3.2 12.9 %collective-permute-start.6 = (bf16[8,7168]{1,0:T(8,128)(2,1)S(1)}, bf16[8,7168]{1,0:T(8,128)(2,1)S(1)}, u32[]{:S(2)}, u32[]{:S(2)}) collective-permute-start(bf16[8,7168]{1,0:T(8,128)(2,1)S(1)} %fusion.12), channel_id=1, source_target_pairs={{0,2},{1,3},{2,0},{3,1},{4,6},{5,7},{6,4},{7,5},{8,10},{9,11},{10,... | collective-permute-start | bytes 344072 | tf_op jit(solution)/shard_map/ppermute | solution.py:186
  7.2 17.6 %slice-start = ((s8[7340032]{0:T(1024)(128)(4,1)}), s8[4194304]{0:T(1024)(128)(4,1)S(1)}, s32[]{:S(2)}) async-start(s8[7340032]{0:T(1024)(128)(4,1)} %bitcast.12), calls=%async_computation | async-start | bytes 8388608
  7.2 17.6 %slice-start.1 = ((s8[7340032]{0:T(1024)(128)(4,1)}), s8[3145728]{0:T(1024)(128)(4,1)S(1)}, s32[]{:S(2)}) async-start(s8[7340032]{0:T(1024)(128)(4,1)} %bitcast.12), calls=%async_computation.1 | async-start | bytes 6291456
  7.2 10.8 %collective-permute-start.4 = (bf16[8,7168]{1,0:T(8,128)(2,1)S(1)}, bf16[8,7168]{1,0:T(8,128)(2,1)S(1)}, u32[]{:S(2)}, u32[]{:S(2)}) collective-permute-start(bf16[8,7168]{1,0:T(8,128)(2,1)S(1)} %get-tuple-element.36), channel_id=1, source_target_pairs={{0,2},{1,3},{2,0},{3,1},{4,6},{5,7},{6,4},{7,5},{8,10},{9,11},{10,... | collective-permute-start | bytes 344072 | tf_op jit(solution)/shard_map/ppermute | solution.py:186
  7.3 12.4 %collective-permute-start.1 = (bf16[8,7168]{1,0:T(8,128)(2,1)S(1)}, bf16[8,7168]{1,0:T(8,128)(2,1)S(1)}, u32[]{:S(2)}, u32[]{:S(2)}) collective-permute-start(bf16[8,7168]{1,0:T(8,128)(2,1)S(1)} %get-tuple-element.36), channel_id=1, source_target_pairs={{0,1},{1,0},{2,3},{3,2},{4,5},{5,4},{6,7},{7,6},{8,9},{9,8},{10,11... | collective-permute-start | bytes 344072 | tf_op jit(solution)/shard_map/ppermute | solution.py:186
  9.1 11.2 %collective-permute-start.3 = (bf16[8,7168]{1,0:T(8,128)(2,1)S(1)}, bf16[8,7168]{1,0:T(8,128)(2,1)S(1)}, u32[]{:S(2)}, u32[]{:S(2)}) collective-permute-start(bf16[8,7168]{1,0:T(8,128)(2,1)S(1)} %fusion.12), channel_id=1, source_target_pairs={{0,9},{1,8},{2,11},{3,10},{4,13},{5,12},{6,15},{7,14},{8,1},{9,0},... | collective-permute-start | bytes 344072 | tf_op jit(solution)/shard_map/ppermute | solution.py:186
  10.5 9.8 %collective-permute-start.2 = (bf16[8,7168]{1,0:T(8,128)(2,1)S(1)}, bf16[8,7168]{1,0:T(8,128)(2,1)S(1)}, u32[]{:S(2)}, u32[]{:S(2)}) collective-permute-start(bf16[8,7168]{1,0:T(8,128)(2,1)S(1)} %fusion.12), channel_id=1, source_target_pairs={{0,8},{1,9},{2,10},{3,11},{4,12},{5,13},{6,14},{7,15},{8,0},{9,1},... | collective-permute-start | bytes 344072 | tf_op jit(solution)/shard_map/ppermute | solution.py:186
  16.0 8.7 %collective-permute-start.8 = (bf16[8,7168]{1,0:T(8,128)(2,1)S(1)}, bf16[8,7168]{1,0:T(8,128)(2,1)S(1)}, u32[]{:S(2)}, u32[]{:S(2)}) collective-permute-start(bf16[8,7168]{1,0:T(8,128)(2,1)S(1)} %collective-permute-done.6), channel_id=1, source_target_pairs={{0,9},{1,8},{2,11},{3,10},{4,13},{5,12},{6,15},{7,14},{8,1},{9,0},... | collective-permute-start | bytes 344072 | tf_op jit(solution)/shard_map/ppermute | solution.py:186
  18.0 6.7 %collective-permute-start.7 = (bf16[8,7168]{1,0:T(8,128)(2,1)S(1)}, bf16[8,7168]{1,0:T(8,128)(2,1)S(1)}, u32[]{:S(2)}, u32[]{:S(2)}) collective-permute-start(bf16[8,7168]{1,0:T(8,128)(2,1)S(1)} %collective-permute-done.6), channel_id=1, source_target_pairs={{0,8},{1,9},{2,10},{3,11},{4,12},{5,13},{6,14},{7,15},{8,0},{9,1},... | collective-permute-start | bytes 344072 | tf_op jit(solution)/shard_map/ppermute | solution.py:186
  19.7 5.0 %collective-permute-start.5 = (bf16[8,7168]{1,0:T(8,128)(2,1)S(1)}, bf16[8,7168]{1,0:T(8,128)(2,1)S(1)}, u32[]{:S(2)}, u32[]{:S(2)}) collective-permute-start(bf16[8,7168]{1,0:T(8,128)(2,1)S(1)} %collective-permute-done.4), channel_id=1, source_target_pairs={{0,1},{1,0},{2,3},{3,2},{4,5},{5,4},{6,7},{7,6},{8,9},{9,8},{10,11... | collective-permute-start | bytes 344072 | tf_op jit(solution)/shard_map/ppermute | solution.py:186
  29.3 6.0 %collective-permute-start.9 = (bf16[8,7168]{1,0:T(8,128)(2,1)S(1)}, bf16[8,7168]{1,0:T(8,128)(2,1)S(1)}, u32[]{:S(2)}, u32[]{:S(2)}) collective-permute-start(bf16[8,7168]{1,0:T(8,128)(2,1)S(1)} %get-tuple-element.28), channel_id=1, source_target_pairs={{0,1},{1,0},{2,3},{3,2},{4,5},{5,4},{6,7},{7,6},{8,9},{9,8},{10,11... | collective-permute-start | bytes 344072 | tf_op jit(solution)/shard_map/ppermute | solution.py:186
  30.4 7.9 %collective-permute-start.10 = (bf16[8,7168]{1,0:T(8,128)(2,1)S(1)}, bf16[8,7168]{1,0:T(8,128)(2,1)S(1)}, u32[]{:S(2)}, u32[]{:S(2)}) collective-permute-start(bf16[8,7168]{1,0:T(8,128)(2,1)S(1)} %get-tuple-element.29), channel_id=1, source_target_pairs={{0,1},{1,0},{2,3},{3,2},{4,5},{5,4},{6,7},{7,6},{8,9},{9,8},{10,11... | collective-permute-start | bytes 344072 | tf_op jit(solution)/shard_map/ppermute | solution.py:186
  35.4 8.7 %collective-permute-start.15 = (bf16[8,7168]{1,0:T(8,128)(2,1)S(1)}, bf16[8,7168]{1,0:T(8,128)(2,1)S(1)}, u32[]{:S(2)}, u32[]{:S(2)}) collective-permute-start(bf16[8,7168]{1,0:T(8,128)(2,1)S(1)} %add_convert_fusion.1), channel_id=1, source_target_pairs={{0,10},{1,11},{2,8},{3,9},{4,14},{5,15},{6,12},{7,13},{8,2},{9,3},... | collective-permute-start | bytes 344072 | tf_op jit(solution)/shard_map/ppermute | solution.py:186
  38.2 9.9 %collective-permute-start.11 = (bf16[8,7168]{1,0:T(8,128)(2,1)S(1)}, bf16[8,7168]{1,0:T(8,128)(2,1)S(1)}, u32[]{:S(2)}, u32[]{:S(2)}) collective-permute-start(bf16[8,7168]{1,0:T(8,128)(2,1)S(1)} %get-tuple-element.30), channel_id=1, source_target_pairs={{0,1},{1,0},{2,3},{3,2},{4,5},{5,4},{6,7},{7,6},{8,9},{9,8},{10,11... | collective-permute-start | bytes 344072 | tf_op jit(solution)/shard_map/ppermute | solution.py:186
  40.3 4.9 %collective-permute-start.13 = (bf16[8,7168]{1,0:T(8,128)(2,1)S(1)}, bf16[8,7168]{1,0:T(8,128)(2,1)S(1)}, u32[]{:S(2)}, u32[]{:S(2)}) collective-permute-start(bf16[8,7168]{1,0:T(8,128)(2,1)S(1)} %get-tuple-element.32), channel_id=1, source_target_pairs={{0,8},{1,9},{2,10},{3,11},{4,12},{5,13},{6,14},{7,15},{8,0},{9,1},... | collective-permute-start | bytes 344072 | tf_op jit(solution)/shard_map/ppermute | solution.py:186
  41.7 6.4 %collective-permute-start.14 = (bf16[8,7168]{1,0:T(8,128)(2,1)S(1)}, bf16[8,7168]{1,0:T(8,128)(2,1)S(1)}, u32[]{:S(2)}, u32[]{:S(2)}) collective-permute-start(bf16[8,7168]{1,0:T(8,128)(2,1)S(1)} %get-tuple-element.33), channel_id=1, source_target_pairs={{0,9},{1,8},{2,11},{3,10},{4,13},{5,12},{6,15},{7,14},{8,1},{9,0},... | collective-permute-start | bytes 344072 | tf_op jit(solution)/shard_map/ppermute | solution.py:186
  41.8 6.9 %collective-permute-start.12 = (bf16[8,7168]{1,0:T(8,128)(2,1)S(1)}, bf16[8,7168]{1,0:T(8,128)(2,1)S(1)}, u32[]{:S(2)}, u32[]{:S(2)}) collective-permute-start(bf16[8,7168]{1,0:T(8,128)(2,1)S(1)} %add_convert_fusion.3), channel_id=1, source_target_pairs={{0,2},{1,3},{2,0},{3,1},{4,6},{5,7},{6,4},{7,5},{8,10},{9,11},{10,... | collective-permute-start | bytes 344072 | tf_op jit(solution)/shard_map/ppermute | solution.py:186
  48.9 1.4 %collective-permute-start.16 = (bf16[8,7168]{1,0:T(8,128)(2,1)S(1)}, bf16[8,7168]{1,0:T(8,128)(2,1)S(1)}, u32[]{:S(2)}, u32[]{:S(2)}) collective-permute-start(bf16[8,7168]{1,0:T(8,128)(2,1)S(1)} %reshape.18), channel_id=1, source_target_pairs={{0,4},{4,0},{8,12},{12,8},{1,5},{5,1},{9,13},{13,9},{2,6},{6,2},{1... | collective-permute-start | bytes 344072 | tf_op jit(solution)/shard_map/ppermute | solution.py:234

commit v7 on v6

--- a/solution.py
+++ b/solution.py
@@ -107,64 +107,70 @@
     )(pltpu.with_memory_space_constraint(weight, pltpu.HBM))
 
 
-def ffn_kernel(rows_ref, gate_ref, up_ref, down_hbm, *refs):
-    out_refs, (down_ref, gate_sum, up_sum, sems) = refs[:-4], refs[-4:]
-    units = down_hbm.shape[1] // PIECES
-    copies = []
-    for piece in range(PIECES):
-        at = pl.ds(piece * units, units)
-        copies.append(pltpu.make_async_copy(down_hbm.at[0, at], down_ref.at[at], sems.at[piece]))
-    for copy in copies:
-        copy.start()
-    depth = rows_ref.shape[1] // STEPS
-    gate_sum[...] = jnp.zeros_like(gate_sum)
-    up_sum[...] = jnp.zeros_like(up_sum)
-
-    @pl.loop(0, STEPS)
-    def _(step):
-        at = pl.ds(pl.multiple_of(step * depth, 128), depth)
-        rows = rows_ref[:, at]
-        gate_sum[...] += jnp.dot(rows, gate_ref[0, at], preferred_element_type=jnp.float32)
-        up_sum[...] += jnp.dot(rows, up_ref[0, at], preferred_element_type=jnp.float32)
-
-    gate, up = gate_sum[...], up_sum[...]
+def ffn_kernel(rows_ref, gate_ref, up_ref, down_ref, *out_refs):
+    rows = rows_ref[...]
+    gate = jnp.dot(rows, gate_ref[0], preferred_element_type=jnp.float32)
+    up = jnp.dot(rows, up_ref[0], preferred_element_type=jnp.float32)
     hidden = (gate / (1.0 + jnp.exp(-gate)) * up).astype(jnp.bfloat16)
-    for copy in copies:
-        copy.wait()
     part, width = out_refs[0].shape
     tile = 1024
     for start in range(0, width, tile):
-        product = jnp.dot(hidden, down_ref[:, start:start + tile], preferred_element_type=jnp.float32)
+        product = jnp.dot(hidden, down_ref[0, :, start:start + tile], preferred_element_type=jnp.float32)
         for i, out_ref in enumerate(out_refs):
             out_ref[:, start:start + tile] = product[i * part:(i + 1) * part].astype(out_ref.dtype)
 
 
-def ffn(rows, gate, up, w_down, part):
+def ffn(rows, weights, part):
     vmem = pl.BlockSpec(memory_space=pltpu.VMEM)
-    units, width = w_down.shape[1:]
+    units, width = weights[2].shape[1:]
     return pl.pallas_call(
         ffn_kernel,
         out_shape=[jax.ShapeDtypeStruct((part, width), jnp.bfloat16)] * (rows.shape[0] // part),
-        in_specs=[vmem] * 3 + [pl.BlockSpec(memory_space=pltpu.HBM)],
+        in_specs=[vmem] * 4,
         out_specs=[vmem] * (rows.shape[0] // part),
-        scratch_shapes=[
-            pltpu.VMEM((units, width), w_down.dtype),
-            pltpu.VMEM((rows.shape[0], units), jnp.float32),
-            pltpu.VMEM((rows.shape[0], units), jnp.float32),
-            pltpu.SemaphoreType.DMA((PIECES,)),
-        ],
-        compiler_params=pltpu.CompilerParams(vmem_limit_bytes=16 * 1024 * 1024),
+        compiler_params=pltpu.CompilerParams(vmem_limit_bytes=8 * 1024 * 1024),
         cost_estimate=pl.CostEstimate(
             flops=6 * rows.shape[0] * width * units,
             bytes_accessed=2 * width * units,
             transcendentals=rows.shape[0] * units,
         ),
-    )(
-        rows,
-        pltpu.with_memory_space_constraint(gate, pltpu.VMEM),
-        pltpu.with_memory_space_constraint(up, pltpu.VMEM),
-        pltpu.with_memory_space_constraint(w_down, pltpu.HBM),
-    )
+    )(rows, *weights)
+
+
+def combine_kernel(mix_ref, mine_ref, other_ref, out_hbm, out_ref, sems):
+    mix = mix_ref[...].astype(jnp.float32)
+    weight = mix.T.astype(jnp.bfloat16)
+    width = out_ref.shape[1]
+    tile = 1024
+    copies = []
+    for i, start in enumerate(range(0, width, tile)):
+        rows = jnp.concatenate(
+            [ref[:, start:start + tile].astype(jnp.float32) for ref in (mine_ref, other_ref)] * 2, axis=0
+        ).astype(jnp.bfloat16)
+        out_ref[:, start:start + tile] = jnp.dot(
+            weight, rows, preferred_element_type=jnp.float32
+        ).astype(out_ref.dtype)
+        at = pl.ds(start, tile)
+        copies.append(pltpu.make_async_copy(out_ref.at[:, at], out_hbm.at[:, at], sems.at[i]))
+        copies[-1].start()
+    for copy in copies:
+        copy.wait()
+
+
+def combine(mix, mine, other):
+    vmem = pl.BlockSpec(memory_space=pltpu.VMEM)
+    shape = (mix.shape[1], mine.shape[1])
+    return pl.pallas_call(
+        combine_kernel,
+        out_shape=jax.ShapeDtypeStruct(shape, jnp.bfloat16),
+        in_specs=[vmem] * 3,
+        out_specs=pl.BlockSpec(memory_space=pltpu.HBM),
+        scratch_shapes=[pltpu.VMEM(shape, jnp.bfloat16), pltpu.SemaphoreType.DMA((shape[1] // 1024,))],
+        compiler_params=pltpu.CompilerParams(vmem_limit_bytes=8 * 1024 * 1024),
+        cost_estimate=pl.CostEstimate(
+            flops=2 * mix.shape[0] * shape[0] * shape[1], bytes_accessed=2 * shape[0] * shape[1], transcendentals=0
+        ),
+    )(mix, mine, other)
 
 
 def local(tokens, expert_ids, gate_weights, w_gate, w_up, w_down):
@@ -196,19 +202,24 @@
         for offset in list(held):
             held[offset ^ bit] = [travel(held[offset][x * size:(x + 1) * size], 0, bit) for x in range(chips)]
             held[offset ^ bit] = jnp.concatenate(held[offset ^ bit], axis=0)
-    ways, pieces = [], []
+    early, late = {}, {}
     for offset in list(held):
         for x in range(chips):
             block = held[offset][x * size:(x + 1) * size]
             for bit in [0] + bits[:1]:
-                ways.append((x, offset ^ bit))
-                pieces.append(travel(block, x, bit) if x or bit else block)
-    rows = jnp.concatenate(pieces, axis=0)
+                arrived = travel(block, x, bit) if x or bit else block
+                (late if offset and (x or bit) else early)[x, offset ^ bit] = arrived
 
     w_up, _ = lax.optimization_barrier((w_up, swapped))
-    partial = ffn(rows, w_gate, hold(w_up), w_down, size)
-
-    parts = dict(zip(ways, partial))
+    weights = [pltpu.with_memory_space_constraint(w, pltpu.VMEM) for w in (w_gate, hold(w_up), w_down)]
+    parts = {}
+    for some in (early, late):
+        blocks = list(some.values())
+        if parts:
+            blocks, _ = lax.optimization_barrier((blocks, parts[0, 0]))
+        if some:
+            parts.update(zip(some, ffn(jnp.concatenate(blocks, axis=0), weights, size)))
+
     home = {x: [] for x in range(chips)}
     relayed = []
     last = [(x, 0, 0) for x in range(chips)]
@@ -232,12 +243,7 @@
     home = jnp.stack([sum(block.astype(jnp.float32) for block in home[x]).astype(jnp.bfloat16) for x in range(chips)])
     mine = home[:, :CAP].reshape(half, width)
     other = lax.ppermute(home[:, CAP:].reshape(half, width), "expert", core_pairs)
-    expert_out = jnp.concatenate([mine, other], axis=0)
-
-    mixed = jnp.einsum(
-        "ct,cd->td", mix, jnp.concatenate([expert_out, expert_out], axis=0), preferred_element_type=jnp.float32
-    )
-    return mixed.astype(jnp.bfloat16)
+    return combine(mix, mine, other)
 
 
 def solution(mesh):

time: 51.8 us -> 49.7 us (0.959)
  waiting for transfers between devices: 17.7 us -> 10.3 us
  Pallas kernels: 9.24 us -> 14.4 us
  starting transfers between devices: 22.5 us -> 24.1 us
  matrix products: 1.34 us -> 0 us
    ppermute x15, waiting for transfers between devices: 15.5 us -> 8.08 us  [travel(): return lax.ppermute(block, ('expert', 'dp'), pairs)]
    pallas_call x1 -> x2, Pallas kernels: 4.57 us -> 7.91 us  [ffn(): pl.pallas_call(ffn_kernel, out_shape=[jax.ShapeDtypeStruct((part, width),...]
    ppermute x15, starting transfers between devices: 21.9 us -> 23.5 us  [travel(): return lax.ppermute(block, ('expert', 'dp'), pairs)]
    dot_general x1 -> x0, matrix products: 1.34 us -> none  [local(): jnp.einsum('ct,cd->td', mix, jnp.concatenate([expert_out, expert_out], ax...]
    pallas_call x0 -> x1, Pallas kernels: none -> 1.22 us  [combine(): pl.pallas_call(combine_kernel, out_shape=jax.ShapeDtypeStruct(shape, jnp....]
    pallas_call x1, Pallas kernels: 3.18 us -> 3.82 us  [hold(): pl.pallas_call(hold_kernel, out_shape=pltpu.VMEM(weight.shape, weight.dty...]
  transfers between devices with their start and end apart: 17 -> 17, of which waited for: 9 -> 8; matrix products, arithmetic and copies ran while one was open for 0% -> 0% of each run, Pallas kernels for 6% -> 16%
where the time goes in v7:
time: 49.7 us; the launch traced here: 49.5 us
  starting transfers between devices  24.1 us (48%)
  Pallas kernels  14.4 us (29%)
  waiting for transfers between devices  10.3 us (21%)
    ppermute x15, starting transfers between devices, travel(): return lax.ppermute(block, ('expert', 'dp'), pairs)  23.5 us
    ppermute x15, waiting for transfers between devices, travel(): return lax.ppermute(block, ('expert', 'dp'), pairs)  8.08 us
    pallas_call x2, Pallas kernels, ffn(): pl.pallas_call(ffn_kernel, out_shape=[jax.ShapeDtypeStruct((part, width),...  7.91 us
    pallas_call x1, Pallas kernels, hold(): pl.pallas_call(hold_kernel, out_shape=pltpu.VMEM(weight.shape, weight.dty...  3.82 us
    pallas_call x1, Pallas kernels, route(): pl.pallas_call(functools.partial(route_kernel, chips), out_shape=[jax.Sha...  1.48 us
    ppermute x1, waiting for transfers between devices, local(): lax.ppermute(home[:, CAP:].reshape(half, width), 'expert', core_pairs)  1.27 us
    pallas_call x1, Pallas kernels, combine(): pl.pallas_call(combine_kernel, out_shape=jax.ShapeDtypeStruct(shape, jnp....  1.22 us
  transfers between devices with their start and end apart: 17, of which 8 were waited for; matrix products, arithmetic and copies ran while one was open for 0% of the time, Pallas kernels for 16%

profile of v7, /device:TPU:0, one launch (start us, length us, event | category | flops | bytes accessed | tf_op | source)
XLA Modules:
  0.0 49.5 jit_solution(15688806908292898929)
XLA Ops:
  0.0 1.5 %shard_map.64 = (bf16[8,7168]{1,0:T(8,128)(2,1)S(1)}, bf16[8,7168]{1,0:T(8,128)(2,1)S(1)}, bf16[32,64]{1,0:T(8,128)(2,1)S(1)}) custom-call(s32[8,64]{1,0:T(8,128)} %bitcast.13, f32[8,64]{1,0:T(8,128)} %bitcast.14, bf16[64,7168]{1,0:T(8,128)(2,1)} %refs_2_.1), custom_call_target="tpu_custom_call" | custom-call | flops 29360128 | bytes 1835008 | tf_op jit(solution)/shard_map/pallas_call | solution.py:65
  1.5 0.5 %collective-permute-start = (bf16[8,7168]{1,0:T(8,128)(2,1)S(1)}, bf16[8,7168]{1,0:T(8,128)(2,1)S(1)}, u32[]{:S(2)}, u32[]{:S(2)}) collective-permute-start(bf16[8,7168]{1,0:T(8,128)(2,1)S(1)} %get-tuple-element.25), channel_id=1, source_target_pairs={{0,4},{4,0},{8,12},{12,8},{1,5},{5,1},{9,13},{13,9},{2,6},{6,2},{1... | collective-permute-start | bytes 344072 | tf_op jit(solution)/shard_map/ppermute | solution.py:197
  2.0 0.1 reshape.15
  2.1 0.9 %collective-permute-done = bf16[8,7168]{1,0:T(8,128)(2,1)S(1)} collective-permute-done((bf16[8,7168]{1,0:T(8,128)(2,1)S(1)}, bf16[8,7168]{1,0:T(8,128)(2,1)S(1)}, u32[]{:S(2)}, u32[]{:S(2)}) %collective-permute-start) | collective-permute-done | bytes 114720 | tf_op jit(solution)/shard_map/ppermute | solution.py:197
  3.0 0.1 reshape.16
  3.0 0.1 constant_dynamic-update-slice_fusion.4
  3.1 0.1 fusion.5
  3.2 4.0 %collective-permute-start.6 = (bf16[8,7168]{1,0:T(8,128)(2,1)S(1)}, bf16[8,7168]{1,0:T(8,128)(2,1)S(1)}, u32[]{:S(2)}, u32[]{:S(2)}) collective-permute-start(bf16[8,7168]{1,0:T(8,128)(2,1)S(1)} %fusion.5), channel_id=1, source_target_pairs={{0,2},{1,3},{2,0},{3,1},{4,6},{5,7},{6,4},{7,5},{8,10},{9,11},{10,... | collective-permute-start | bytes 344072 | tf_op jit(solution)/shard_map/ppermute | solution.py:192
  7.2 0.0 slice-start
  7.2 1.6 %collective-permute-start.1 = (bf16[8,7168]{1,0:T(8,128)(2,1)S(1)}, bf16[8,7168]{1,0:T(8,128)(2,1)S(1)}, u32[]{:S(2)}, u32[]{:S(2)}) collective-permute-start(bf16[8,7168]{1,0:T(8,128)(2,1)S(1)} %get-tuple-element.42), channel_id=1, source_target_pairs={{0,1},{1,0},{2,3},{3,2},{4,5},{5,4},{6,7},{7,6},{8,9},{9,8},{10,11... | collective-permute-start | bytes 344072 | tf_op jit(solution)/shard_map/ppermute | solution.py:192
  8.8 0.3 collective-permute-start.4
  9.1 1.5 %collective-permute-start.2 = (bf16[8,7168]{1,0:T(8,128)(2,1)S(1)}, bf16[8,7168]{1,0:T(8,128)(2,1)S(1)}, u32[]{:S(2)}, u32[]{:S(2)}) collective-permute-start(bf16[8,7168]{1,0:T(8,128)(2,1)S(1)} %fusion.5), channel_id=1, source_target_pairs={{0,8},{1,9},{2,10},{3,11},{4,12},{5,13},{6,14},{7,15},{8,0},{9,1},... | collective-permute-start | bytes 344072 | tf_op jit(solution)/shard_map/ppermute | solution.py:192
  10.6 0.2 collective-permute-start.3
  10.8 3.8 %shard_map.65.up_ref = bf16[1,7168,512]{2,1,0:T(8,128)(2,1)S(1)} custom-call(bf16[1,7168,512]{2,1,0:T(8,128)(2,1)} %source), custom_call_target="tpu_custom_call" | custom-call | bytes 14680064 | tf_op jit(solution)/shard_map/pallas_call | solution.py:99
  14.6 0.0 collective-permute-done.6
  14.6 1.6 %collective-permute-start.7 = (bf16[8,7168]{1,0:T(8,128)(2,1)S(1)}, bf16[8,7168]{1,0:T(8,128)(2,1)S(1)}, u32[]{:S(2)}, u32[]{:S(2)}) collective-permute-start(bf16[8,7168]{1,0:T(8,128)(2,1)S(1)} %collective-permute-done.6), channel_id=1, source_target_pairs={{0,8},{1,9},{2,10},{3,11},{4,12},{5,13},{6,14},{7,15},{8,0},{9,1},... | collective-permute-start | bytes 344072 | tf_op jit(solution)/shard_map/ppermute | solution.py:192
  16.2 0.0 collective-permute-done.1
  16.2 1.5 %collective-permute-start.8 = (bf16[8,7168]{1,0:T(8,128)(2,1)S(1)}, bf16[8,7168]{1,0:T(8,128)(2,1)S(1)}, u32[]{:S(2)}, u32[]{:S(2)}) collective-permute-start(bf16[8,7168]{1,0:T(8,128)(2,1)S(1)} %collective-permute-done.6), channel_id=1, source_target_pairs={{0,9},{1,8},{2,11},{3,10},{4,13},{5,12},{6,15},{7,14},{8,1},{9,0},... | collective-permute-start | bytes 344072 | tf_op jit(solution)/shard_map/ppermute | solution.py:192
  17.7 0.4 collective-permute-done.4
  18.1 0.6 %collective-permute-start.5 = (bf16[8,7168]{1,0:T(8,128)(2,1)S(1)}, bf16[8,7168]{1,0:T(8,128)(2,1)S(1)}, u32[]{:S(2)}, u32[]{:S(2)}) collective-permute-start(bf16[8,7168]{1,0:T(8,128)(2,1)S(1)} %collective-permute-done.4), channel_id=1, source_target_pairs={{0,1},{1,0},{2,3},{3,2},{4,5},{5,4},{6,7},{7,6},{8,9},{9,8},{10,11... | collective-permute-start | bytes 344072 | tf_op jit(solution)/shard_map/ppermute | solution.py:192
  18.8 0.0 collective-permute-done.2
  18.8 0.7 %collective-permute-done.3 = bf16[8,7168]{1,0:T(8,128)(2,1)S(1)} collective-permute-done((bf16[8,7168]{1,0:T(8,128)(2,1)S(1)}, bf16[8,7168]{1,0:T(8,128)(2,1)S(1)}, u32[]{:S(2)}, u32[]{:S(2)}) %collective-permute-start.3) | collective-permute-done | bytes 114720 | tf_op jit(solution)/shard_map/ppermute | solution.py:192
  19.6 0.0 slice-done
  19.6 0.0 slice-done.1
  19.6 0.0 copy-done
  19.6 4.0 %shard_map.66 = (bf16[8,7168]{1,0:T(8,128)(2,1)S(1)}, bf16[8,7168]{1,0:T(8,128)(2,1)S(1)}, bf16[8,7168]{1,0:T(8,128)(2,1)S(1)}, bf16[8,7168]{1,0:T(8,128)(2,1)S(1)}, bf16[8,7168]{1,0:T(8,128)(2,1)S(1)}) custom-call(bf16[40,7168]{1,0:T(8,128)(2,1)S(1)} %constant_dynamic-update-slice_fusion.rows_ref, bf16[1,7168,512]{2,1,0:T(8,128)(2,1)S(1)} %bitcast.12, ...), custom_call_target="tpu_custom_call" | custom-call | flops 880803840 | bytes 7340032 | tf_op jit(solution)/shard_map/pallas_call | solution.py:126
  23.6 0.0 collective-permute-done.5
  23.6 0.0 collective-permute-done.7
  23.6 0.0 collective-permute-done.8
  23.6 3.9 %shard_map.67 = (bf16[8,7168]{1,0:T(8,128)(2,1)S(1)}, bf16[8,7168]{1,0:T(8,128)(2,1)S(1)}, bf16[8,7168]{1,0:T(8,128)(2,1)S(1)}) custom-call(bf16[24,7168]{1,0:T(8,128)(2,1)S(1)} %pad_maximum_fusion.rows_ref, bf16[1,7168,512]{2,1,0:T(8,128)(2,1)S(1)} %bitcast.12, bf16[1,7168,512]{2,1,0:T(8,128)(2,1)S(1)} %shard_map.65.up_ref, bf16[1,512,7168]{2,1,0:T(8,128)(2,1)S(1)} %copy-done), custom_call_target="tpu_custom_call" | custom-call | flops 528482304 | bytes 7340032 | tf_op jit(solution)/shard_map/pallas_call | solution.py:126
  27.6 1.8 %collective-permute-start.10 = (bf16[8,7168]{1,0:T(8,128)(2,1)S(1)}, bf16[8,7168]{1,0:T(8,128)(2,1)S(1)}, u32[]{:S(2)}, u32[]{:S(2)}) collective-permute-start(bf16[8,7168]{1,0:T(8,128)(2,1)S(1)} %get-tuple-element.35), channel_id=1, source_target_pairs={{0,1},{1,0},{2,3},{3,2},{4,5},{5,4},{6,7},{7,6},{8,9},{9,8},{10,11... | collective-permute-start | bytes 344072 | tf_op jit(solution)/shard_map/ppermute | solution.py:192
  29.4 0.2 collective-permute-start.9
  29.6 3.5 %collective-permute-done.10 = bf16[8,7168]{1,0:T(8,128)(2,1)S(1)} collective-permute-done((bf16[8,7168]{1,0:T(8,128)(2,1)S(1)}, bf16[8,7168]{1,0:T(8,128)(2,1)S(1)}, u32[]{:S(2)}, u32[]{:S(2)}) %collective-permute-start.10) | collective-permute-done | bytes 114720 | tf_op jit(solution)/shard_map/ppermute | solution.py:192
  33.1 3.3 %collective-permute-start.12 = (bf16[8,7168]{1,0:T(8,128)(2,1)S(1)}, bf16[8,7168]{1,0:T(8,128)(2,1)S(1)}, u32[]{:S(2)}, u32[]{:S(2)}) collective-permute-start(bf16[8,7168]{1,0:T(8,128)(2,1)S(1)} %add_convert_fusion.3), channel_id=1, source_target_pairs={{0,2},{1,3},{2,0},{3,1},{4,6},{5,7},{6,4},{7,5},{8,10},{9,11},{10,... | collective-permute-start | bytes 344072 | tf_op jit(solution)/shard_map/ppermute | solution.py:192
  36.4 0.0 collective-permute-done.9
  36.4 0.5 collective-permute-start.11
  36.9 1.5 %collective-permute-start.13 = (bf16[8,7168]{1,0:T(8,128)(2,1)S(1)}, bf16[8,7168]{1,0:T(8,128)(2,1)S(1)}, u32[]{:S(2)}, u32[]{:S(2)}) collective-permute-start(bf16[8,7168]{1,0:T(8,128)(2,1)S(1)} %get-tuple-element.38), channel_id=1, source_target_pairs={{0,8},{1,9},{2,10},{3,11},{4,12},{5,13},{6,14},{7,15},{8,0},{9,1},... | collective-permute-start | bytes 344072 | tf_op jit(solution)/shard_map/ppermute | solution.py:192
  38.4 1.5 %collective-permute-start.14 = (bf16[8,7168]{1,0:T(8,128)(2,1)S(1)}, bf16[8,7168]{1,0:T(8,128)(2,1)S(1)}, u32[]{:S(2)}, u32[]{:S(2)}) collective-permute-start(bf16[8,7168]{1,0:T(8,128)(2,1)S(1)} %get-tuple-element.39), channel_id=1, source_target_pairs={{0,9},{1,8},{2,11},{3,10},{4,13},{5,12},{6,15},{7,14},{8,1},{9,0},... | collective-permute-start | bytes 344072 | tf_op jit(solution)/shard_map/ppermute | solution.py:192
  39.9 3.3 %collective-permute-start.15 = (bf16[8,7168]{1,0:T(8,128)(2,1)S(1)}, bf16[8,7168]{1,0:T(8,128)(2,1)S(1)}, u32[]{:S(2)}, u32[]{:S(2)}) collective-permute-start(bf16[8,7168]{1,0:T(8,128)(2,1)S(1)} %add_convert_fusion.1), channel_id=1, source_target_pairs={{0,10},{1,11},{2,8},{3,9},{4,14},{5,15},{6,12},{7,13},{8,2},{9,3},... | collective-permute-start | bytes 344072 | tf_op jit(solution)/shard_map/ppermute | solution.py:192
  43.2 0.0 collective-permute-done.12
  43.2 0.0 collective-permute-done.11
  43.3 0.5 collective-permute-done.13
  43.8 1.3 %collective-permute-done.14 = bf16[8,7168]{1,0:T(8,128)(2,1)S(1)} collective-permute-done((bf16[8,7168]{1,0:T(8,128)(2,1)S(1)}, bf16[8,7168]{1,0:T(8,128)(2,1)S(1)}, u32[]{:S(2)}, u32[]{:S(2)}) %collective-permute-start.14) | collective-permute-done | bytes 114720 | tf_op jit(solution)/shard_map/ppermute | solution.py:192
  45.1 1.7 %collective-permute-done.15 = bf16[8,7168]{1,0:T(8,128)(2,1)S(1)} collective-permute-done((bf16[8,7168]{1,0:T(8,128)(2,1)S(1)}, bf16[8,7168]{1,0:T(8,128)(2,1)S(1)}, u32[]{:S(2)}, u32[]{:S(2)}) %collective-permute-start.15) | collective-permute-done | bytes 114720 | tf_op jit(solution)/shard_map/ppermute | solution.py:192
  46.8 0.1 pad_maximum_fusion.1
  46.9 0.1 collective-permute-start.16
  47.0 1.3 %collective-permute-done.16.other_ref = bf16[8,7168]{1,0:T(8,128)(2,1)S(1)} collective-permute-done((bf16[8,7168]{1,0:T(8,128)(2,1)S(1)}, bf16[8,7168]{1,0:T(8,128)(2,1)S(1)}, u32[]{:S(2)}, u32[]{:S(2)}) %collective-permute-start.16) | collective-permute-done | bytes 114720 | tf_op jit(solution)/shard_map/ppermute | solution.py:245
  48.3 1.2 %shard_map.68 = bf16[64,7168]{1,0:T(8,128)(2,1)} custom-call(bf16[32,64]{1,0:T(8,128)(2,1)S(1)} %get-tuple-element.23.mix_ref, bf16[8,7168]{1,0:T(8,128)(2,1)S(1)} %reshape.17.mine_ref, bf16[8,7168]{1,0:T(8,128)(2,1)S(1)} %collective-permute-done.16.other_ref), custom_call_target="tpu_custom_call" | custom-call | flops 29360128 | bytes 917504 | tf_op jit(solution)/shard_map/pallas_call | solution.py:163
  (14 shorter events, 0.3 us)
Async XLA Ops:
  1.5 1.5 %collective-permute-start = (bf16[8,7168]{1,0:T(8,128)(2,1)S(1)}, bf16[8,7168]{1,0:T(8,128)(2,1)S(1)}, u32[]{:S(2)}, u32[]{:S(2)}) collective-permute-start(bf16[8,7168]{1,0:T(8,128)(2,1)S(1)} %get-tuple-element.25), channel_id=1, source_target_pairs={{0,4},{4,0},{8,12},{12,8},{1,5},{5,1},{9,13},{13,9},{2,6},{6,2},{1... | collective-permute-start | bytes 344072 | tf_op jit(solution)/shard_map/ppermute | solution.py:197
  3.2 11.4 %collective-permute-start.6 = (bf16[8,7168]{1,0:T(8,128)(2,1)S(1)}, bf16[8,7168]{1,0:T(8,128)(2,1)S(1)}, u32[]{:S(2)}, u32[]{:S(2)}) collective-permute-start(bf16[8,7168]{1,0:T(8,128)(2,1)S(1)} %fusion.5), channel_id=1, source_target_pairs={{0,2},{1,3},{2,0},{3,1},{4,6},{5,7},{6,4},{7,5},{8,10},{9,11},{10,... | collective-permute-start | bytes 344072 | tf_op jit(solution)/shard_map/ppermute | solution.py:192
  7.2 12.4 %slice-start = ((s8[7340032]{0:T(1024)(128)(4,1)}), s8[4194304]{0:T(1024)(128)(4,1)S(1)}, s32[]{:S(2)}) async-start(s8[7340032]{0:T(1024)(128)(4,1)} %bitcast.11), calls=%async_computation | async-start | bytes 8388608
  7.2 12.4 %slice-start.1 = ((s8[7340032]{0:T(1024)(128)(4,1)}), s8[3145728]{0:T(1024)(128)(4,1)S(1)}, s32[]{:S(2)}) async-start(s8[7340032]{0:T(1024)(128)(4,1)} %bitcast.11), calls=%async_computation.1 | async-start | bytes 6291456
  7.2 12.4 %copy-start = (bf16[1,512,7168]{2,1,0:T(8,128)(2,1)S(1)}, bf16[1,512,7168]{2,1,0:T(8,128)(2,1)}, u32[]{:S(2)}) copy-start(bf16[1,512,7168]{2,1,0:T(8,128)(2,1)} %down_ref.3) | copy-start | bytes 22020100
  7.2 9.0 %collective-permute-start.1 = (bf16[8,7168]{1,0:T(8,128)(2,1)S(1)}, bf16[8,7168]{1,0:T(8,128)(2,1)S(1)}, u32[]{:S(2)}, u32[]{:S(2)}) collective-permute-start(bf16[8,7168]{1,0:T(8,128)(2,1)S(1)} %get-tuple-element.42), channel_id=1, source_target_pairs={{0,1},{1,0},{2,3},{3,2},{4,5},{5,4},{6,7},{7,6},{8,9},{9,8},{10,11... | collective-permute-start | bytes 344072 | tf_op jit(solution)/shard_map/ppermute | solution.py:192
  8.8 9.4 %collective-permute-start.4 = (bf16[8,7168]{1,0:T(8,128)(2,1)S(1)}, bf16[8,7168]{1,0:T(8,128)(2,1)S(1)}, u32[]{:S(2)}, u32[]{:S(2)}) collective-permute-start(bf16[8,7168]{1,0:T(8,128)(2,1)S(1)} %get-tuple-element.42), channel_id=1, source_target_pairs={{0,2},{1,3},{2,0},{3,1},{4,6},{5,7},{6,4},{7,5},{8,10},{9,11},{10,... | collective-permute-start | bytes 344072 | tf_op jit(solution)/shard_map/ppermute | solution.py:192
  9.1 9.7 %collective-permute-start.2 = (bf16[8,7168]{1,0:T(8,128)(2,1)S(1)}, bf16[8,7168]{1,0:T(8,128)(2,1)S(1)}, u32[]{:S(2)}, u32[]{:S(2)}) collective-permute-start(bf16[8,7168]{1,0:T(8,128)(2,1)S(1)} %fusion.5), channel_id=1, source_target_pairs={{0,8},{1,9},{2,10},{3,11},{4,12},{5,13},{6,14},{7,15},{8,0},{9,1},... | collective-permute-start | bytes 344072 | tf_op jit(solution)/shard_map/ppermute | solution.py:192
  10.6 8.9 %collective-permute-start.3 = (bf16[8,7168]{1,0:T(8,128)(2,1)S(1)}, bf16[8,7168]{1,0:T(8,128)(2,1)S(1)}, u32[]{:S(2)}, u32[]{:S(2)}) collective-permute-start(bf16[8,7168]{1,0:T(8,128)(2,1)S(1)} %fusion.5), channel_id=1, source_target_pairs={{0,9},{1,8},{2,11},{3,10},{4,13},{5,12},{6,15},{7,14},{8,1},{9,0},... | collective-permute-start | bytes 344072 | tf_op jit(solution)/shard_map/ppermute | solution.py:192
  14.6 9.0 %collective-permute-start.7 = (bf16[8,7168]{1,0:T(8,128)(2,1)S(1)}, bf16[8,7168]{1,0:T(8,128)(2,1)S(1)}, u32[]{:S(2)}, u32[]{:S(2)}) collective-permute-start(bf16[8,7168]{1,0:T(8,128)(2,1)S(1)} %collective-permute-done.6), channel_id=1, source_target_pairs={{0,8},{1,9},{2,10},{3,11},{4,12},{5,13},{6,14},{7,15},{8,0},{9,1},... | collective-permute-start | bytes 344072 | tf_op jit(solution)/shard_map/ppermute | solution.py:192
  16.2 7.4 %collective-permute-start.8 = (bf16[8,7168]{1,0:T(8,128)(2,1)S(1)}, bf16[8,7168]{1,0:T(8,128)(2,1)S(1)}, u32[]{:S(2)}, u32[]{:S(2)}) collective-permute-start(bf16[8,7168]{1,0:T(8,128)(2,1)S(1)} %collective-permute-done.6), channel_id=1, source_target_pairs={{0,9},{1,8},{2,11},{3,10},{4,13},{5,12},{6,15},{7,14},{8,1},{9,0},... | collective-permute-start | bytes 344072 | tf_op jit(solution)/shard_map/ppermute | solution.py:192
  18.1 5.5 %collective-permute-start.5 = (bf16[8,7168]{1,0:T(8,128)(2,1)S(1)}, bf16[8,7168]{1,0:T(8,128)(2,1)S(1)}, u32[]{:S(2)}, u32[]{:S(2)}) collective-permute-start(bf16[8,7168]{1,0:T(8,128)(2,1)S(1)} %collective-permute-done.4), channel_id=1, source_target_pairs={{0,1},{1,0},{2,3},{3,2},{4,5},{5,4},{6,7},{7,6},{8,9},{9,8},{10,11... | collective-permute-start | bytes 344072 | tf_op jit(solution)/shard_map/ppermute | solution.py:192
  27.6 5.5 %collective-permute-start.10 = (bf16[8,7168]{1,0:T(8,128)(2,1)S(1)}, bf16[8,7168]{1,0:T(8,128)(2,1)S(1)}, u32[]{:S(2)}, u32[]{:S(2)}) collective-permute-start(bf16[8,7168]{1,0:T(8,128)(2,1)S(1)} %get-tuple-element.35), channel_id=1, source_target_pairs={{0,1},{1,0},{2,3},{3,2},{4,5},{5,4},{6,7},{7,6},{8,9},{9,8},{10,11... | collective-permute-start | bytes 344072 | tf_op jit(solution)/shard_map/ppermute | solution.py:192
  29.4 7.0 %collective-permute-start.9 = (bf16[8,7168]{1,0:T(8,128)(2,1)S(1)}, bf16[8,7168]{1,0:T(8,128)(2,1)S(1)}, u32[]{:S(2)}, u32[]{:S(2)}) collective-permute-start(bf16[8,7168]{1,0:T(8,128)(2,1)S(1)} %get-tuple-element.34), channel_id=1, source_target_pairs={{0,1},{1,0},{2,3},{3,2},{4,5},{5,4},{6,7},{7,6},{8,9},{9,8},{10,11... | collective-permute-start | bytes 344072 | tf_op jit(solution)/shard_map/ppermute | solution.py:192
  33.1 10.1 %collective-permute-start.12 = (bf16[8,7168]{1,0:T(8,128)(2,1)S(1)}, bf16[8,7168]{1,0:T(8,128)(2,1)S(1)}, u32[]{:S(2)}, u32[]{:S(2)}) collective-permute-start(bf16[8,7168]{1,0:T(8,128)(2,1)S(1)} %add_convert_fusion.3), channel_id=1, source_target_pairs={{0,2},{1,3},{2,0},{3,1},{4,6},{5,7},{6,4},{7,5},{8,10},{9,11},{10,... | collective-permute-start | bytes 344072 | tf_op jit(solution)/shard_map/ppermute | solution.py:192
  36.4 6.8 %collective-permute-start.11 = (bf16[8,7168]{1,0:T(8,128)(2,1)S(1)}, bf16[8,7168]{1,0:T(8,128)(2,1)S(1)}, u32[]{:S(2)}, u32[]{:S(2)}) collective-permute-start(bf16[8,7168]{1,0:T(8,128)(2,1)S(1)} %get-tuple-element.36), channel_id=1, source_target_pairs={{0,1},{1,0},{2,3},{3,2},{4,5},{5,4},{6,7},{7,6},{8,9},{9,8},{10,11... | collective-permute-start | bytes 344072 | tf_op jit(solution)/shard_map/ppermute | solution.py:192
  36.9 6.9 %collective-permute-start.13 = (bf16[8,7168]{1,0:T(8,128)(2,1)S(1)}, bf16[8,7168]{1,0:T(8,128)(2,1)S(1)}, u32[]{:S(2)}, u32[]{:S(2)}) collective-permute-start(bf16[8,7168]{1,0:T(8,128)(2,1)S(1)} %get-tuple-element.38), channel_id=1, source_target_pairs={{0,8},{1,9},{2,10},{3,11},{4,12},{5,13},{6,14},{7,15},{8,0},{9,1},... | collective-permute-start | bytes 344072 | tf_op jit(solution)/shard_map/ppermute | solution.py:192
  38.4 6.7 %collective-permute-start.14 = (bf16[8,7168]{1,0:T(8,128)(2,1)S(1)}, bf16[8,7168]{1,0:T(8,128)(2,1)S(1)}, u32[]{:S(2)}, u32[]{:S(2)}) collective-permute-start(bf16[8,7168]{1,0:T(8,128)(2,1)S(1)} %get-tuple-element.39), channel_id=1, source_target_pairs={{0,9},{1,8},{2,11},{3,10},{4,13},{5,12},{6,15},{7,14},{8,1},{9,0},... | collective-permute-start | bytes 344072 | tf_op jit(solution)/shard_map/ppermute | solution.py:192
  39.9 6.8 %collective-permute-start.15 = (bf16[8,7168]{1,0:T(8,128)(2,1)S(1)}, bf16[8,7168]{1,0:T(8,128)(2,1)S(1)}, u32[]{:S(2)}, u32[]{:S(2)}) collective-permute-start(bf16[8,7168]{1,0:T(8,128)(2,1)S(1)} %add_convert_fusion.1), channel_id=1, source_target_pairs={{0,10},{1,11},{2,8},{3,9},{4,14},{5,15},{6,12},{7,13},{8,2},{9,3},... | collective-permute-start | bytes 344072 | tf_op jit(solution)/shard_map/ppermute | solution.py:192
  46.9 1.4 %collective-permute-start.16 = (bf16[8,7168]{1,0:T(8,128)(2,1)S(1)}, bf16[8,7168]{1,0:T(8,128)(2,1)S(1)}, u32[]{:S(2)}, u32[]{:S(2)}) collective-permute-start(bf16[8,7168]{1,0:T(8,128)(2,1)S(1)} %reshape.18), channel_id=1, source_target_pairs={{0,4},{4,0},{8,12},{12,8},{1,5},{5,1},{9,13},{13,9},{2,6},{6,2},{1... | collective-permute-start | bytes 344072 | tf_op jit(solution)/shard_map/ppermute | solution.py:245

commit v8 on v7

--- a/solution.py
+++ b/solution.py
@@ -198,17 +198,21 @@
     blocks = jnp.concatenate([kept.reshape(chips, CAP, width), swapped], axis=1)
     size = CORES * CAP
     held = {0: blocks.reshape(chips * size, width)}
+    early, late = {(0, 0): blocks[0]}, {}
+    for x, bit in [(x, bit) for x in range(chips) for bit in reversed([0] + bits[:1])]:
+        if x or bit:
+            early[x, bit] = travel(blocks[x], x, bit)
     for bit in reversed(bits[1:]):
         for offset in list(held):
             held[offset ^ bit] = [travel(held[offset][x * size:(x + 1) * size], 0, bit) for x in range(chips)]
             held[offset ^ bit] = jnp.concatenate(held[offset ^ bit], axis=0)
-    early, late = {}, {}
     for offset in list(held):
-        for x in range(chips):
-            block = held[offset][x * size:(x + 1) * size]
-            for bit in [0] + bits[:1]:
-                arrived = travel(block, x, bit) if x or bit else block
-                (late if offset and (x or bit) else early)[x, offset ^ bit] = arrived
+        if offset:
+            for x in range(chips):
+                block = held[offset][x * size:(x + 1) * size]
+                for bit in [0] + bits[:1]:
+                    arrived = travel(block, x, bit) if x or bit else block
+                    (late if x or bit else early)[x, offset ^ bit] = arrived
 
     w_up, _ = lax.optimization_barrier((w_up, swapped))
     weights = [pltpu.with_memory_space_constraint(w, pltpu.VMEM) for w in (w_gate, hold(w_up), w_down)]
@@ -233,7 +237,7 @@
                     onward = (x, offset ^ bit)
                     parts[onward] = (parts[onward].astype(jnp.float32) + arrived.astype(jnp.float32)).astype(jnp.bfloat16)
                     relayed.append(arrived)
-    plain = [(x, offset) for x, offset, bit in last if offset <= 1 and relayed and (x or offset)]
+    plain = [(x, offset) for x, offset, bit in last if offset == 1 and relayed]
     waited, _ = lax.optimization_barrier(([parts[way] for way in plain], relayed))
     parts.update(zip(plain, waited))
     for x, offset, bit in last:

time: 49.7 us -> 49.4 us (level)
  starting transfers between devices: 24.1 us -> 23.3 us
    ppermute x15, starting transfers between devices: 23.5 us -> 22.7 us  [travel(): return lax.ppermute(block, ('expert', 'dp'), pairs)]
  transfers between devices with their start and end apart: 17 -> 17, of which waited for: 8 -> 10; matrix products, arithmetic and copies ran while one was open for 0% -> 0% of each run, Pallas kernels for 16% -> 16%
where the time goes in v8:
time: 49.4 us; the launch traced here: 49.3 us
  starting transfers between devices  23.3 us (47%)
  Pallas kernels  14.4 us (29%)
  waiting for transfers between devices  10.7 us (22%)
    ppermute x15, starting transfers between devices, travel(): return lax.ppermute(block, ('expert', 'dp'), pairs)  22.7 us
    ppermute x15, waiting for transfers between devices, travel(): return lax.ppermute(block, ('expert', 'dp'), pairs)  8.55 us
    pallas_call x2, Pallas kernels, ffn(): pl.pallas_call(ffn_kernel, out_shape=[jax.ShapeDtypeStruct((part, width),...  7.91 us
    pallas_call x1, Pallas kernels, hold(): pl.pallas_call(hold_kernel, out_shape=pltpu.VMEM(weight.shape, weight.dty...  3.82 us
    pallas_call x1, Pallas kernels, route(): pl.pallas_call(functools.partial(route_kernel, chips), out_shape=[jax.Sha...  1.48 us
    ppermute x1, waiting for transfers between devices, local(): lax.ppermute(home[:, CAP:].reshape(half, width), 'expert', core_pairs)  1.27 us
    pallas_call x1, Pallas kernels, combine(): pl.pallas_call(combine_kernel, out_shape=jax.ShapeDtypeStruct(shape, jnp....  1.21 us
  transfers between devices with their start and end apart: 17, of which 10 were waited for; matrix products, arithmetic and copies ran while one was open for 0% of the time, Pallas kernels for 16%

profile of v8, /device:TPU:0, one launch (start us, length us, event | category | flops | bytes accessed | tf_op | source)
XLA Modules:
  0.0 49.3 jit_solution(10679059337541034371)
XLA Ops:
  0.0 1.5 %shard_map.64 = (bf16[8,7168]{1,0:T(8,128)(2,1)S(1)}, bf16[8,7168]{1,0:T(8,128)(2,1)S(1)}, bf16[32,64]{1,0:T(8,128)(2,1)S(1)}) custom-call(s32[8,64]{1,0:T(8,128)} %bitcast.13, f32[8,64]{1,0:T(8,128)} %bitcast.14, bf16[64,7168]{1,0:T(8,128)(2,1)} %refs_2_.1), custom_call_target="tpu_custom_call" | custom-call | flops 29360128 | bytes 1835008 | tf_op jit(solution)/shard_map/pallas_call | solution.py:65
  1.5 0.5 %collective-permute-start = (bf16[8,7168]{1,0:T(8,128)(2,1)S(1)}, bf16[8,7168]{1,0:T(8,128)(2,1)S(1)}, u32[]{:S(2)}, u32[]{:S(2)}) collective-permute-start(bf16[8,7168]{1,0:T(8,128)(2,1)S(1)} %get-tuple-element.24), channel_id=1, source_target_pairs={{0,4},{4,0},{8,12},{12,8},{1,5},{5,1},{9,13},{13,9},{2,6},{6,2},{1... | collective-permute-start | bytes 344072 | tf_op jit(solution)/shard_map/ppermute | solution.py:197
  2.0 0.1 reshape.15
  2.1 0.9 %collective-permute-done = bf16[8,7168]{1,0:T(8,128)(2,1)S(1)} collective-permute-done((bf16[8,7168]{1,0:T(8,128)(2,1)S(1)}, bf16[8,7168]{1,0:T(8,128)(2,1)S(1)}, u32[]{:S(2)}, u32[]{:S(2)}) %collective-permute-start) | collective-permute-done | bytes 114720 | tf_op jit(solution)/shard_map/ppermute | solution.py:197
  3.0 0.1 reshape.16
  3.0 0.1 constant_dynamic-update-slice_fusion.4
  3.1 0.1 fusion.5
  3.2 4.0 %collective-permute-start.6 = (bf16[8,7168]{1,0:T(8,128)(2,1)S(1)}, bf16[8,7168]{1,0:T(8,128)(2,1)S(1)}, u32[]{:S(2)}, u32[]{:S(2)}) collective-permute-start(bf16[8,7168]{1,0:T(8,128)(2,1)S(1)} %fusion.5), channel_id=1, source_target_pairs={{0,2},{1,3},{2,0},{3,1},{4,6},{5,7},{6,4},{7,5},{8,10},{9,11},{10,... | collective-permute-start | bytes 344072 | tf_op jit(solution)/shard_map/ppermute | solution.py:192
  7.2 0.0 slice-start
  7.2 1.6 %collective-permute-start.1 = (bf16[8,7168]{1,0:T(8,128)(2,1)S(1)}, bf16[8,7168]{1,0:T(8,128)(2,1)S(1)}, u32[]{:S(2)}, u32[]{:S(2)}) collective-permute-start(bf16[8,7168]{1,0:T(8,128)(2,1)S(1)} %get-tuple-element.40), channel_id=1, source_target_pairs={{0,1},{1,0},{2,3},{3,2},{4,5},{5,4},{6,7},{7,6},{8,9},{9,8},{10,11... | collective-permute-start | bytes 344072 | tf_op jit(solution)/shard_map/ppermute | solution.py:192
  8.8 0.3 collective-permute-start.4
  9.1 1.4 %collective-permute-start.2 = (bf16[8,7168]{1,0:T(8,128)(2,1)S(1)}, bf16[8,7168]{1,0:T(8,128)(2,1)S(1)}, u32[]{:S(2)}, u32[]{:S(2)}) collective-permute-start(bf16[8,7168]{1,0:T(8,128)(2,1)S(1)} %fusion.5), channel_id=1, source_target_pairs={{0,9},{1,8},{2,11},{3,10},{4,13},{5,12},{6,15},{7,14},{8,1},{9,0},... | collective-permute-start | bytes 344072 | tf_op jit(solution)/shard_map/ppermute | solution.py:192
  10.5 0.3 collective-permute-start.3
  10.8 3.8 %shard_map.65.up_ref = bf16[1,7168,512]{2,1,0:T(8,128)(2,1)S(1)} custom-call(bf16[1,7168,512]{2,1,0:T(8,128)(2,1)} %source), custom_call_target="tpu_custom_call" | custom-call | bytes 14680064 | tf_op jit(solution)/shard_map/pallas_call | solution.py:99
  14.6 0.0 collective-permute-done.6
  14.6 1.6 %collective-permute-start.7 = (bf16[8,7168]{1,0:T(8,128)(2,1)S(1)}, bf16[8,7168]{1,0:T(8,128)(2,1)S(1)}, u32[]{:S(2)}, u32[]{:S(2)}) collective-permute-start(bf16[8,7168]{1,0:T(8,128)(2,1)S(1)} %collective-permute-done.6), channel_id=1, source_target_pairs={{0,8},{1,9},{2,10},{3,11},{4,12},{5,13},{6,14},{7,15},{8,0},{9,1},... | collective-permute-start | bytes 344072 | tf_op jit(solution)/shard_map/ppermute | solution.py:192
  16.2 0.0 collective-permute-done.1
  16.2 1.5 %collective-permute-start.8 = (bf16[8,7168]{1,0:T(8,128)(2,1)S(1)}, bf16[8,7168]{1,0:T(8,128)(2,1)S(1)}, u32[]{:S(2)}, u32[]{:S(2)}) collective-permute-start(bf16[8,7168]{1,0:T(8,128)(2,1)S(1)} %collective-permute-done.6), channel_id=1, source_target_pairs={{0,9},{1,8},{2,11},{3,10},{4,13},{5,12},{6,15},{7,14},{8,1},{9,0},... | collective-permute-start | bytes 344072 | tf_op jit(solution)/shard_map/ppermute | solution.py:192
  17.7 0.4 collective-permute-done.4
  18.1 0.6 %collective-permute-start.5 = (bf16[8,7168]{1,0:T(8,128)(2,1)S(1)}, bf16[8,7168]{1,0:T(8,128)(2,1)S(1)}, u32[]{:S(2)}, u32[]{:S(2)}) collective-permute-start(bf16[8,7168]{1,0:T(8,128)(2,1)S(1)} %collective-permute-done.4), channel_id=1, source_target_pairs={{0,1},{1,0},{2,3},{3,2},{4,5},{5,4},{6,7},{7,6},{8,9},{9,8},{10,11... | collective-permute-start | bytes 344072 | tf_op jit(solution)/shard_map/ppermute | solution.py:192
  18.8 0.8 %collective-permute-done.2 = bf16[8,7168]{1,0:T(8,128)(2,1)S(1)} collective-permute-done((bf16[8,7168]{1,0:T(8,128)(2,1)S(1)}, bf16[8,7168]{1,0:T(8,128)(2,1)S(1)}, u32[]{:S(2)}, u32[]{:S(2)}) %collective-permute-start.2) | collective-permute-done | bytes 114720 | tf_op jit(solution)/shard_map/ppermute | solution.py:192
  19.5 0.0 collective-permute-done.3
  19.6 0.0 slice-done
  19.6 0.0 slice-done.1
  19.6 0.0 copy-done
  19.6 4.0 %shard_map.66 = (bf16[8,7168]{1,0:T(8,128)(2,1)S(1)}, bf16[8,7168]{1,0:T(8,128)(2,1)S(1)}, bf16[8,7168]{1,0:T(8,128)(2,1)S(1)}, bf16[8,7168]{1,0:T(8,128)(2,1)S(1)}, bf16[8,7168]{1,0:T(8,128)(2,1)S(1)}) custom-call(bf16[40,7168]{1,0:T(8,128)(2,1)S(1)} %constant_dynamic-update-slice_fusion.rows_ref, bf16[1,7168,512]{2,1,0:T(8,128)(2,1)S(1)} %bitcast.12, ...), custom_call_target="tpu_custom_call" | custom-call | flops 880803840 | bytes 7340032 | tf_op jit(solution)/shard_map/pallas_call | solution.py:126
  23.6 0.3 collective-permute-done.5
  23.9 0.0 collective-permute-done.7
  23.9 0.0 collective-permute-done.8
  23.9 3.9 %shard_map.67 = (bf16[8,7168]{1,0:T(8,128)(2,1)S(1)}, bf16[8,7168]{1,0:T(8,128)(2,1)S(1)}, bf16[8,7168]{1,0:T(8,128)(2,1)S(1)}) custom-call(bf16[24,7168]{1,0:T(8,128)(2,1)S(1)} %pad_maximum_fusion.rows_ref, bf16[1,7168,512]{2,1,0:T(8,128)(2,1)S(1)} %bitcast.12, bf16[1,7168,512]{2,1,0:T(8,128)(2,1)S(1)} %shard_map.65.up_ref, bf16[1,512,7168]{2,1,0:T(8,128)(2,1)S(1)} %copy-done), custom_call_target="tpu_custom_call" | custom-call | flops 528482304 | bytes 7340032 | tf_op jit(solution)/shard_map/pallas_call | solution.py:126
  27.8 1.6 %collective-permute-start.10 = (bf16[8,7168]{1,0:T(8,128)(2,1)S(1)}, bf16[8,7168]{1,0:T(8,128)(2,1)S(1)}, u32[]{:S(2)}, u32[]{:S(2)}) collective-permute-start(bf16[8,7168]{1,0:T(8,128)(2,1)S(1)} %get-tuple-element.33), channel_id=1, source_target_pairs={{0,1},{1,0},{2,3},{3,2},{4,5},{5,4},{6,7},{7,6},{8,9},{9,8},{10,11... | collective-permute-start | bytes 344072 | tf_op jit(solution)/shard_map/ppermute | solution.py:192
  29.4 1.0 %collective-permute-start.13 = (bf16[8,7168]{1,0:T(8,128)(2,1)S(1)}, bf16[8,7168]{1,0:T(8,128)(2,1)S(1)}, u32[]{:S(2)}, u32[]{:S(2)}) collective-permute-start(bf16[8,7168]{1,0:T(8,128)(2,1)S(1)} %get-tuple-element.36), channel_id=1, source_target_pairs={{0,8},{1,9},{2,10},{3,11},{4,12},{5,13},{6,14},{7,15},{8,0},{9,1},... | collective-permute-start | bytes 344072 | tf_op jit(solution)/shard_map/ppermute | solution.py:192
  30.4 0.5 collective-permute-start.9
  30.9 2.3 %collective-permute-done.10 = bf16[8,7168]{1,0:T(8,128)(2,1)S(1)} collective-permute-done((bf16[8,7168]{1,0:T(8,128)(2,1)S(1)}, bf16[8,7168]{1,0:T(8,128)(2,1)S(1)}, u32[]{:S(2)}, u32[]{:S(2)}) %collective-permute-start.10) | collective-permute-done | bytes 114720 | tf_op jit(solution)/shard_map/ppermute | solution.py:192
  33.3 3.1 %collective-permute-start.12 = (bf16[8,7168]{1,0:T(8,128)(2,1)S(1)}, bf16[8,7168]{1,0:T(8,128)(2,1)S(1)}, u32[]{:S(2)}, u32[]{:S(2)}) collective-permute-start(bf16[8,7168]{1,0:T(8,128)(2,1)S(1)} %add_convert_fusion.3), channel_id=1, source_target_pairs={{0,2},{1,3},{2,0},{3,1},{4,6},{5,7},{6,4},{7,5},{8,10},{9,11},{10,... | collective-permute-start | bytes 344072 | tf_op jit(solution)/shard_map/ppermute | solution.py:192
  36.4 0.1 collective-permute-done.9
  36.5 0.1 collective-permute-start.11
  36.6 2.8 %collective-permute-start.14 = (bf16[8,7168]{1,0:T(8,128)(2,1)S(1)}, bf16[8,7168]{1,0:T(8,128)(2,1)S(1)}, u32[]{:S(2)}, u32[]{:S(2)}) collective-permute-start(bf16[8,7168]{1,0:T(8,128)(2,1)S(1)} %get-tuple-element.37), channel_id=1, source_target_pairs={{0,9},{1,8},{2,11},{3,10},{4,13},{5,12},{6,15},{7,14},{8,1},{9,0},... | collective-permute-start | bytes 344072 | tf_op jit(solution)/shard_map/ppermute | solution.py:192
  39.4 2.3 %collective-permute-start.15 = (bf16[8,7168]{1,0:T(8,128)(2,1)S(1)}, bf16[8,7168]{1,0:T(8,128)(2,1)S(1)}, u32[]{:S(2)}, u32[]{:S(2)}) collective-permute-start(bf16[8,7168]{1,0:T(8,128)(2,1)S(1)} %add_convert_fusion.1), channel_id=1, source_target_pairs={{0,10},{1,11},{2,8},{3,9},{4,14},{5,15},{6,12},{7,13},{8,2},{9,3},... | collective-permute-start | bytes 344072 | tf_op jit(solution)/shard_map/ppermute | solution.py:192
  41.7 0.0 collective-permute-done.12
  41.7 1.1 %collective-permute-done.11 = bf16[8,7168]{1,0:T(8,128)(2,1)S(1)} collective-permute-done((bf16[8,7168]{1,0:T(8,128)(2,1)S(1)}, bf16[8,7168]{1,0:T(8,128)(2,1)S(1)}, u32[]{:S(2)}, u32[]{:S(2)}) %collective-permute-start.11) | collective-permute-done | bytes 114720 | tf_op jit(solution)/shard_map/ppermute | solution.py:192
  42.9 0.0 collective-permute-done.13
  42.9 1.6 %collective-permute-done.14 = bf16[8,7168]{1,0:T(8,128)(2,1)S(1)} collective-permute-done((bf16[8,7168]{1,0:T(8,128)(2,1)S(1)}, bf16[8,7168]{1,0:T(8,128)(2,1)S(1)}, u32[]{:S(2)}, u32[]{:S(2)}) %collective-permute-start.14) | collective-permute-done | bytes 114720 | tf_op jit(solution)/shard_map/ppermute | solution.py:192
  44.5 2.0 %collective-permute-done.15 = bf16[8,7168]{1,0:T(8,128)(2,1)S(1)} collective-permute-done((bf16[8,7168]{1,0:T(8,128)(2,1)S(1)}, bf16[8,7168]{1,0:T(8,128)(2,1)S(1)}, u32[]{:S(2)}, u32[]{:S(2)}) %collective-permute-start.15) | collective-permute-done | bytes 114720 | tf_op jit(solution)/shard_map/ppermute | solution.py:192
  46.5 0.1 pad_maximum_fusion.1
  46.7 0.1 collective-permute-start.16
  46.8 1.3 %collective-permute-done.16.other_ref = bf16[8,7168]{1,0:T(8,128)(2,1)S(1)} collective-permute-done((bf16[8,7168]{1,0:T(8,128)(2,1)S(1)}, bf16[8,7168]{1,0:T(8,128)(2,1)S(1)}, u32[]{:S(2)}, u32[]{:S(2)}) %collective-permute-start.16) | collective-permute-done | bytes 114720 | tf_op jit(solution)/shard_map/ppermute | solution.py:249
  48.0 1.2 %shard_map.68 = bf16[64,7168]{1,0:T(8,128)(2,1)} custom-call(bf16[32,64]{1,0:T(8,128)(2,1)S(1)} %get-tuple-element.22.mix_ref, bf16[8,7168]{1,0:T(8,128)(2,1)S(1)} %reshape.17.mine_ref, bf16[8,7168]{1,0:T(8,128)(2,1)S(1)} %collective-permute-done.16.other_ref), custom_call_target="tpu_custom_call" | custom-call | flops 29360128 | bytes 917504 | tf_op jit(solution)/shard_map/pallas_call | solution.py:163
  (14 shorter events, 0.3 us)
Async XLA Ops:
  1.5 1.5 %collective-permute-start = (bf16[8,7168]{1,0:T(8,128)(2,1)S(1)}, bf16[8,7168]{1,0:T(8,128)(2,1)S(1)}, u32[]{:S(2)}, u32[]{:S(2)}) collective-permute-start(bf16[8,7168]{1,0:T(8,128)(2,1)S(1)} %get-tuple-element.24), channel_id=1, source_target_pairs={{0,4},{4,0},{8,12},{12,8},{1,5},{5,1},{9,13},{13,9},{2,6},{6,2},{1... | collective-permute-start | bytes 344072 | tf_op jit(solution)/shard_map/ppermute | solution.py:197
  3.2 11.4 %collective-permute-start.6 = (bf16[8,7168]{1,0:T(8,128)(2,1)S(1)}, bf16[8,7168]{1,0:T(8,128)(2,1)S(1)}, u32[]{:S(2)}, u32[]{:S(2)}) collective-permute-start(bf16[8,7168]{1,0:T(8,128)(2,1)S(1)} %fusion.5), channel_id=1, source_target_pairs={{0,2},{1,3},{2,0},{3,1},{4,6},{5,7},{6,4},{7,5},{8,10},{9,11},{10,... | collective-permute-start | bytes 344072 | tf_op jit(solution)/shard_map/ppermute | solution.py:192
  7.2 12.4 %slice-start = ((s8[7340032]{0:T(1024)(128)(4,1)}), s8[4194304]{0:T(1024)(128)(4,1)S(1)}, s32[]{:S(2)}) async-start(s8[7340032]{0:T(1024)(128)(4,1)} %bitcast.11), calls=%async_computation | async-start | bytes 8388608
  7.2 12.4 %slice-start.1 = ((s8[7340032]{0:T(1024)(128)(4,1)}), s8[3145728]{0:T(1024)(128)(4,1)S(1)}, s32[]{:S(2)}) async-start(s8[7340032]{0:T(1024)(128)(4,1)} %bitcast.11), calls=%async_computation.1 | async-start | bytes 6291456
  7.2 12.4 %copy-start = (bf16[1,512,7168]{2,1,0:T(8,128)(2,1)S(1)}, bf16[1,512,7168]{2,1,0:T(8,128)(2,1)}, u32[]{:S(2)}) copy-start(bf16[1,512,7168]{2,1,0:T(8,128)(2,1)} %down_ref.3) | copy-start | bytes 22020100
  7.2 9.0 %collective-permute-start.1 = (bf16[8,7168]{1,0:T(8,128)(2,1)S(1)}, bf16[8,7168]{1,0:T(8,128)(2,1)S(1)}, u32[]{:S(2)}, u32[]{:S(2)}) collective-permute-start(bf16[8,7168]{1,0:T(8,128)(2,1)S(1)} %get-tuple-element.40), channel_id=1, source_target_pairs={{0,1},{1,0},{2,3},{3,2},{4,5},{5,4},{6,7},{7,6},{8,9},{9,8},{10,11... | collective-permute-start | bytes 344072 | tf_op jit(solution)/shard_map/ppermute | solution.py:192
  8.8 9.4 %collective-permute-start.4 = (bf16[8,7168]{1,0:T(8,128)(2,1)S(1)}, bf16[8,7168]{1,0:T(8,128)(2,1)S(1)}, u32[]{:S(2)}, u32[]{:S(2)}) collective-permute-start(bf16[8,7168]{1,0:T(8,128)(2,1)S(1)} %get-tuple-element.40), channel_id=1, source_target_pairs={{0,2},{1,3},{2,0},{3,1},{4,6},{5,7},{6,4},{7,5},{8,10},{9,11},{10,... | collective-permute-start | bytes 344072 | tf_op jit(solution)/shard_map/ppermute | solution.py:192
  9.1 10.4 %collective-permute-start.2 = (bf16[8,7168]{1,0:T(8,128)(2,1)S(1)}, bf16[8,7168]{1,0:T(8,128)(2,1)S(1)}, u32[]{:S(2)}, u32[]{:S(2)}) collective-permute-start(bf16[8,7168]{1,0:T(8,128)(2,1)S(1)} %fusion.5), channel_id=1, source_target_pairs={{0,9},{1,8},{2,11},{3,10},{4,13},{5,12},{6,15},{7,14},{8,1},{9,0},... | collective-permute-start | bytes 344072 | tf_op jit(solution)/shard_map/ppermute | solution.py:192
  10.5 9.1 %collective-permute-start.3 = (bf16[8,7168]{1,0:T(8,128)(2,1)S(1)}, bf16[8,7168]{1,0:T(8,128)(2,1)S(1)}, u32[]{:S(2)}, u32[]{:S(2)}) collective-permute-start(bf16[8,7168]{1,0:T(8,128)(2,1)S(1)} %fusion.5), channel_id=1, source_target_pairs={{0,8},{1,9},{2,10},{3,11},{4,12},{5,13},{6,14},{7,15},{8,0},{9,1},... | collective-permute-start | bytes 344072 | tf_op jit(solution)/shard_map/ppermute | solution.py:192
  14.6 9.2 %collective-permute-start.7 = (bf16[8,7168]{1,0:T(8,128)(2,1)S(1)}, bf16[8,7168]{1,0:T(8,128)(2,1)S(1)}, u32[]{:S(2)}, u32[]{:S(2)}) collective-permute-start(bf16[8,7168]{1,0:T(8,128)(2,1)S(1)} %collective-permute-done.6), channel_id=1, source_target_pairs={{0,8},{1,9},{2,10},{3,11},{4,12},{5,13},{6,14},{7,15},{8,0},{9,1},... | collective-permute-start | bytes 344072 | tf_op jit(solution)/shard_map/ppermute | solution.py:192
  16.2 7.7 %collective-permute-start.8 = (bf16[8,7168]{1,0:T(8,128)(2,1)S(1)}, bf16[8,7168]{1,0:T(8,128)(2,1)S(1)}, u32[]{:S(2)}, u32[]{:S(2)}) collective-permute-start(bf16[8,7168]{1,0:T(8,128)(2,1)S(1)} %collective-permute-done.6), channel_id=1, source_target_pairs={{0,9},{1,8},{2,11},{3,10},{4,13},{5,12},{6,15},{7,14},{8,1},{9,0},... | collective-permute-start | bytes 344072 | tf_op jit(solution)/shard_map/ppermute | solution.py:192
  18.1 5.7 %collective-permute-start.5 = (bf16[8,7168]{1,0:T(8,128)(2,1)S(1)}, bf16[8,7168]{1,0:T(8,128)(2,1)S(1)}, u32[]{:S(2)}, u32[]{:S(2)}) collective-permute-start(bf16[8,7168]{1,0:T(8,128)(2,1)S(1)} %collective-permute-done.4), channel_id=1, source_target_pairs={{0,1},{1,0},{2,3},{3,2},{4,5},{5,4},{6,7},{7,6},{8,9},{9,8},{10,11... | collective-permute-start | bytes 344072 | tf_op jit(solution)/shard_map/ppermute | solution.py:192
  27.8 5.4 %collective-permute-start.10 = (bf16[8,7168]{1,0:T(8,128)(2,1)S(1)}, bf16[8,7168]{1,0:T(8,128)(2,1)S(1)}, u32[]{:S(2)}, u32[]{:S(2)}) collective-permute-start(bf16[8,7168]{1,0:T(8,128)(2,1)S(1)} %get-tuple-element.33), channel_id=1, source_target_pairs={{0,1},{1,0},{2,3},{3,2},{4,5},{5,4},{6,7},{7,6},{8,9},{9,8},{10,11... | collective-permute-start | bytes 344072 | tf_op jit(solution)/shard_map/ppermute | solution.py:192
  29.4 13.5 %collective-permute-start.13 = (bf16[8,7168]{1,0:T(8,128)(2,1)S(1)}, bf16[8,7168]{1,0:T(8,128)(2,1)S(1)}, u32[]{:S(2)}, u32[]{:S(2)}) collective-permute-start(bf16[8,7168]{1,0:T(8,128)(2,1)S(1)} %get-tuple-element.36), channel_id=1, source_target_pairs={{0,8},{1,9},{2,10},{3,11},{4,12},{5,13},{6,14},{7,15},{8,0},{9,1},... | collective-permute-start | bytes 344072 | tf_op jit(solution)/shard_map/ppermute | solution.py:192
  30.4 6.0 %collective-permute-start.9 = (bf16[8,7168]{1,0:T(8,128)(2,1)S(1)}, bf16[8,7168]{1,0:T(8,128)(2,1)S(1)}, u32[]{:S(2)}, u32[]{:S(2)}) collective-permute-start(bf16[8,7168]{1,0:T(8,128)(2,1)S(1)} %get-tuple-element.32), channel_id=1, source_target_pairs={{0,1},{1,0},{2,3},{3,2},{4,5},{5,4},{6,7},{7,6},{8,9},{9,8},{10,11... | collective-permute-start | bytes 344072 | tf_op jit(solution)/shard_map/ppermute | solution.py:192
  33.3 8.5 %collective-permute-start.12 = (bf16[8,7168]{1,0:T(8,128)(2,1)S(1)}, bf16[8,7168]{1,0:T(8,128)(2,1)S(1)}, u32[]{:S(2)}, u32[]{:S(2)}) collective-permute-start(bf16[8,7168]{1,0:T(8,128)(2,1)S(1)} %add_convert_fusion.3), channel_id=1, source_target_pairs={{0,2},{1,3},{2,0},{3,1},{4,6},{5,7},{6,4},{7,5},{8,10},{9,11},{10,... | collective-permute-start | bytes 344072 | tf_op jit(solution)/shard_map/ppermute | solution.py:192
  36.5 6.4 %collective-permute-start.11 = (bf16[8,7168]{1,0:T(8,128)(2,1)S(1)}, bf16[8,7168]{1,0:T(8,128)(2,1)S(1)}, u32[]{:S(2)}, u32[]{:S(2)}) collective-permute-start(bf16[8,7168]{1,0:T(8,128)(2,1)S(1)} %get-tuple-element.34), channel_id=1, source_target_pairs={{0,1},{1,0},{2,3},{3,2},{4,5},{5,4},{6,7},{7,6},{8,9},{9,8},{10,11... | collective-permute-start | bytes 344072 | tf_op jit(solution)/shard_map/ppermute | solution.py:192
  36.6 7.9 %collective-permute-start.14 = (bf16[8,7168]{1,0:T(8,128)(2,1)S(1)}, bf16[8,7168]{1,0:T(8,128)(2,1)S(1)}, u32[]{:S(2)}, u32[]{:S(2)}) collective-permute-start(bf16[8,7168]{1,0:T(8,128)(2,1)S(1)} %get-tuple-element.37), channel_id=1, source_target_pairs={{0,9},{1,8},{2,11},{3,10},{4,13},{5,12},{6,15},{7,14},{8,1},{9,0},... | collective-permute-start | bytes 344072 | tf_op jit(solution)/shard_map/ppermute | solution.py:192
  39.4 7.1 %collective-permute-start.15 = (bf16[8,7168]{1,0:T(8,128)(2,1)S(1)}, bf16[8,7168]{1,0:T(8,128)(2,1)S(1)}, u32[]{:S(2)}, u32[]{:S(2)}) collective-permute-start(bf16[8,7168]{1,0:T(8,128)(2,1)S(1)} %add_convert_fusion.1), channel_id=1, source_target_pairs={{0,10},{1,11},{2,8},{3,9},{4,14},{5,15},{6,12},{7,13},{8,2},{9,3},... | collective-permute-start | bytes 344072 | tf_op jit(solution)/shard_map/ppermute | solution.py:192
  46.7 1.4 %collective-permute-start.16 = (bf16[8,7168]{1,0:T(8,128)(2,1)S(1)}, bf16[8,7168]{1,0:T(8,128)(2,1)S(1)}, u32[]{:S(2)}, u32[]{:S(2)}) collective-permute-start(bf16[8,7168]{1,0:T(8,128)(2,1)S(1)} %reshape.18), channel_id=1, source_target_pairs={{0,4},{4,0},{8,12},{12,8},{1,5},{5,1},{9,13},{13,9},{2,6},{6,2},{1... | collective-permute-start | bytes 344072 | tf_op jit(solution)/shard_map/ppermute | solution.py:249
